TPU v7x, 32 devices: a whole 2x2x4 slice. The times are simulated.
32 devices in a mesh: ball: 4 (over y, x), region: 8 (over z, core).
Axes of the slice: x: 2, y: 2, z: 4, core: 2. Of those that a mesh axis runs over, the one named last changes fastest.
Arguments:
- points: bfloat16 [4, 8, 1024, 256], P('ball', 'region'), may hold values from -6 to 6
- gain_attn: float32 [256], replicated, may hold values from 0.1 to 1.9
- w_query_key: bfloat16 [256, 512], replicated, may hold values from -7 to 7
- w_value: bfloat16 [256, 256], replicated, may hold values from -0.375 to 0.375
- w_out: bfloat16 [256, 256], replicated, may hold values from -0.375 to 0.375
- gain_mlp: float32 [256], replicated, may hold values from 0.1 to 1.9
- w_up: bfloat16 [256, 1024], replicated, may hold values from -0.375 to 0.375
- w_down: bfloat16 [1024, 256], replicated, may hold values from -0.1875 to 0.1875
- cluster_dest: int32 [4, 8, 16], P('ball', 'region'), may hold values from 0 to 63, as said below
Outputs:
- block_out: bfloat16 [4, 8, 1024, 256], P('ball', 'region')
Inputs may be any that keep to these rules, and one draw needn't show every extreme that they name: cluster_dest[l, r, c] = o * 16 + s sends cluster c of lane l, region r to slot s of lane o, region r. Within one region all values are distinct. Each lane sends exactly 8 clusters to each of 2 owner lanes and none to the others, and the offsets (o - l) mod 4 of those owners are the same set for every lane of one region.
All inputs are finite; a program needn't handle non-finite values.
Results may differ from a plain program's by a relative error of at most 0.012.
The roundings to bfloat16 on the way count: a program that leaves them out, or rounds other values in their place, can miss the bound.
Values may be sent and summed in bfloat16 or wider, within the bound.
No kernel may reach another device: no remote copies, remote signals or barrier semaphores. Data moves between devices by JAX's collectives and lax.ppermute only.
A program may use at most 64 MiB of HBM per device.

v0:
```python
import math

import jax
import jax.numpy as jnp
from jax import lax
from jax.sharding import PartitionSpec as P

HEADS = 8
BALL = 1024
CLUSTER = 64
POOL = 16


def rms_norm(row_data, gain_vector):
    widened = row_data.astype(jnp.float32)
    scaling = lax.rsqrt(jnp.mean(widened * widened, axis=1, keepdims=True) + 1e-06)
    return (widened * scaling * gain_vector).astype(jnp.bfloat16)


def attend_columns(query_cols, key_parts, value_parts):
    columns, row_count = query_cols.shape
    head_size = columns // HEADS
    query_heads = query_cols.reshape(HEADS, head_size, row_count)
    key_heads = tuple((part.reshape(HEADS, head_size, part.shape[1]) for part in key_parts))
    value_heads = tuple((part.reshape(HEADS, head_size, part.shape[1]) for part in value_parts))
    scale = 1.0 / math.sqrt(head_size)

    def one_head(operands):
        query_head, key_list, value_list = operands
        scores = [
            jnp.einsum("dn,dm->nm", query_head, key_head, preferred_element_type=jnp.float32)
            * scale
            for key_head in key_list
        ]
        row_max = scores[0].max(axis=1, keepdims=True)
        for extra in scores[1:]:
            row_max = jnp.maximum(row_max, extra.max(axis=1, keepdims=True))
        exponents = [jnp.exp(block - row_max) for block in scores]
        total = exponents[0].sum(axis=1, keepdims=True)
        for extra in exponents[1:]:
            total = total + extra.sum(axis=1, keepdims=True)
        mixed = jnp.zeros((head_size, row_count), jnp.float32)
        for exponent, value_head in zip(exponents, value_list):
            weights = (exponent / total).astype(jnp.bfloat16)
            mixed = mixed + jnp.einsum(
                "nm,dm->dn", weights, value_head, preferred_element_type=jnp.float32
            )
        return mixed.astype(jnp.bfloat16)

    result = lax.map(one_head, (query_heads, key_heads, value_heads))
    return result.reshape(columns, row_count)


def per_device(
    points, gain_attn, w_query_key, w_value, w_out, gain_mlp, w_up, w_down, cluster_dest
):
    columns = points.shape[-1]
    flat = points.reshape(-1, columns)
    row_count = flat.shape[0]
    lanes = lax.axis_size("ball")
    clusters = row_count // CLUSTER
    capacity = 2 * clusters // lanes
    ball_count = row_count // BALL
    ball_ids = jnp.arange(ball_count, dtype=jnp.int32)

    def project(states):
        paired = jnp.dot(states, w_query_key, preferred_element_type=jnp.float32).astype(
            jnp.bfloat16
        )
        projected = jnp.dot(states, w_value, preferred_element_type=jnp.float32).astype(
            jnp.bfloat16
        )
        return (paired[:, :columns], paired[:, columns:], projected)

    normed = rms_norm(flat, gain_attn)
    query, keys, values = project(normed)
    query_cols, key_cols, value_cols = (query.T, keys.T, values.T)

    def pooled(source_cols):
        summed = jnp.sum(source_cols.reshape(columns, -1, POOL), axis=2, dtype=jnp.float32)
        return (summed / math.sqrt(POOL)).astype(jnp.bfloat16)

    gathered_keys, gathered_values = (
        lax.all_gather(pooled(key_cols), "region", axis=1, tiled=True),
        lax.all_gather(pooled(value_cols), "region", axis=1, tiled=True),
    )

    def near_ball(index):
        return attend_columns(query_cols, (key_cols, gathered_keys), (value_cols, gathered_values))

    near = lax.map(near_ball, ball_ids)
    near_out = jnp.einsum("bcn,cf->bnf", near, w_out, preferred_element_type=jnp.float32).reshape(
        row_count, columns
    )
    targets = cluster_dest.reshape(-1)
    owner = targets // clusters
    slot = targets % clusters
    cluster_ids = jnp.arange(clusters, dtype=jnp.int32)
    earlier = (owner[:, None] == owner[None, :]) & (cluster_ids[None, :] < cluster_ids[:, None])
    rank = jnp.sum(earlier.astype(jnp.int32), axis=1)
    position = owner * capacity + rank
    placing = jnp.arange(lanes * capacity, dtype=jnp.int32)[:, None] == position[None, :]
    place_matrix = placing.astype(jnp.bfloat16)
    sent_ids = jnp.max(jnp.where(placing, slot[None, :], -1), axis=1).reshape(lanes, capacity)
    inner = normed.shape[1]
    packed = jnp.dot(
        place_matrix, normed.reshape(clusters, CLUSTER * inner), preferred_element_type=jnp.float32
    )
    got_states = lax.all_to_all(
        packed.astype(jnp.bfloat16).reshape(lanes, capacity * CLUSTER, inner),
        "ball",
        split_axis=0,
        concat_axis=0,
        tiled=True,
    )
    got_ids = lax.all_to_all(sent_ids, "ball", split_axis=0, concat_axis=0, tiled=True)
    fill_matrix = (cluster_ids[:, None] == got_ids.reshape(1, -1)).astype(jnp.bfloat16)
    inner = got_states.shape[2]
    settled = jnp.dot(
        fill_matrix,
        got_states.reshape(lanes * capacity, CLUSTER * inner),
        preferred_element_type=jnp.float32,
    )
    rotated_query, rotated_keys, rotated_values = project(
        settled.astype(jnp.bfloat16).reshape(row_count, inner)
    )
    rot_query_cols, rot_key_cols, rot_value_cols = (
        rotated_query.T,
        rotated_keys.T,
        rotated_values.T,
    )

    def far_ball(index):
        return attend_columns(rot_query_cols, (rot_key_cols,), (rot_value_cols,))

    far_rotated = lax.map(far_ball, ball_ids).transpose(0, 2, 1).reshape(row_count, columns)
    outgoing = jnp.einsum(
        "sk,sw->kw",
        fill_matrix,
        far_rotated.reshape(clusters, CLUSTER * columns),
        preferred_element_type=jnp.float32,
    )
    outgoing = outgoing.astype(jnp.bfloat16).reshape(lanes, capacity * CLUSTER, columns)
    returned = lax.all_to_all(outgoing, "ball", split_axis=0, concat_axis=0, tiled=True)
    far = jnp.einsum(
        "kc,kw->cw",
        place_matrix,
        returned.reshape(lanes * capacity, CLUSTER * columns),
        preferred_element_type=jnp.float32,
    )
    far = far.astype(jnp.bfloat16).reshape(row_count, columns)
    after = (
        flat.astype(jnp.float32)
        + near_out
        + jnp.dot(far, w_out, preferred_element_type=jnp.float32)
    ).astype(jnp.bfloat16)
    normed_mlp = rms_norm(after, gain_mlp)
    hidden = jax.nn.gelu(
        jnp.dot(normed_mlp, w_up, preferred_element_type=jnp.float32), approximate=True
    ).astype(jnp.bfloat16)
    block_out = (
        after.astype(jnp.float32) + jnp.dot(hidden, w_down, preferred_element_type=jnp.float32)
    ).astype(jnp.bfloat16)
    return block_out.reshape(points.shape)


def solution(mesh):
    placed = (
        P("ball", "region", None, None),
        P(),
        P(),
        P(),
        P(),
        P(),
        P(),
        P(),
        P("ball", "region", None),
    )
    return jax.shard_map(
        per_device,
        mesh=mesh,
        in_specs=placed,
        out_specs=P("ball", "region", None, None),
        check_vma=False,
    )
```

profile of v0, /device:TPU:0, one launch (start us, length us, event | category | flops | bytes accessed | tf_op | source)
XLA Modules:
  0.0 153.4 jit_solution(1661704209578717907)
XLA Ops:
  1.7 5.2 %all-to-all-start = ((s32[4,1,8]{2,1,0:T(1,128)}), s32[4,1,8]{2,1,0:T(1,128)S(1)}, u32[]{:S(2)}, u32[]{:S(2)}) async-start(s32[4,1,8]{2,1,0:T(1,128)} %bitcast.23), calls=%async_computation | async-start | bytes 4096 | tf_op jit(solution)/shard_map/all_to_all | solution.py:116
  10.2 2.0 %convert_reduce_fusion = (f32[256,64]{0,1:T(8,128)}, bf16[1024,256]{1,0:T(8,128)(2,1)S(1)}) fusion(bf16[256,256]{1,0:T(8,128)(2,1)} %param.16, bf16[1,1,1024,256]{2,3,1,0:T(8,128)(2,1)S(1)} %copy.41, f32[256]{0:T(256)} %param.14, f32[1024]{0:T(1024)S(1)} %add_rsqrt_fusion.1), kind=kOutput, calls=%fused_computation.80 | convolution fusion | flops 136036352 | bytes 1250304 | tf_op jit(solution)/shard_map/dot_general | solution.py:70
  19.2 2.3 %reshape.228 = bf16[4,512,256]{2,1,0:T(8,128)(2,1)} reshape(bf16[32,16384]{1,0:T(8,128)(2,1)} %convolution_convert_fusion.1) | data formatting | bytes 2097152 | tf_op jit(solution)/shard_map/reshape | solution.py:110
  21.5 4.2 %all-to-all-start.1 = ((bf16[4,512,256]{2,1,0:T(8,128)(2,1)}), bf16[4,512,256]{2,1,0:T(8,128)(2,1)S(1)}, u32[]{:S(2)}, u32[]{:S(2)}) async-start(bf16[4,512,256]{2,1,0:T(8,128)(2,1)} %reshape.228), calls=%async_computation.1 | async-start | bytes 2097152 | tf_op jit(solution)/shard_map/all_to_all | solution.py:109
  25.9 14.4 %all_gather.6 = bf16[256,512]{0,1:T(8,128)(2,1)S(1)} all-gather(bf16[256,64]{0,1:T(8,128)(2,1)S(1)} %multiply_convert_fusion.3), channel_id=1, replica_groups=mesh['ball'=4,'region'=8] {'region'}, dimensions={1}, use_global_device_ids=true | all-gather | bytes 294912 | tf_op jit(solution)/shard_map/all_gather | solution.py:84
  42.1 14.2 %all_gather.7 = bf16[256,512]{0,1:T(8,128)(2,1)S(1)} all-gather(bf16[256,64]{0,1:T(8,128)(2,1)S(1)} %multiply_convert_fusion.2), channel_id=1, replica_groups=mesh['ball'=4,'region'=8] {'region'}, dimensions={1}, use_global_device_ids=true | all-gather | bytes 294912 | tf_op jit(solution)/shard_map/all_gather | solution.py:85
  60.3 19.3 %while.35 = (s32[]{:T(128)}, bf16[8,32,1024]{2,1,0:T(8,128)(2,1)S(1)}, bf16[8,32,1024]{2,1,0:T(8,128)(2,1)S(1)}, bf16[8,32,1024]{2,1,0:T(8,128)(2,1)S(1)}, bf16[8,32,1024]{2,1,0:T(8,128)(2,1)S(1)}, /*index=5*/s32[]{:T(128)}) while((s32[]{:T(128)}, bf16[8,32,1024]{2,1,0:T(8,128)(2,1)S(1)}, bf16[8,32,1024]{2,1,0:T(8,128)(2,1)S(1)}, ...), condition=%wide.region_14.15_spmd, body=%wide.region_11.14_spmd.sunk | while | flops 143685632 | bytes 12867661 | solution.py:50
  81.9 4.2 %all-to-all-start.2 = ((bf16[4,512,256]{2,1,0:T(8,128)(2,1)}), bf16[4,512,256]{2,1,0:T(8,128)(2,1)S(1)}, u32[]{:S(2)}, u32[]{:S(2)}) async-start(bf16[4,512,256]{2,1,0:T(8,128)(2,1)} %reshape.234), calls=%async_computation.2 | async-start | bytes 2097152 | tf_op jit(solution)/shard_map/all_to_all | solution.py:144
  86.2 57.4 %while.34 = (s32[]{:T(128)}, bf16[8,32,1024]{2,1,0:T(8,128)(2,1)S(1)}, bf16[8,32,1024]{2,1,0:T(8,128)(2,1)}, bf16[8,32,1024]{2,1,0:T(8,128)(2,1)}, bf16[8,32,102...) while((s32[]{:T(128)}, ...), condition=%wide.region_8.0_spmd, body=%wide.region_3.8_spmd.sunk | while | flops 215545856 | bytes 19598432 | solution.py:50
  86.2 1.7 %multiply_reduce_fusion.6 = (f32[1024]{0:T(1024)S(1)}, f32[1024,1024]{0,1:T(8,128)S(1)}) fusion(bf16[8,32,1024]{2,1,0:T(8,128)(2,1)} %get-tuple-element.268, s32[]{:T(128)S(6)} %copy.58, bf16[8,32,1024]{2,1,0:T(8,128)(2,1)} %get-tuple-element.267), kind=kOutput, calls=%fused_computation.2.clone.1 | convolution fusion | flops 69204992 | bytes 4330496 | tf_op jit(solution)/shard_map/while/body/eval_jaxpr/while/body/eval_jaxpr/dn,dm->nm/dot_general | solution.py:31
  90.3 1.8 %fusion.106 = f32[32,1024]{1,0:T(8,128)S(1)} fusion(f32[1024,1024]{0,1:T(8,128)S(1)} %get-tuple-element.237, f32[1024]{0:T(1024)S(1)} %add.171, f32[1024]{0:T(1024)S(1)} %max.9, bf16[8,32,1024]{2,1,0:T(8,128)(2,1)} %get-tuple-element.266, s32[]{:T(128)S(6)} %copy.58), kind=kOutput, calls=%fused_computation.6.clone.1 | convolution fusion | flops 71303168 | bytes 4399108 | tf_op jit(solution)/shard_map/while/body/eval_jaxpr/while/body/eval_jaxpr/nm,dm->dn/dot_general | solution.py:45
  93.4 1.6 %multiply_reduce_fusion.6 = (f32[1024]{0:T(1024)S(1)}, f32[1024,1024]{0,1:T(8,128)S(1)}) fusion(bf16[8,32,1024]{2,1,0:T(8,128)(2,1)} %get-tuple-element.268, s32[]{:T(128)S(6)} %copy.58, bf16[8,32,1024]{2,1,0:T(8,128)(2,1)} %get-tuple-element.267), kind=kOutput, calls=%fused_computation.2.clone.1 | convolution fusion | flops 69204992 | bytes 4330496 | tf_op jit(solution)/shard_map/while/body/eval_jaxpr/while/body/eval_jaxpr/dn,dm->nm/dot_general | solution.py:31
  97.5 1.8 %fusion.106 = f32[32,1024]{1,0:T(8,128)S(1)} fusion(f32[1024,1024]{0,1:T(8,128)S(1)} %get-tuple-element.237, f32[1024]{0:T(1024)S(1)} %add.171, f32[1024]{0:T(1024)S(1)} %max.9, bf16[8,32,1024]{2,1,0:T(8,128)(2,1)} %get-tuple-element.266, s32[]{:T(128)S(6)} %copy.58), kind=kOutput, calls=%fused_computation.6.clone.1 | convolution fusion | flops 71303168 | bytes 4399108 | tf_op jit(solution)/shard_map/while/body/eval_jaxpr/while/body/eval_jaxpr/nm,dm->dn/dot_general | solution.py:45
  100.5 1.6 %multiply_reduce_fusion.6 = (f32[1024]{0:T(1024)S(1)}, f32[1024,1024]{0,1:T(8,128)S(1)}) fusion(bf16[8,32,1024]{2,1,0:T(8,128)(2,1)} %get-tuple-element.268, s32[]{:T(128)S(6)} %copy.58, bf16[8,32,1024]{2,1,0:T(8,128)(2,1)} %get-tuple-element.267), kind=kOutput, calls=%fused_computation.2.clone.1 | convolution fusion | flops 69204992 | bytes 4330496 | tf_op jit(solution)/shard_map/while/body/eval_jaxpr/while/body/eval_jaxpr/dn,dm->nm/dot_general | solution.py:31
  104.6 1.8 %fusion.106 = f32[32,1024]{1,0:T(8,128)S(1)} fusion(f32[1024,1024]{0,1:T(8,128)S(1)} %get-tuple-element.237, f32[1024]{0:T(1024)S(1)} %add.171, f32[1024]{0:T(1024)S(1)} %max.9, bf16[8,32,1024]{2,1,0:T(8,128)(2,1)} %get-tuple-element.266, s32[]{:T(128)S(6)} %copy.58), kind=kOutput, calls=%fused_computation.6.clone.1 | convolution fusion | flops 71303168 | bytes 4399108 | tf_op jit(solution)/shard_map/while/body/eval_jaxpr/while/body/eval_jaxpr/nm,dm->dn/dot_general | solution.py:45
  107.7 1.6 %multiply_reduce_fusion.6 = (f32[1024]{0:T(1024)S(1)}, f32[1024,1024]{0,1:T(8,128)S(1)}) fusion(bf16[8,32,1024]{2,1,0:T(8,128)(2,1)} %get-tuple-element.268, s32[]{:T(128)S(6)} %copy.58, bf16[8,32,1024]{2,1,0:T(8,128)(2,1)} %get-tuple-element.267), kind=kOutput, calls=%fused_computation.2.clone.1 | convolution fusion | flops 69204992 | bytes 4330496 | tf_op jit(solution)/shard_map/while/body/eval_jaxpr/while/body/eval_jaxpr/dn,dm->nm/dot_general | solution.py:31
  111.8 1.8 %fusion.106 = f32[32,1024]{1,0:T(8,128)S(1)} fusion(f32[1024,1024]{0,1:T(8,128)S(1)} %get-tuple-element.237, f32[1024]{0:T(1024)S(1)} %add.171, f32[1024]{0:T(1024)S(1)} %max.9, bf16[8,32,1024]{2,1,0:T(8,128)(2,1)} %get-tuple-element.266, s32[]{:T(128)S(6)} %copy.58), kind=kOutput, calls=%fused_computation.6.clone.1 | convolution fusion | flops 71303168 | bytes 4399108 | tf_op jit(solution)/shard_map/while/body/eval_jaxpr/while/body/eval_jaxpr/nm,dm->dn/dot_general | solution.py:45
  114.9 1.6 %multiply_reduce_fusion.6 = (f32[1024]{0:T(1024)S(1)}, f32[1024,1024]{0,1:T(8,128)S(1)}) fusion(bf16[8,32,1024]{2,1,0:T(8,128)(2,1)} %get-tuple-element.268, s32[]{:T(128)S(6)} %copy.58, bf16[8,32,1024]{2,1,0:T(8,128)(2,1)} %get-tuple-element.267), kind=kOutput, calls=%fused_computation.2.clone.1 | convolution fusion | flops 69204992 | bytes 4330496 | tf_op jit(solution)/shard_map/while/body/eval_jaxpr/while/body/eval_jaxpr/dn,dm->nm/dot_general | solution.py:31
  119.0 1.8 %fusion.106 = f32[32,1024]{1,0:T(8,128)S(1)} fusion(f32[1024,1024]{0,1:T(8,128)S(1)} %get-tuple-element.237, f32[1024]{0:T(1024)S(1)} %add.171, f32[1024]{0:T(1024)S(1)} %max.9, bf16[8,32,1024]{2,1,0:T(8,128)(2,1)} %get-tuple-element.266, s32[]{:T(128)S(6)} %copy.58), kind=kOutput, calls=%fused_computation.6.clone.1 | convolution fusion | flops 71303168 | bytes 4399108 | tf_op jit(solution)/shard_map/while/body/eval_jaxpr/while/body/eval_jaxpr/nm,dm->dn/dot_general | solution.py:45
  126.1 1.8 %fusion.106 = f32[32,1024]{1,0:T(8,128)S(1)} fusion(f32[1024,1024]{0,1:T(8,128)S(1)} %get-tuple-element.237, f32[1024]{0:T(1024)S(1)} %add.171, f32[1024]{0:T(1024)S(1)} %max.9, bf16[8,32,1024]{2,1,0:T(8,128)(2,1)} %get-tuple-element.266, s32[]{:T(128)S(6)} %copy.58), kind=kOutput, calls=%fused_computation.6.clone.1 | convolution fusion | flops 71303168 | bytes 4399108 | tf_op jit(solution)/shard_map/while/body/eval_jaxpr/while/body/eval_jaxpr/nm,dm->dn/dot_general | solution.py:45
  133.3 1.8 %fusion.106 = f32[32,1024]{1,0:T(8,128)S(1)} fusion(f32[1024,1024]{0,1:T(8,128)S(1)} %get-tuple-element.237, f32[1024]{0:T(1024)S(1)} %add.171, f32[1024]{0:T(1024)S(1)} %max.9, bf16[8,32,1024]{2,1,0:T(8,128)(2,1)} %get-tuple-element.266, s32[]{:T(128)S(6)} %copy.58), kind=kOutput, calls=%fused_computation.6.clone.1 | convolution fusion | flops 71303168 | bytes 4399108 | tf_op jit(solution)/shard_map/while/body/eval_jaxpr/while/body/eval_jaxpr/nm,dm->dn/dot_general | solution.py:45
  136.4 1.6 %multiply_reduce_fusion.6 = (f32[1024]{0:T(1024)S(1)}, f32[1024,1024]{0,1:T(8,128)S(1)}) fusion(bf16[8,32,1024]{2,1,0:T(8,128)(2,1)} %get-tuple-element.268, s32[]{:T(128)S(6)} %copy.58, bf16[8,32,1024]{2,1,0:T(8,128)(2,1)} %get-tuple-element.267), kind=kOutput, calls=%fused_computation.2.clone.1 | convolution fusion | flops 69204992 | bytes 4330496 | tf_op jit(solution)/shard_map/while/body/eval_jaxpr/while/body/eval_jaxpr/dn,dm->nm/dot_general | solution.py:31
  140.5 1.8 %fusion.106 = f32[32,1024]{1,0:T(8,128)S(1)} fusion(f32[1024,1024]{0,1:T(8,128)S(1)} %get-tuple-element.237, f32[1024]{0:T(1024)S(1)} %add.171, f32[1024]{0:T(1024)S(1)} %max.9, bf16[8,32,1024]{2,1,0:T(8,128)(2,1)} %get-tuple-element.266, s32[]{:T(128)S(6)} %copy.58), kind=kOutput, calls=%fused_computation.6.clone.1 | convolution fusion | flops 71303168 | bytes 4399108 | tf_op jit(solution)/shard_map/while/body/eval_jaxpr/while/body/eval_jaxpr/nm,dm->dn/dot_general | solution.py:45
  149.3 3.1 %fusion.52 = bf16[1,1,1024,256]{2,3,1,0:T(8,128)(2,1)S(1)} fusion(bf16[1024,256]{1,0:T(8,128)(2,1)S(1)} %copy-done, bf16[256,1024]{1,0:T(8,128)(2,1)} %param.19, bf16[1024,256]{0,1:T(8,128)(2,1)S(1)} %get-tuple-element.161, f32[256]{0:T(256)S(1)} %copy-done.6, f32[1024]{0:T(1024)S(1)} %add_rsqrt_fusion), kind=kOutput, calls=%fused_computation.76 | convolution fusion | flops 1085014016 | bytes 2102272 | tf_op jit(solution)/shard_map/dot_general | solution.py:162
  (138 shorter events, 79.2 us)
Async XLA Ops:
  0.0 149.3 %copy-start = (bf16[1024,256]{1,0:T(8,128)(2,1)S(1)}, bf16[1024,256]{1,0:T(8,128)(2,1)}, u32[]{:S(2)}) copy-start(bf16[1024,256]{1,0:T(8,128)(2,1)} %param.20) | copy-start | bytes 1572868
  0.0 13.2 %copy-start.5 = (f32[256]{0:T(256)S(1)}, f32[256]{0:T(256)}, u32[]{:S(2)}) copy-start(f32[256]{0:T(256)} %param.14) | copy-start | bytes 3076
  0.0 13.2 %copy-start.2 = (bf16[256,512]{1,0:T(8,128)(2,1)S(1)}, bf16[256,512]{1,0:T(8,128)(2,1)}, u32[]{:S(2)}) copy-start(bf16[256,512]{1,0:T(8,128)(2,1)} %param.15) | copy-start | bytes 786436
  1.7 19.8 %all-to-all-start = ((s32[4,1,8]{2,1,0:T(1,128)}), s32[4,1,8]{2,1,0:T(1,128)S(1)}, u32[]{:S(2)}, u32[]{:S(2)}) async-start(s32[4,1,8]{2,1,0:T(1,128)} %bitcast.23), calls=%async_computation | async-start | bytes 4096 | tf_op jit(solution)/shard_map/all_to_all | solution.py:116
  21.5 36.7 %all-to-all-start.1 = ((bf16[4,512,256]{2,1,0:T(8,128)(2,1)}), bf16[4,512,256]{2,1,0:T(8,128)(2,1)S(1)}, u32[]{:S(2)}, u32[]{:S(2)}) async-start(bf16[4,512,256]{2,1,0:T(8,128)(2,1)} %reshape.228), calls=%async_computation.1 | async-start | bytes 2097152 | tf_op jit(solution)/shard_map/all_to_all | solution.py:109
  25.7 33.6 %copy-start.4 = (bf16[256,256]{1,0:T(8,128)(2,1)S(1)}, bf16[256,256]{1,0:T(8,128)(2,1)}, u32[]{:S(2)}) copy-start(bf16[256,256]{1,0:T(8,128)(2,1)} %param.16) | copy-start | bytes 393220
  81.9 63.8 %all-to-all-start.2 = ((bf16[4,512,256]{2,1,0:T(8,128)(2,1)}), bf16[4,512,256]{2,1,0:T(8,128)(2,1)S(1)}, u32[]{:S(2)}, u32[]{:S(2)}) async-start(bf16[4,512,256]{2,1,0:T(8,128)(2,1)} %reshape.234), calls=%async_computation.2 | async-start | bytes 2097152 | tf_op jit(solution)/shard_map/all_to_all | solution.py:144
  86.1 58.2 %copy-start.3 = (bf16[256,256]{1,0:T(8,128)(2,1)S(1)}, bf16[256,256]{1,0:T(8,128)(2,1)}, u32[]{:S(2)}) copy-start(bf16[256,256]{1,0:T(8,128)(2,1)} %param.17) | copy-start | bytes 393220
  143.5 0.8 copy-start.1
  144.3 5.0 %copy-start.6 = (f32[256]{0:T(256)S(1)}, f32[256]{0:T(256)}, u32[]{:S(2)}) copy-start(f32[256]{0:T(256)} %param.18) | copy-start | bytes 3076
where the time goes:
time: 156 us; the launch traced here: 153 us
  matrix products  73.6 us (47%)
  blocking collectives  28.6 us (18%)
  other arithmetic  18.7 us (12%)
  local copies, waits for them, and re-layouts  18.2 us (12%)
  starting transfers between devices  13.6 us (9%)
    dot_general x24, matrix products, one_head(): jnp.einsum('nm,dm->dn', weights, value_head, preferred_element_type=jnp.f...  31.6 us
    dot_general x24, matrix products, one_head(): jnp.einsum('dn,dm->nm', query_head, key_head, preferred_element_type=jnp....  29.9 us
    all_gather x1, blocking collectives, per_device(): lax.all_gather(pooled(key_cols), 'region', axis=1, tiled=True)  14.4 us
    all_gather x1, blocking collectives, per_device(): lax.all_gather(pooled(value_cols), 'region', axis=1, tiled=True)  14.2 us
    reduce_sum x16, other arithmetic, one_head(): total = exponents[0].sum(axis=1, keepdims=True)  11.7 us
    all_to_all x1, starting transfers between devices, per_device(): lax.all_to_all(sent_ids, 'ball', split_axis=0, concat_axis=0, tiled=True)  5.17 us
    all_to_all x1, starting transfers between devices, per_device(): lax.all_to_all(packed.astype(jnp.bfloat16).reshape(lanes, capacity * CLUS...  4.2 us
    all_to_all x1, starting transfers between devices, per_device(): lax.all_to_all(outgoing, 'ball', split_axis=0, concat_axis=0, tiled=True)  4.19 us
  transfers between devices with their start and end apart: 3, of which 0 were waited for; matrix products, arithmetic and copies ran while one was open for 50% of the time, Pallas kernels for 0%

commit v1 on v0

v1 whole, which is shorter than its diff:
```python
import functools
import math

import jax
import jax.numpy as jnp
from jax import lax
from jax.experimental import pallas as pl
from jax.experimental.pallas import tpu as pltpu
from jax.sharding import PartitionSpec as P

HEADS = 8
BALL = 1024
CLUSTER = 64
POOL = 16
LANE_TILE = 128
BLOCK = 512
VMEM_LIMIT = 48 * 1024 * 1024

bf16 = jnp.bfloat16
f32 = jnp.float32


def in_vmem():
    return pl.BlockSpec(memory_space=pltpu.VMEM)


def in_smem():
    return pl.BlockSpec(memory_space=pltpu.SMEM)


def anywhere():
    return pl.BlockSpec(memory_space=pl.ANY)


def params():
    return pltpu.CompilerParams(vmem_limit_bytes=VMEM_LIMIT)


def cost(flops, moved, transcendentals=0):
    return pl.CostEstimate(
        flops=int(flops), bytes_accessed=int(moved), transcendentals=int(transcendentals)
    )


def rms_norm(rows, gain):
    widened = rows.astype(f32)
    scaling = lax.rsqrt(jnp.mean(widened * widened, axis=1, keepdims=True) + 1e-06)
    return (widened * scaling * gain).astype(bf16)


def dot32(left, right):
    return jnp.dot(left, right, preferred_element_type=f32)


def owner_offset(dest_ref, cluster, clusters, lanes, me):
    owner = dest_ref[cluster] // clusters
    return lax.rem(owner - me + lanes, lanes)


def set_keys(kt_ref, first, keys):
    kt_ref[:, first : first + keys.shape[0]] = keys.T


def set_values(ve_ref, first, values):
    count, columns = values.shape
    for group in range(columns // LANE_TILE):
        ve_ref[group, first : first + count, :LANE_TILE] = values[
            :, group * LANE_TILE : (group + 1) * LANE_TILE
        ]
        ve_ref[group, first : first + count, LANE_TILE:] = jnp.ones((count, LANE_TILE), bf16)


def run_heads(jobs, query_of, kt_ref, ve_ref, head_size, finish):
    per_tile = LANE_TILE // head_size
    columns = kt_ref.shape[0]
    head_of_lane = lax.broadcasted_iota(jnp.int32, (1, columns), 1) // head_size
    factor = math.log2(math.e) / math.sqrt(head_size)

    def scores(job):
        tag, head, first, end = job
        masked = jnp.where(head_of_lane == head, query_of(tag), bf16(0))
        return dot32(masked, kt_ref[:, first:end])

    current = scores(jobs[0])
    for index, job in enumerate(jobs):
        following = scores(jobs[index + 1]) if index + 1 < len(jobs) else None
        tag, head, first, end = job
        row_max = jnp.max(current, axis=1, keepdims=True)
        weights = jnp.exp2((current - row_max) * factor).astype(bf16)
        mixed = dot32(weights, ve_ref[head // per_tile, first:end, :])
        finish(tag, head, mixed[:, :LANE_TILE], mixed[:, LANE_TILE:], row_max)
        current = following


def place_head(kept, head, per_tile, head_size, new):
    lane = lax.broadcasted_iota(jnp.int32, (1, LANE_TILE), 1) // head_size
    if kept is None:
        return jnp.broadcast_to(new, (new.shape[0], LANE_TILE))
    return jnp.where(lane == head % per_tile, new, kept)


def full_attention(jobs, query_of, kt_ref, ve_ref, columns, out_of):
    head_size = columns // HEADS
    per_tile = LANE_TILE // head_size
    kept = {}

    def finish(tag, head, mixed, total, row_max):
        group = head // per_tile
        kept[tag, group] = place_head(
            kept.get((tag, group)), head, per_tile, head_size, mixed / total
        )
        if head % per_tile == per_tile - 1:
            out_of(tag, group, kept.pop((tag, group)).astype(bf16))

    run_heads(jobs, query_of, kt_ref, ve_ref, head_size, finish)


def pack_kernel(lanes, clusters, dest_ref, points_ref, *rest):
    packed = rest[:lanes]
    counts, sems = rest[lanes:]
    me = lax.axis_index("ball")
    for offset in range(lanes):
        counts[offset] = 0

    def copy(cluster, target, place):
        return pltpu.make_async_copy(
            points_ref.at[pl.ds(cluster * CLUSTER, CLUSTER)],
            target.at[pl.ds(place, CLUSTER)],
            sems.at[cluster],
        )

    for cluster in range(clusters):
        offset = owner_offset(dest_ref, cluster, clusters, lanes, me)
        rank = counts[offset]
        counts[offset] = rank + 1
        place = pl.multiple_of(rank * CLUSTER, CLUSTER)
        for which in range(lanes):

            @pl.when(offset == which)
            def _(cluster=cluster, which=which, place=place):
                copy(cluster, packed[which], place).start()

    for cluster in range(clusters):
        copy(cluster, packed[0], 0).wait()


def project_kernel(points_ref, gain_ref, wqk_ref, wv_ref, q_ref, k_ref, v_ref, pool_ref):
    rows, columns = points_ref.shape
    normed = rms_norm(points_ref[...], gain_ref[...])
    paired = dot32(normed, wqk_ref[...]).astype(bf16)
    values = dot32(normed, wv_ref[...]).astype(bf16)
    keys = paired[:, columns:]
    q_ref[...] = paired[:, :columns]
    k_ref[...] = keys
    v_ref[...] = values
    pooled = rows // POOL
    row = lax.broadcasted_iota(jnp.int32, (pooled, rows), 0)
    column = lax.broadcasted_iota(jnp.int32, (pooled, rows), 1)
    averaging = jnp.where(column // POOL == row, 1.0 / math.sqrt(POOL), 0.0).astype(bf16)
    pool_ref[:pooled] = dot32(averaging, keys).astype(bf16)
    pool_ref[pooled:] = dot32(averaging, values).astype(bf16)


def near_part_kernel(group, q_ref, k_ref, v_ref, o_ref, m_ref, l_ref, kt_ref, ve_ref):
    rows, columns = o_ref.shape[0], k_ref.shape[1]
    key_count = k_ref.shape[0]
    head_size = columns // HEADS
    per_tile = LANE_TILE // head_size
    tile = slice(group * LANE_TILE, (group + 1) * LANE_TILE)
    set_keys(kt_ref, 0, k_ref[:, tile])
    ve_ref[0, :, :LANE_TILE] = v_ref[:, tile]
    ve_ref[0, :, LANE_TILE:] = jnp.ones((key_count, LANE_TILE), bf16)
    kept = {}

    def finish(tag, head, mixed, total, row_max):
        for name, new in (("o", mixed), ("m", row_max), ("l", total)):
            kept[tag, name] = place_head(kept.get((tag, name)), head, per_tile, head_size, new)
        if head == per_tile - 1:
            block = pl.ds(tag, min(BLOCK, rows))
            o_ref[block] = kept.pop((tag, "o"))
            m_ref[block] = kept.pop((tag, "m"))
            l_ref[block] = kept.pop((tag, "l"))

    jobs = [
        (start, head, 0, key_count)
        for start in range(0, rows, BLOCK)
        for head in range(per_tile)
    ]
    run_heads(
        jobs,
        lambda start: q_ref[pl.ds(start, min(BLOCK, rows)), tile],
        kt_ref,
        ve_ref,
        head_size,
        finish,
    )


def near_kernel(parts, q_ref, k_ref, v_ref, pool_ref, *rest):
    partial = [rest[3 * part : 3 * part + 3] for part in range(parts)]
    out_ref, kt_ref, ve_ref = rest[3 * parts :]
    rows, columns = q_ref.shape
    local = k_ref.shape[0]
    regions = pool_ref.shape[0]
    pooled = pool_ref.shape[1] // 2
    total_keys = local + regions * pooled
    head_size = columns // HEADS
    per_tile = LANE_TILE // head_size
    early = partial[0][0].shape[0]
    factor = math.log2(math.e) / math.sqrt(head_size)
    set_keys(kt_ref, 0, k_ref[...])
    set_values(ve_ref, 0, v_ref[...])
    set_keys(kt_ref, local, jnp.concatenate([pool_ref[r, :pooled] for r in range(regions)], axis=0))
    set_values(
        ve_ref, local, jnp.concatenate([pool_ref[r, pooled:] for r in range(regions)], axis=0)
    )
    kept = {}

    def finish(tag, head, mixed, total, row_max):
        group = head // per_tile
        if tag < early:
            for name, new in (("o", mixed), ("m", row_max), ("l", total)):
                kept[tag, group, name] = place_head(
                    kept.get((tag, group, name)), head, per_tile, head_size, new
                )
        else:
            kept[tag, group, "o"] = place_head(
                kept.get((tag, group, "o")), head, per_tile, head_size, mixed / total
            )
        if head % per_tile < per_tile - 1:
            return
        block = pl.ds(tag, BLOCK)
        result = kept.pop((tag, group, "o"))
        if tag < early:
            o_ref, m_ref, l_ref = partial[group]
            new_max, new_total = kept.pop((tag, group, "m")), kept.pop((tag, group, "l"))
            old_max = m_ref[block]
            top = jnp.maximum(new_max, old_max)
            new_part = jnp.exp2((new_max - top) * factor)
            old_part = jnp.exp2((old_max - top) * factor)
            result = (result * new_part + o_ref[block] * old_part) / (
                new_total * new_part + l_ref[block] * old_part
            )
        out_ref[block, group * LANE_TILE : (group + 1) * LANE_TILE] = result.astype(bf16)

    jobs = [
        (start, head, local if start < early else 0, total_keys)
        for start in range(0, rows, BLOCK)
        for head in range(HEADS)
    ]
    run_heads(jobs, lambda start: q_ref[pl.ds(start, BLOCK)], kt_ref, ve_ref, head_size, finish)


def far_kernel(lanes, clusters, dest_ref, *rest):
    arrived = rest[:lanes]
    gain_ref, wqk_ref, wv_ref = rest[lanes : lanes + 3]
    leaving = rest[lanes + 3 : 2 * lanes + 3]
    x_ref, q_ref, y_ref, kt_ref, ve_ref, member, in_sems, out_sems = rest[2 * lanes + 3 :]
    rows, columns = x_ref.shape
    share = arrived[0].shape[0]
    me = lax.axis_index("ball")
    for offset in range(lanes):
        member[offset] = 0
    for cluster in range(clusters):
        member[owner_offset(dest_ref, cluster, clusters, lanes, me)] = 1
    places, place = [], 0
    for offset in range(lanes):
        places.append(pl.multiple_of(place * share, share))
        place = place + member[offset]

    def fetch(offset):
        return pltpu.make_async_copy(
            arrived[offset], x_ref.at[pl.ds(places[offset], share)], in_sems.at[offset]
        )

    def give(offset):
        return pltpu.make_async_copy(
            y_ref.at[pl.ds(places[offset], share)], leaving[offset], out_sems.at[offset]
        )

    def for_members(act):
        for offset in range(lanes):

            @pl.when(member[offset] == 1)
            def _(offset=offset):
                act(offset)

    for_members(lambda offset: fetch(offset).start())
    for_members(lambda offset: fetch(offset).wait())
    normed = rms_norm(x_ref[...], gain_ref[...])
    paired = dot32(normed, wqk_ref[...]).astype(bf16)
    q_ref[...] = paired[:, :columns]
    set_keys(kt_ref, 0, paired[:, columns:])
    set_values(ve_ref, 0, dot32(normed, wv_ref[...]).astype(bf16))

    def store(tag, group, result):
        y_ref[pl.ds(tag, BLOCK), group * LANE_TILE : (group + 1) * LANE_TILE] = result

    jobs = [(start, head, 0, rows) for start in range(0, rows, BLOCK) for head in range(HEADS)]
    full_attention(
        jobs, lambda start: q_ref[pl.ds(start, BLOCK)], kt_ref, ve_ref, columns, store
    )
    for_members(lambda offset: give(offset).start())
    for_members(lambda offset: give(offset).wait())


def finish_kernel(lanes, clusters, dest_ref, points_ref, near_ref, *rest):
    returned = rest[:lanes]
    wo_ref, gain_ref, up_ref, down_ref, out_ref, far_ref, counts, sems = rest[lanes:]
    me = lax.axis_index("ball")
    for offset in range(lanes):
        counts[offset] = 0

    def copy(cluster, source, place):
        return pltpu.make_async_copy(
            source.at[pl.ds(place, CLUSTER)],
            far_ref.at[pl.ds(cluster * CLUSTER, CLUSTER)],
            sems.at[cluster],
        )

    for cluster in range(clusters):
        offset = owner_offset(dest_ref, cluster, clusters, lanes, me)
        rank = counts[offset]
        counts[offset] = rank + 1
        place = pl.multiple_of(rank * CLUSTER, CLUSTER)
        for which in range(lanes):

            @pl.when(offset == which)
            def _(cluster=cluster, which=which, place=place):
                copy(cluster, returned[which], place).start()

    for cluster in range(clusters):
        copy(cluster, returned[0], 0).wait()
    rows = points_ref.shape[0]
    for start in range(0, rows, BLOCK):
        block = pl.ds(start, BLOCK)
        after = (
            points_ref[block].astype(f32)
            + dot32(near_ref[block], wo_ref[...])
            + dot32(far_ref[block], wo_ref[...])
        ).astype(bf16)
        normed = rms_norm(after, gain_ref[...])
        hidden = jax.nn.gelu(dot32(normed, up_ref[...]), approximate=True).astype(bf16)
        out_ref[block] = (after.astype(f32) + dot32(hidden, down_ref[...])).astype(bf16)


def per_device(
    points, gain_attn, w_query_key, w_value, w_out, gain_mlp, w_up, w_down, cluster_dest
):
    columns = points.shape[-1]
    flat = points.reshape(-1, columns)
    rows = flat.shape[0]
    lanes, regions = lax.axis_size("ball"), lax.axis_size("region")
    clusters = rows // CLUSTER
    share = 2 * clusters // lanes * CLUSTER
    pooled = rows // POOL
    dest = cluster_dest.reshape(clusters)
    gain_first = gain_attn.reshape(1, columns)
    gain_second = gain_mlp.reshape(1, columns)
    groups = columns // LANE_TILE
    early = rows // 2
    wide = jax.ShapeDtypeStruct((rows, columns), bf16)
    piece = jax.ShapeDtypeStruct((share, columns), bf16)

    def attention_cost(queries, keys, heads):
        return cost(4 * heads * queries * keys * 256, 4 * rows * columns, heads * queries * keys)

    def shift(data, offset):
        return lax.ppermute(data, "ball", [(i, (i + offset) % lanes) for i in range(lanes)])

    packed = pl.pallas_call(
        functools.partial(pack_kernel, lanes, clusters),
        out_shape=[piece] * lanes,
        in_specs=[in_smem(), anywhere()],
        out_specs=[anywhere()] * lanes,
        scratch_shapes=[
            pltpu.SMEM((lanes,), jnp.int32),
            pltpu.SemaphoreType.DMA((clusters,)),
        ],
        cost_estimate=cost(0, 4 * rows * columns),
        compiler_params=params(),
        name="pack",
    )(dest, flat)
    arrived = [packed[0]] + [shift(packed[d], d) for d in range(1, lanes)]

    query, keys, values, pool = pl.pallas_call(
        project_kernel,
        out_shape=[wide] * 3 + [jax.ShapeDtypeStruct((2 * pooled, columns), bf16)],
        in_specs=[in_vmem()] * 4,
        out_specs=[in_vmem()] * 4,
        cost_estimate=cost(6 * rows * columns * columns, 10 * rows * columns),
        compiler_params=params(),
        name="project",
    )(flat, gain_first, w_query_key, w_value)

    gathered = pool.reshape(1, 2 * pooled, columns)
    step = regions // 2
    while step:
        other = lax.ppermute(gathered, "region", [(i, i ^ step) for i in range(regions)])
        gathered = jnp.concatenate([gathered, other], axis=0)
        step //= 2

    partial = []
    for group in range(groups):
        partial += pl.pallas_call(
            functools.partial(near_part_kernel, group),
            out_shape=[jax.ShapeDtypeStruct((early, LANE_TILE), f32)] * 3,
            in_specs=[in_vmem()] * 3,
            out_specs=[in_vmem()] * 3,
            scratch_shapes=[
                pltpu.VMEM((LANE_TILE, rows), bf16),
                pltpu.VMEM((1, rows, 2 * LANE_TILE), bf16),
            ],
            cost_estimate=attention_cost(early, rows, HEADS // groups),
            compiler_params=params(),
            name="near_part",
        )(query, keys, values)

    leaving = pl.pallas_call(
        functools.partial(far_kernel, lanes, clusters),
        out_shape=[piece] * lanes,
        in_specs=[in_smem()] + [anywhere()] * lanes + [in_vmem()] * 3,
        out_specs=[anywhere()] * lanes,
        scratch_shapes=[
            pltpu.VMEM((rows, columns), bf16),
            pltpu.VMEM((rows, columns), bf16),
            pltpu.VMEM((rows, columns), bf16),
            pltpu.VMEM((columns, rows), bf16),
            pltpu.VMEM((groups, rows, 2 * LANE_TILE), bf16),
            pltpu.SMEM((lanes,), jnp.int32),
            pltpu.SemaphoreType.DMA((lanes,)),
            pltpu.SemaphoreType.DMA((lanes,)),
        ],
        cost_estimate=attention_cost(rows, rows, HEADS),
        compiler_params=params(),
        name="far",
    )(dest, *arrived, gain_first, w_query_key, w_value)
    returned = [leaving[0]] + [shift(leaving[d], lanes - d) for d in range(1, lanes)]

    near_keys = rows + regions * pooled
    near = pl.pallas_call(
        functools.partial(near_kernel, groups),
        out_shape=wide,
        in_specs=[in_vmem()] * (4 + 3 * groups),
        out_specs=in_vmem(),
        scratch_shapes=[
            pltpu.VMEM((columns, near_keys), bf16),
            pltpu.VMEM((groups, near_keys, 2 * LANE_TILE), bf16),
        ],
        cost_estimate=attention_cost(rows, near_keys - rows // 2, HEADS),
        compiler_params=params(),
        name="near",
    )(query, keys, values, gathered, *partial)

    block_out = pl.pallas_call(
        functools.partial(finish_kernel, lanes, clusters),
        out_shape=wide,
        in_specs=[in_smem()] + [in_vmem()] * 2 + [anywhere()] * lanes + [in_vmem()] * 4,
        out_specs=in_vmem(),
        scratch_shapes=[
            pltpu.VMEM((rows, columns), bf16),
            pltpu.SMEM((lanes,), jnp.int32),
            pltpu.SemaphoreType.DMA((clusters,)),
        ],
        cost_estimate=cost(20 * rows * columns * columns, 8 * rows * columns),
        compiler_params=params(),
        name="finish",
    )(dest, flat, near, *returned, w_out, gain_second, w_up, w_down)
    return block_out.reshape(points.shape)


def solution(mesh):
    placed = (
        P("ball", "region", None, None),
        P(),
        P(),
        P(),
        P(),
        P(),
        P(),
        P(),
        P("ball", "region", None),
    )
    return jax.shard_map(
        per_device,
        mesh=mesh,
        in_specs=placed,
        out_specs=P("ball", "region", None, None),
        check_vma=False,
    )
```

time: 156 us -> 57.4 us (0.37); the launches traced: 153 us -> 57.2 us
  matrix products: 73.6 us -> 0 us
  Pallas kernels: 0 us -> 35.9 us
  blocking collectives: 28.6 us -> 0 us
  other arithmetic: 18.7 us -> 0.1 us
  local copies, waits for them, and re-layouts: 18.2 us -> 4.27 us
  waiting for transfers between devices: 0.01 us -> 2.73 us
    dot_general x59 -> x0, matrix products: 73.6 us -> none  [the longest x24 31.6 us: one_head(): jnp.einsum('nm,dm->dn', weights, value_head, preferred_element_type=jnp.f...]
    pallas_call x0 -> x7, Pallas kernels: none -> 35.9 us  [the longest x1 11.5 us: per_device(): pl.pallas_call(functools.partial(far_kernel, lanes, clusters), out_shape=...]
    all_gather x2 -> x0, blocking collectives: 28.6 us -> none  [the longest x1 14.4 us: per_device(): lax.all_gather(pooled(key_cols), 'region', axis=1, tiled=True)]
    reduce_sum x27 -> x0, other arithmetic: 15.2 us -> none  [the longest x16 11.7 us: one_head(): total = exponents[0].sum(axis=1, keepdims=True)]
    ppermute x0 -> x9, starting transfers between devices: none -> 13.8 us  [the longest x6 8.01 us: shift(): lax.ppermute(data, 'ball', [(i, (i + offset) % lanes) for i in range(lane...]
    all_to_all x3 -> x0, starting transfers between devices: 13.6 us -> none  [the longest x1 5.17 us: per_device(): lax.all_to_all(sent_ids, 'ball', split_axis=0, concat_axis=0, tiled=True)]
    reshape x7 -> x0, local copies, waits for them, and re-layouts: 7 us -> none  [the longest x1 2.35 us: per_device(): packed.astype(jnp.bfloat16).reshape(lanes, capacity * CLUSTER, inner)]
    convert_element_type x4 -> x0, local copies, waits for them, and re-layouts: 3.94 us -> none  [the longest x2 2.61 us: per_device(): flat.astype(jnp.float32) + near_out]
  transfers between devices with their start and end apart: 3 -> 9, of which waited for: 0 -> 4; matrix products, arithmetic and copies ran while one was open for 50% -> 0% of each run, Pallas kernels for 0% -> 52%
where the time goes in v1:
time: 57.4 us; the launch traced here: 57.2 us
  Pallas kernels  35.9 us (63%)
  starting transfers between devices  13.8 us (24%)
  local copies, waits for them, and re-layouts  4.27 us (7%)
  waiting for transfers between devices  2.73 us (5%)
    pallas_call x1, Pallas kernels, per_device(): pl.pallas_call(functools.partial(far_kernel, lanes, clusters), out_shape=...  11.5 us
    pallas_call x1, Pallas kernels, per_device(): pl.pallas_call(functools.partial(near_kernel, groups), out_shape=wide, in...  10.7 us
    ppermute x6, starting transfers between devices, shift(): lax.ppermute(data, 'ball', [(i, (i + offset) % lanes) for i in range(lane...  8.01 us
    pallas_call x2, Pallas kernels, per_device(): pl.pallas_call(functools.partial(near_part_kernel, group), out_shape=[jax...  5.82 us
    ppermute x3, starting transfers between devices, per_device(): lax.ppermute(gathered, 'region', [(i, i ^ step) for i in range(regions)])  5.79 us
    pallas_call x1, Pallas kernels, per_device(): pl.pallas_call(functools.partial(finish_kernel, lanes, clusters), out_sha...  5.14 us
    unnamed x24, local copies, waits for them, and re-layouts  4.27 us
    ppermute x6, waiting for transfers between devices, shift(): lax.ppermute(data, 'ball', [(i, (i + offset) % lanes) for i in range(lane...  2.27 us
  transfers between devices with their start and end apart: 9, of which 4 were waited for; matrix products, arithmetic and copies ran while one was open for 0% of the time, Pallas kernels for 52%

profile of v1, /device:TPU:0, one launch (start us, length us, event | category | flops | bytes accessed | tf_op | source)
XLA Modules:
  0.0 57.2 jit_solution(11384330396505053933)
XLA Ops:
  0.0 0.7 %copy-done.10 = f32[256]{0:T(256)S(1)} copy-done((f32[256]{0:T(256)S(1)}, f32[256]{0:T(256)}, u32[]{:S(2)}) %copy-start.10) | copy-done | bytes 1048
  0.7 1.0 %copy-done = bf16[1,1,1024,256]{3,2,1,0:T(8,128)(2,1)S(1)} copy-done((bf16[1,1,1024,256]{3,2,1,0:T(8,128)(2,1)S(1)}, bf16[1,1,1024,256]{3,2,1,0:T(8,128)(2,1)}, u32[]{:S(2)}) %copy-start) | copy-done | bytes 524312
  1.7 0.9 %copy-done.5 = bf16[256,512]{1,0:T(8,128)(2,1)S(1)} copy-done((bf16[256,512]{1,0:T(8,128)(2,1)S(1)}, bf16[256,512]{1,0:T(8,128)(2,1)}, u32[]{:S(2)}) %copy-start.5) | copy-done | bytes 262168
  2.7 0.9 %copy-done.7 = bf16[256,256]{1,0:T(8,128)(2,1)S(1)} copy-done((bf16[256,256]{1,0:T(8,128)(2,1)S(1)}, bf16[256,256]{1,0:T(8,128)(2,1)}, u32[]{:S(2)}) %copy-start.7) | copy-done | bytes 131096
  3.6 0.9 %project.1 = (bf16[1024,256]{1,0:T(8,128)(2,1)S(1)}, bf16[1024,256]{1,0:T(8,128)(2,1)S(1)}, bf16[1024,256]{1,0:T(8,128)(2,1)S(1)}, bf16[128,256]{1,0:T(8,128)(2,1)S(1)}) custom-call(bf16[1024,256]{1,0:T(8,128)(2,1)S(1)} %bitcast.10, f32[1,256]{1,0:T(1,128)S(1)} %bitcast.16, bf16[256,512]{1,0:T(8,128)(2,1)S(1)} %copy-done.5, bf16[256,256]{1,0:T(8,128)(2,1)S(1)} %copy-done.7), custom_call_target="tpu_custom_call" | custom-call | flops 402653184 | bytes 2621440 | tf_op jit(solution)/shard_map/project/pallas_call | solution.py:386
  4.5 4.1 %collective-permute-start = (bf16[1,128,256]{2,1,0:T(8,128)(2,1)S(1)}, bf16[1,128,256]{2,1,0:T(8,128)(2,1)S(1)}, u32[]{:S(2)}, u32[]{:S(2)}) collective-permute-start(bf16[1,128,256]{2,1,0:T(8,128)(2,1)S(1)} %bitcast.6), channel_id=1, source_target_pairs={{0,4},{1,5},{2,6},{3,7},{4,0},{5,1},{6,2},{7,3},{8,12},{9,13},{10,... | collective-permute-start | bytes 196616 | tf_op jit(solution)/shard_map/ppermute | solution.py:399
  8.6 1.9 %pack.1 = (bf16[512,256]{1,0:T(8,128)(2,1)S(1)}, bf16[512,256]{1,0:T(8,128)(2,1)S(1)}, bf16[512,256]{1,0:T(8,128)(2,1)S(1)}, bf16[512,256]{1,0:T(8,128)(2,1)S(1)}) custom-call(s32[16]{0:T(128)S(1)} %bitcast.13, bf16[1024,256]{1,0:T(8,128)(2,1)S(1)} %bitcast.11), custom_call_target="tpu_custom_call" | custom-call | bytes 1048576 | tf_op jit(solution)/shard_map/pack/pallas_call | solution.py:371
  10.5 1.5 %collective-permute-start.3 = (bf16[512,256]{1,0:T(8,128)(2,1)S(1)}, bf16[512,256]{1,0:T(8,128)(2,1)S(1)}, u32[]{:S(2)}, u32[]{:S(2)}) collective-permute-start(bf16[512,256]{1,0:T(8,128)(2,1)S(1)} %get-tuple-element.34), channel_id=1, source_target_pairs={{0,8},{8,16},{16,24},{24,0},{1,9},{9,17},{17,25},{25,1},{2,10},{10... | collective-permute-start | bytes 786440 | tf_op jit(solution)/shard_map/ppermute | solution.py:369
  12.1 1.5 %collective-permute-start.4 = (bf16[512,256]{1,0:T(8,128)(2,1)S(1)}, bf16[512,256]{1,0:T(8,128)(2,1)S(1)}, u32[]{:S(2)}, u32[]{:S(2)}) collective-permute-start(bf16[512,256]{1,0:T(8,128)(2,1)S(1)} %get-tuple-element.35), channel_id=1, source_target_pairs={{0,16},{8,24},{16,0},{24,8},{1,17},{9,25},{17,1},{25,9},{2,18},{10... | collective-permute-start | bytes 786440 | tf_op jit(solution)/shard_map/ppermute | solution.py:369
  13.6 1.4 %collective-permute-start.5 = (bf16[512,256]{1,0:T(8,128)(2,1)S(1)}, bf16[512,256]{1,0:T(8,128)(2,1)S(1)}, u32[]{:S(2)}, u32[]{:S(2)}) collective-permute-start(bf16[512,256]{1,0:T(8,128)(2,1)S(1)} %get-tuple-element.36), channel_id=1, source_target_pairs={{0,24},{8,0},{16,8},{24,16},{1,25},{9,1},{17,9},{25,17},{2,26},{10... | collective-permute-start | bytes 786440 | tf_op jit(solution)/shard_map/ppermute | solution.py:369
  15.0 2.9 %near_part.3 = (f32[512,128]{1,0:T(8,128)S(1)}, f32[512,128]{1,0:T(8,128)S(1)}, f32[512,128]{1,0:T(8,128)S(1)}) custom-call(bf16[1024,256]{1,0:T(8,128)(2,1)S(1)} %get-tuple-element.23.q_ref, bf16[1024,256]{1,0:T(8,128)(2,1)S(1)} %get-tuple-element.24.k_ref, bf16[1024,256]{1,0:T(8,128)(2,1)S(1)} %get-tuple-element.25.v_ref), custom_call_target="tpu_custom_call" | custom-call | flops 2147483648 | bytes 1048576 | tf_op jit(solution)/shard_map/near_part/pallas_call | solution.py:405
  18.0 1.6 %collective-permute-start.1 = (bf16[2,128,256]{2,1,0:T(8,128)(2,1)S(1)}, bf16[2,128,256]{2,1,0:T(8,128)(2,1)S(1)}, u32[]{:S(2)}, u32[]{:S(2)}) collective-permute-start(bf16[2,128,256]{2,1,0:T(8,128)(2,1)S(1)} %pad_maximum_fusion.2), channel_id=1, source_target_pairs={{0,2},{1,3},{2,0},{3,1},{4,6},{5,7},{6,4},{7,5},{8,10},{9,11},{10,... | collective-permute-start | bytes 393224 | tf_op jit(solution)/shard_map/ppermute | solution.py:399
  19.6 2.9 %near_part.2 = (f32[512,128]{1,0:T(8,128)S(1)}, f32[512,128]{1,0:T(8,128)S(1)}, f32[512,128]{1,0:T(8,128)S(1)}) custom-call(bf16[1024,256]{1,0:T(8,128)(2,1)S(1)} %get-tuple-element.23.q_ref, bf16[1024,256]{1,0:T(8,128)(2,1)S(1)} %get-tuple-element.24.k_ref, bf16[1024,256]{1,0:T(8,128)(2,1)S(1)} %get-tuple-element.25.v_ref), custom_call_target="tpu_custom_call" | custom-call | flops 2147483648 | bytes 1048576 | tf_op jit(solution)/shard_map/near_part/pallas_call | solution.py:405
  22.6 0.5 collective-permute-done.1
  23.1 1.7 %collective-permute-done.4.rest_2_ = bf16[512,256]{1,0:T(8,128)(2,1)S(1)} collective-permute-done((bf16[512,256]{1,0:T(8,128)(2,1)S(1)}, bf16[512,256]{1,0:T(8,128)(2,1)S(1)}, u32[]{:S(2)}, u32[]{:S(2)}) %collective-permute-start.4) | collective-permute-done | bytes 262176 | tf_op jit(solution)/shard_map/ppermute | solution.py:369
  24.9 0.1 collective-permute-done.5.rest_3_
  25.0 11.5 %far.1 = (bf16[512,256]{1,0:T(8,128)(2,1)S(1)}, bf16[512,256]{1,0:T(8,128)(2,1)S(1)}, bf16[512,256]{1,0:T(8,128)(2,1)S(1)}, bf16[512,256]{1,0:T(8,128)(2,1)S(1)}) custom-call(s32[16]{0:T(128)S(1)} %bitcast.14, bf16[512,256]{1,0:T(8,128)(2,1)S(1)} %get-tuple-element.33.rest_0_, bf16[512,256]{1,0:T(8,128)(2,1)S(1)} %collective-permute-done.3.rest_1_, ...), custom_call_target="tpu_custom_call" | custom-call | flops 8589934592 | bytes 1048576 | tf_op jit(solution)/shard_map/far/pallas_call | solution.py:419
  36.4 1.7 %collective-permute-start.6 = (bf16[512,256]{1,0:T(8,128)(2,1)S(1)}, bf16[512,256]{1,0:T(8,128)(2,1)S(1)}, u32[]{:S(2)}, u32[]{:S(2)}) collective-permute-start(bf16[512,256]{1,0:T(8,128)(2,1)S(1)} %get-tuple-element.38), channel_id=1, source_target_pairs={{0,24},{8,0},{16,8},{24,16},{1,25},{9,1},{17,9},{25,17},{2,26},{10... | collective-permute-start | bytes 786440 | tf_op jit(solution)/shard_map/ppermute | solution.py:369
  38.1 1.5 %collective-permute-start.7 = (bf16[512,256]{1,0:T(8,128)(2,1)S(1)}, bf16[512,256]{1,0:T(8,128)(2,1)S(1)}, u32[]{:S(2)}, u32[]{:S(2)}) collective-permute-start(bf16[512,256]{1,0:T(8,128)(2,1)S(1)} %get-tuple-element.39), channel_id=1, source_target_pairs={{0,16},{8,24},{16,0},{24,8},{1,17},{9,25},{17,1},{25,9},{2,18},{10... | collective-permute-start | bytes 786440 | tf_op jit(solution)/shard_map/ppermute | solution.py:369
  39.7 0.3 collective-permute-start.8
  40.1 10.7 %near.1.near_ref = bf16[1024,256]{1,0:T(8,128)(2,1)S(1)} custom-call(bf16[1024,256]{1,0:T(8,128)(2,1)S(1)} %get-tuple-element.23.q_ref, bf16[1024,256]{1,0:T(8,128)(2,1)S(1)} %get-tuple-element.24.k_ref, bf16[1024,256]{1,0:T(8,128)(2,1)S(1)} %get-tuple-element.25.v_ref, bf16[8,128,256]{2,1,0:T(8,128)(2,1)S(1)} %pad_maximum_fusion.pool_ref, ...), custom_call_target="tpu_custom_call" | custom-call | flops 8589934592 | bytes 1048576 | tf_op jit(solution)/shard_map/near/pallas_call | solution.py:441
  50.8 0.4 collective-permute-done.8.rest_3_
  51.2 0.7 %copy-done.11 = f32[256]{0:T(256)S(1)} copy-done((f32[256]{0:T(256)S(1)}, f32[256]{0:T(256)}, u32[]{:S(2)}) %copy-start.11) | copy-done | bytes 1048
  51.9 5.1 %finish.1 = bf16[1024,256]{1,0:T(8,128)(2,1)} custom-call(s32[16]{0:T(128)S(1)} %bitcast.15, bf16[1024,256]{1,0:T(8,128)(2,1)S(1)} %bitcast.12, bf16[1024,256]{1,0:T(8,128)(2,1)S(1)} %near.1.near_ref, bf16[512,256]{1,0:T(8,128)(2,1)S(1)} %get-tuple-element.37.rest_0_, bf16[512,256]{1,0:T(8,128)(2,1)S(1)} %collective-permute-done.6.rest_1_, ...), custom_call_target="tpu_custom_call" | custom-call | flops 1342177280 | bytes 2097152 | tf_op jit(solution)/shard_map/finish/pallas_call | solution.py:455
  (28 shorter events, 0.2 us)
Async XLA Ops:
  0.0 0.7 %copy-start.10 = (f32[256]{0:T(256)S(1)}, f32[256]{0:T(256)}, u32[]{:S(2)}) copy-start(f32[256]{0:T(256)} %param.10) | copy-start | bytes 3076
  0.7 1.0 %copy-start = (bf16[1,1,1024,256]{3,2,1,0:T(8,128)(2,1)S(1)}, bf16[1,1,1024,256]{3,2,1,0:T(8,128)(2,1)}, u32[]{:S(2)}) copy-start(bf16[1,1,1024,256]{3,2,1,0:T(8,128)(2,1)} %param.9) | copy-start | bytes 1572868
  1.7 0.9 %copy-start.5 = (bf16[256,512]{1,0:T(8,128)(2,1)S(1)}, bf16[256,512]{1,0:T(8,128)(2,1)}, u32[]{:S(2)}) copy-start(bf16[256,512]{1,0:T(8,128)(2,1)} %rest_5_.1) | copy-start | bytes 786436
  2.7 0.9 %copy-start.7 = (bf16[256,256]{1,0:T(8,128)(2,1)S(1)}, bf16[256,256]{1,0:T(8,128)(2,1)}, u32[]{:S(2)}) copy-start(bf16[256,256]{1,0:T(8,128)(2,1)} %rest_6_.2) | copy-start | bytes 393220
  4.5 4.1 %copy-start.2 = (s32[1,1,16]{2,1,0:T(1,128)S(1)}, s32[1,1,16]{2,1,0:T(1,128)}, u32[]{:S(2)}) copy-start(s32[1,1,16]{2,1,0:T(1,128)} %param.17) | copy-start | bytes 196
  4.5 13.4 %collective-permute-start = (bf16[1,128,256]{2,1,0:T(8,128)(2,1)S(1)}, bf16[1,128,256]{2,1,0:T(8,128)(2,1)S(1)}, u32[]{:S(2)}, u32[]{:S(2)}) collective-permute-start(bf16[1,128,256]{2,1,0:T(8,128)(2,1)S(1)} %bitcast.6), channel_id=1, source_target_pairs={{0,4},{1,5},{2,6},{3,7},{4,0},{5,1},{6,2},{7,3},{8,12},{9,13},{10,... | collective-permute-start | bytes 196616 | tf_op jit(solution)/shard_map/ppermute | solution.py:399
  10.5 12.6 %collective-permute-start.3 = (bf16[512,256]{1,0:T(8,128)(2,1)S(1)}, bf16[512,256]{1,0:T(8,128)(2,1)S(1)}, u32[]{:S(2)}, u32[]{:S(2)}) collective-permute-start(bf16[512,256]{1,0:T(8,128)(2,1)S(1)} %get-tuple-element.34), channel_id=1, source_target_pairs={{0,8},{8,16},{16,24},{24,0},{1,9},{9,17},{17,25},{25,1},{2,10},{10... | collective-permute-start | bytes 786440 | tf_op jit(solution)/shard_map/ppermute | solution.py:369
  12.1 12.8 %collective-permute-start.4 = (bf16[512,256]{1,0:T(8,128)(2,1)S(1)}, bf16[512,256]{1,0:T(8,128)(2,1)S(1)}, u32[]{:S(2)}, u32[]{:S(2)}) collective-permute-start(bf16[512,256]{1,0:T(8,128)(2,1)S(1)} %get-tuple-element.35), channel_id=1, source_target_pairs={{0,16},{8,24},{16,0},{24,8},{1,17},{9,25},{17,1},{25,9},{2,18},{10... | collective-permute-start | bytes 786440 | tf_op jit(solution)/shard_map/ppermute | solution.py:369
  13.6 11.3 %collective-permute-start.5 = (bf16[512,256]{1,0:T(8,128)(2,1)S(1)}, bf16[512,256]{1,0:T(8,128)(2,1)S(1)}, u32[]{:S(2)}, u32[]{:S(2)}) collective-permute-start(bf16[512,256]{1,0:T(8,128)(2,1)S(1)} %get-tuple-element.36), channel_id=1, source_target_pairs={{0,24},{8,0},{16,8},{24,16},{1,25},{9,1},{17,9},{25,17},{2,26},{10... | collective-permute-start | bytes 786440 | tf_op jit(solution)/shard_map/ppermute | solution.py:369
  18.0 5.0 %collective-permute-start.1 = (bf16[2,128,256]{2,1,0:T(8,128)(2,1)S(1)}, bf16[2,128,256]{2,1,0:T(8,128)(2,1)S(1)}, u32[]{:S(2)}, u32[]{:S(2)}) collective-permute-start(bf16[2,128,256]{2,1,0:T(8,128)(2,1)S(1)} %pad_maximum_fusion.2), channel_id=1, source_target_pairs={{0,2},{1,3},{2,0},{3,1},{4,6},{5,7},{6,4},{7,5},{8,10},{9,11},{10,... | collective-permute-start | bytes 393224 | tf_op jit(solution)/shard_map/ppermute | solution.py:399
  22.5 2.4 %copy-start.6 = (bf16[256,512]{1,0:T(8,128)(2,1)S(1)}, bf16[256,512]{1,0:T(8,128)(2,1)}, u32[]{:S(2)}) copy-start(bf16[256,512]{1,0:T(8,128)(2,1)} %rest_5_.1) | copy-start | bytes 786436
  22.6 2.4 %copy-start.8 = (bf16[256,256]{1,0:T(8,128)(2,1)S(1)}, bf16[256,256]{1,0:T(8,128)(2,1)}, u32[]{:S(2)}) copy-start(bf16[256,256]{1,0:T(8,128)(2,1)} %rest_6_.2) | copy-start | bytes 393220
  23.1 16.9 %collective-permute-start.2 = (bf16[4,128,256]{2,1,0:T(8,128)(2,1)S(1)}, bf16[4,128,256]{2,1,0:T(8,128)(2,1)S(1)}, u32[]{:S(2)}, u32[]{:S(2)}) collective-permute-start(bf16[4,128,256]{2,1,0:T(8,128)(2,1)S(1)} %pad_maximum_fusion.1), channel_id=1, source_target_pairs={{0,1},{1,0},{2,3},{3,2},{4,5},{5,4},{6,7},{7,6},{8,9},{9,8},{10,11... | collective-permute-start | bytes 786440 | tf_op jit(solution)/shard_map/ppermute | solution.py:399
  36.4 14.3 %collective-permute-start.6 = (bf16[512,256]{1,0:T(8,128)(2,1)S(1)}, bf16[512,256]{1,0:T(8,128)(2,1)S(1)}, u32[]{:S(2)}, u32[]{:S(2)}) collective-permute-start(bf16[512,256]{1,0:T(8,128)(2,1)S(1)} %get-tuple-element.38), channel_id=1, source_target_pairs={{0,24},{8,0},{16,8},{24,16},{1,25},{9,1},{17,9},{25,17},{2,26},{10... | collective-permute-start | bytes 786440 | tf_op jit(solution)/shard_map/ppermute | solution.py:369
  38.1 12.6 %collective-permute-start.7 = (bf16[512,256]{1,0:T(8,128)(2,1)S(1)}, bf16[512,256]{1,0:T(8,128)(2,1)S(1)}, u32[]{:S(2)}, u32[]{:S(2)}) collective-permute-start(bf16[512,256]{1,0:T(8,128)(2,1)S(1)} %get-tuple-element.39), channel_id=1, source_target_pairs={{0,16},{8,24},{16,0},{24,8},{1,17},{9,25},{17,1},{25,9},{2,18},{10... | collective-permute-start | bytes 786440 | tf_op jit(solution)/shard_map/ppermute | solution.py:369
  39.7 11.5 %collective-permute-start.8 = (bf16[512,256]{1,0:T(8,128)(2,1)S(1)}, bf16[512,256]{1,0:T(8,128)(2,1)S(1)}, u32[]{:S(2)}, u32[]{:S(2)}) collective-permute-start(bf16[512,256]{1,0:T(8,128)(2,1)S(1)} %get-tuple-element.40), channel_id=1, source_target_pairs={{0,8},{8,16},{16,24},{24,0},{1,9},{9,17},{17,25},{25,1},{2,10},{10... | collective-permute-start | bytes 786440 | tf_op jit(solution)/shard_map/ppermute | solution.py:369
  40.0 11.2 %copy-start.1 = (bf16[1,1,1024,256]{3,2,1,0:T(8,128)(2,1)S(1)}, bf16[1,1,1024,256]{3,2,1,0:T(8,128)(2,1)}, u32[]{:S(2)}) copy-start(bf16[1,1,1024,256]{3,2,1,0:T(8,128)(2,1)} %param.9) | copy-start | bytes 1572868
  40.0 11.2 %copy-start.3 = (bf16[256,1024]{1,0:T(8,128)(2,1)S(1)}, bf16[256,1024]{1,0:T(8,128)(2,1)}, u32[]{:S(2)}) copy-start(bf16[256,1024]{1,0:T(8,128)(2,1)} %rest_6_.3) | copy-start | bytes 1572868
  40.0 11.2 %copy-start.4 = (bf16[1024,256]{1,0:T(8,128)(2,1)S(1)}, bf16[1024,256]{1,0:T(8,128)(2,1)}, u32[]{:S(2)}) copy-start(bf16[1024,256]{1,0:T(8,128)(2,1)} %rest_7_.1) | copy-start | bytes 1572868
  40.1 11.2 %copy-start.9 = (bf16[256,256]{1,0:T(8,128)(2,1)S(1)}, bf16[256,256]{1,0:T(8,128)(2,1)}, u32[]{:S(2)}) copy-start(bf16[256,256]{1,0:T(8,128)(2,1)} %rest_4_.1) | copy-start | bytes 393220
  51.2 0.7 %copy-start.11 = (f32[256]{0:T(256)S(1)}, f32[256]{0:T(256)}, u32[]{:S(2)}) copy-start(f32[256]{0:T(256)} %param.14) | copy-start | bytes 3076

commit v2 on v0

v2 whole, which is shorter than its diff:
```python
import functools
import math

import jax
import jax.numpy as jnp
from jax import lax
from jax.experimental import pallas as pl
from jax.experimental.pallas import tpu as pltpu
from jax.sharding import PartitionSpec as P

HEADS = 8
CLUSTER = 64
POOL = 16
TILE = 128
SLOW_BLOCK = 256
SAFE_EXPONENT = 104.0
VMEM_LIMIT = 48 * 1024 * 1024

bf16 = jnp.bfloat16
f32 = jnp.float32


def in_vmem():
    return pl.BlockSpec(memory_space=pltpu.VMEM)


def in_smem():
    return pl.BlockSpec(memory_space=pltpu.SMEM)


def anywhere():
    return pl.BlockSpec(memory_space=pl.ANY)


def params():
    return pltpu.CompilerParams(vmem_limit_bytes=VMEM_LIMIT)


def cost(flops, moved, transcendentals=0):
    return pl.CostEstimate(
        flops=int(flops), bytes_accessed=int(moved), transcendentals=int(transcendentals)
    )


def rms_norm(rows, gain):
    widened = rows.astype(f32)
    scaling = lax.rsqrt(jnp.mean(widened * widened, axis=1, keepdims=True) + 1e-06)
    return (widened * scaling * gain).astype(bf16)


def dot32(left, right):
    return jnp.dot(left, right, preferred_element_type=f32)


def packed_places(dest_ref, clusters, lanes, slots, counts):
    me = lax.axis_index("ball")
    capacity = 2 * clusters // lanes
    offsets = []
    for offset in range(lanes):
        slots[offset] = 0
        counts[offset] = 0
    for cluster in range(clusters):
        offset = lax.rem(dest_ref[cluster] // clusters - me + lanes, lanes)
        slots[offset] = 1
        offsets.append(offset)
    if capacity * 2 == clusters:
        low, high = offsets[0], offsets[0]
        for offset in offsets[1:]:
            low, high = jnp.minimum(low, offset), jnp.maximum(high, offset)
        swap = high - low > lanes // 2
        slots[low] = jnp.where(swap, 1, 0)
        slots[high] = jnp.where(swap, 0, 1)
        across = high - low == lanes // 2
    else:
        taken = 0
        for offset in range(lanes):
            here = slots[offset]
            slots[offset] = taken
            taken = taken + here
        across = None
    places = []
    for offset in offsets:
        rank = counts[offset]
        counts[offset] = rank + 1
        place = (slots[offset] * capacity + rank) * CLUSTER
        places.append(pl.multiple_of(place, CLUSTER))
    return places, across


def factor_of(head_size):
    return math.log2(math.e) / math.sqrt(head_size)


def extended_values(values, head_size):
    columns, rows = values.shape[1], values.shape[0]
    turned = values.T
    ones = jnp.ones((16, rows), bf16)
    return [
        jnp.concatenate([turned[h * head_size : (h + 1) * head_size], ones], axis=0)
        for h in range(columns // head_size)
    ]


def masked_query(query, head, head_size):
    row = lax.broadcasted_iota(jnp.int32, (TILE, 1), 0) // head_size
    return jnp.where(row == head % (TILE // head_size), query, bf16(0))


def run_jobs(jobs, ahead=1):
    waiting = [scores() for scores, _ in jobs[:ahead]]
    for index, (_, finish) in enumerate(jobs):
        if index + ahead < len(jobs):
            waiting.append(jobs[index + ahead][0]())
        finish(waiting.pop(0))


def plain_weights(scores, head_size):
    return jnp.exp2(scores * factor_of(head_size)).astype(bf16)


def head_norms(rows, head_size):
    columns = rows.shape[1]
    widened = rows.astype(f32)
    channel = lax.broadcasted_iota(jnp.int32, (columns, TILE), 0) // head_size
    head = lax.broadcasted_iota(jnp.int32, (columns, TILE), 1)
    members = (channel == head).astype(bf16)
    return jnp.max(dot32((widened * widened).astype(bf16), members), axis=0, keepdims=True)


def exponents_safe(query_norms, key_norms, head_size):
    limit = (SAFE_EXPONENT / factor_of(head_size)) ** 2
    return jnp.max(query_norms * key_norms) <= limit


def shifted_attention(qt_ref, start, count, parts, head_size, out_ref):
    per_tile = TILE // head_size

    def step(index, carry):
        head = index % HEADS
        block = pl.multiple_of(start + index // HEADS * SLOW_BLOCK, SLOW_BLOCK)
        tile = pl.multiple_of(head // per_tile * TILE, TILE)
        query = masked_query(
            qt_ref[pl.ds(tile, TILE), pl.ds(block, SLOW_BLOCK)], head, head_size
        )
        loaded = [part(pl.ds(tile, TILE), head) for part in parts]
        scores = [dot32(keys, query) for keys, _ in loaded]
        top = jnp.max(scores[0], axis=0, keepdims=True)
        for more in scores[1:]:
            top = jnp.maximum(top, jnp.max(more, axis=0, keepdims=True))
        mixed = 0.0
        for block_scores, (_, values) in zip(scores, loaded):
            mixed = mixed + dot32(values, plain_weights(block_scores - top, head_size))
        rows = pl.ds(pl.multiple_of(head * head_size, head_size), head_size)
        out_ref[rows, pl.ds(block, SLOW_BLOCK)] = (
            mixed[:head_size] / mixed[head_size : head_size + 1]
        ).astype(bf16)
        return carry

    lax.fori_loop(0, HEADS * (count // SLOW_BLOCK), step, 0)


def pack_kernel(lanes, clusters, dest_ref, points_ref, packed_ref, slots, counts, sems):
    places, _ = packed_places(dest_ref, clusters, lanes, slots, counts)
    copies = [
        pltpu.make_async_copy(
            points_ref.at[pl.ds(cluster * CLUSTER, CLUSTER)],
            packed_ref.at[pl.ds(place, CLUSTER)],
            sems.at[cluster],
        )
        for cluster, place in enumerate(places)
    ]
    for copy in copies:
        copy.start()
    for copy in copies:
        copy.wait()


def project_kernel(
    head_size, points_ref, gain_ref, wqk_ref, wv_ref, qt_ref, k_ref, vt_ref, pool_ref, norms_ref
):
    rows, columns = points_ref.shape
    normed = rms_norm(points_ref[...], gain_ref[...])
    paired = dot32(normed, wqk_ref[...]).astype(bf16)
    values = dot32(normed, wv_ref[...]).astype(bf16)
    query, keys = paired[:, :columns], paired[:, columns:]
    k_ref[...] = keys
    pooled = rows // POOL
    row = lax.broadcasted_iota(jnp.int32, (pooled, rows), 0)
    column = lax.broadcasted_iota(jnp.int32, (pooled, rows), 1)
    averaging = jnp.where(column // POOL == row, 1.0 / math.sqrt(POOL), 0.0).astype(bf16)
    pool_ref[:pooled] = dot32(averaging, keys).astype(bf16)
    pool_ref[pooled:] = dot32(averaging, values).astype(bf16)
    qt_ref[...] = query.T
    for head, extended in enumerate(extended_values(values, head_size)):
        vt_ref[head] = extended
    norms_ref[0:1] = head_norms(query, head_size)
    norms_ref[1:2] = head_norms(keys, head_size)


def near_part_kernel(group, head_size, qt_ref, k_ref, vt_ref, o_ref):
    per_tile = TILE // head_size
    kept = o_ref.shape[1]
    tile = slice(group * TILE, (group + 1) * TILE)

    def job(inner):
        head = group * per_tile + inner

        def scores():
            return dot32(k_ref[:, tile], masked_query(qt_ref[tile, :], head, head_size))

        def finish(values):
            mixed = dot32(vt_ref[head], plain_weights(values, head_size))
            o_ref[inner] = mixed[:kept]

        return scores, finish

    run_jobs([job(inner) for inner in range(per_tile)])


def far_fast(head_size, qt_ref, k_ref, vt_ref, kr_ref, vr_ref, y_ref):
    half = k_ref.shape[0] // 2
    per_tile = TILE // head_size
    jobs = []
    sums = {}

    def job(side, head, own):
        tile = slice(head // per_tile * TILE, (head // per_tile + 1) * TILE)
        queries = slice(side * half, (side + 1) * half)
        rows = queries if own else slice((1 - side) * half, (2 - side) * half)
        key_ref, value_ref = (k_ref, vt_ref) if own else (kr_ref, vr_ref)

        def scores():
            query = masked_query(qt_ref[tile, queries], head, head_size)
            return dot32(key_ref[rows, tile], query)

        def finish(values):
            mixed = dot32(value_ref[head, :, rows], plain_weights(values, head_size))
            if own:
                sums[side, head] = mixed
                return
            mixed = mixed + sums.pop((side, head))
            y_ref[head * head_size : (head + 1) * head_size, queries] = (
                mixed[:head_size] / mixed[head_size : head_size + 1]
            ).astype(bf16)

        return scores, finish

    for side in range(2):
        for head in range(HEADS):
            for own in (True, False):
                jobs.append(job(side, head, own))
    run_jobs(jobs)


def far_kernel(
    lanes, clusters, head_size, dest_ref, next_ref, prior_ref, across_ref, qt_ref, k_ref, vt_ref,
    norms_ref, gain_ref, wqk_ref, wv_ref, out_ref, x_ref, kr_ref, vr_ref, y_ref, slots, counts,
    sems,
):
    rows, columns = x_ref.shape
    half = rows // 2
    _, across = packed_places(dest_ref, clusters, lanes, slots, counts)

    def whole():
        return pltpu.make_async_copy(across_ref, x_ref, sems.at[0])

    def first():
        return pltpu.make_async_copy(next_ref, x_ref.at[pl.ds(0, half)], sems.at[0])

    def second():
        return pltpu.make_async_copy(prior_ref, x_ref.at[pl.ds(half, half)], sems.at[1])

    @pl.when(across)
    def _():
        whole().start()
        whole().wait()

    @pl.when(jnp.logical_not(across))
    def _():
        first().start()
        second().start()
        first().wait()
        second().wait()

    normed = rms_norm(x_ref[...], gain_ref[...])
    keys = dot32(normed, wqk_ref[:, columns:]).astype(bf16)
    values = dot32(normed, wv_ref[...]).astype(bf16)
    kr_ref[...] = keys
    for head, extended in enumerate(extended_values(values, head_size)):
        vr_ref[head] = extended
    key_norms = jnp.maximum(norms_ref[1:2], head_norms(keys, head_size))
    safe = exponents_safe(norms_ref[0:1], key_norms, head_size)

    @pl.when(safe)
    def _():
        far_fast(head_size, qt_ref, k_ref, vt_ref, kr_ref, vr_ref, y_ref)

    @pl.when(jnp.logical_not(safe))
    def _():
        for side in range(2):
            mine = slice(side * half, (side + 1) * half)
            other = slice((1 - side) * half, (2 - side) * half)
            shifted_attention(
                qt_ref,
                side * half,
                half,
                [
                    lambda tile, head, mine=mine: (k_ref[mine, tile], vt_ref[head, :, mine]),
                    lambda tile, head, other=other: (kr_ref[other, tile], vr_ref[head, :, other]),
                ],
                head_size,
                y_ref,
            )

    out_ref[...] = y_ref[...].T


def finish_kernel(
    lanes, clusters, head_size, groups, dest_ref, points_ref, far_ref, qt_ref, k_ref, vt_ref,
    norms_ref, pool_ref, *rest
):
    partial = rest[:groups]
    (wo_ref, gain_ref, up_ref, down_ref, out_ref, kp_ref, vp_ref, y_ref, done_ref, slots, counts,
     sems) = rest[groups:]
    rows, columns = points_ref.shape
    per_tile = TILE // head_size
    kept = partial[0].shape[1]
    regions, pooled = pool_ref.shape[0], pool_ref.shape[1] // 2
    for region in range(regions):
        kp_ref[region * pooled : (region + 1) * pooled] = pool_ref[region, :pooled]
    gathered = jnp.concatenate([pool_ref[r, pooled:] for r in range(regions)], axis=0)
    for head, extended in enumerate(extended_values(gathered, head_size)):
        vp_ref[head] = extended
    key_norms = jnp.maximum(norms_ref[1:2], head_norms(kp_ref[...], head_size))
    safe = exponents_safe(norms_ref[0:1], key_norms, head_size)

    def job(head):
        tile = slice(head // per_tile * TILE, (head // per_tile + 1) * TILE)

        def scores():
            return dot32(kp_ref[:, tile], masked_query(qt_ref[tile, :], head, head_size))

        def finish(values):
            mixed = dot32(vp_ref[head], plain_weights(values, head_size))[:kept]
            mixed = mixed + partial[head // per_tile][head % per_tile]
            y_ref[head * head_size : (head + 1) * head_size, :] = (
                mixed[:head_size] / mixed[head_size : head_size + 1]
            ).astype(bf16)

        return scores, finish

    @pl.when(safe)
    def _():
        run_jobs([job(head) for head in range(HEADS)])

    @pl.when(jnp.logical_not(safe))
    def _():
        shifted_attention(
            qt_ref,
            0,
            rows,
            [
                lambda tile, head: (k_ref[:, tile], vt_ref[head]),
                lambda tile, head: (kp_ref[:, tile], vp_ref[head]),
            ],
            head_size,
            y_ref,
        )

    step = min(rows, 512)
    for start in range(0, rows, step):
        block = slice(start, start + step)
        after = (
            points_ref[block].astype(f32)
            + dot32(y_ref[:, block].T, wo_ref[...])
            + dot32(far_ref[block], wo_ref[...])
        ).astype(bf16)
        normed = rms_norm(after, gain_ref[...])
        hidden = jax.nn.gelu(dot32(normed, up_ref[...]), approximate=True).astype(bf16)
        done_ref[block] = (after.astype(f32) + dot32(hidden, down_ref[...])).astype(bf16)
    places, _ = packed_places(dest_ref, clusters, lanes, slots, counts)
    copies = [
        pltpu.make_async_copy(
            done_ref.at[pl.ds(place, CLUSTER)],
            out_ref.at[pl.ds(cluster * CLUSTER, CLUSTER)],
            sems.at[cluster],
        )
        for cluster, place in enumerate(places)
    ]
    for copy in copies:
        copy.start()
    for copy in copies:
        copy.wait()


def owner_far_kernel(head_size, x_ref, gain_ref, wqk_ref, wv_ref, out_ref, qt, k, vt, y):
    rows, columns = x_ref.shape
    normed = rms_norm(x_ref[...], gain_ref[...])
    paired = dot32(normed, wqk_ref[...]).astype(bf16)
    values = dot32(normed, wv_ref[...]).astype(bf16)
    qt[...] = paired[:, :columns].T
    k[...] = paired[:, columns:]
    for head, extended in enumerate(extended_values(values, head_size)):
        vt[head] = extended
    shifted_attention(
        qt, 0, rows, [lambda tile, head: (k[:, tile], vt[head])], head_size, y
    )
    out_ref[...] = y[...].T


def per_device(
    points, gain_attn, w_query_key, w_value, w_out, gain_mlp, w_up, w_down, cluster_dest
):
    columns = points.shape[-1]
    flat = points.reshape(-1, columns)
    rows = flat.shape[0]
    lanes, regions = lax.axis_size("ball"), lax.axis_size("region")
    clusters = rows // CLUSTER
    share = 2 * clusters // lanes * CLUSTER
    owners = rows // share
    pooled = rows // POOL
    head_size = columns // HEADS
    tall = head_size + 16
    kept = head_size + 8
    dest = cluster_dest.reshape(clusters)
    gain_first = gain_attn.reshape(1, columns)
    gain_second = gain_mlp.reshape(1, columns)
    groups = columns // TILE
    wide = jax.ShapeDtypeStruct((rows, columns), bf16)
    turned = jax.ShapeDtypeStruct((columns, rows), bf16)
    extended = jax.ShapeDtypeStruct((HEADS, tall, rows), bf16)
    scalars = [pltpu.SMEM((lanes,), jnp.int32)] * 2

    def attention_cost(queries, keys, heads):
        return cost(3 * heads * queries * keys * 256, 4 * rows * columns, heads * queries * keys)

    def shift(data, offset):
        return lax.ppermute(data, "ball", [(i, (i + offset) % lanes) for i in range(lanes)])

    packed = pl.pallas_call(
        functools.partial(pack_kernel, lanes, clusters),
        out_shape=wide,
        in_specs=[in_smem(), anywhere()],
        out_specs=anywhere(),
        scratch_shapes=scalars + [pltpu.SemaphoreType.DMA((clusters,))],
        cost_estimate=cost(0, 4 * rows * columns),
        compiler_params=params(),
        name="pack",
    )(dest, flat)

    pair_path = owners == 2 and lanes == 4
    if pair_path:
        from_next = shift(packed[:share], lanes - 1)
        from_prior = shift(packed[share:], 1)
        from_across = shift(packed, 2)

    query, keys, values, pool, norms = pl.pallas_call(
        functools.partial(project_kernel, head_size),
        out_shape=[
            turned,
            wide,
            extended,
            jax.ShapeDtypeStruct((2 * pooled, columns), bf16),
            jax.ShapeDtypeStruct((8, TILE), f32),
        ],
        in_specs=[in_vmem()] * 4,
        out_specs=[in_vmem()] * 5,
        cost_estimate=cost(6 * rows * columns * columns, 10 * rows * columns),
        compiler_params=params(),
        name="project",
    )(packed, gain_first, w_query_key, w_value)

    gathered = pool.reshape(1, 2 * pooled, columns)
    step = regions // 2
    while step:
        other = lax.ppermute(gathered, "region", [(i, i ^ step) for i in range(regions)])
        gathered = jnp.concatenate([gathered, other], axis=0)
        step //= 2

    partial = [
        pl.pallas_call(
            functools.partial(near_part_kernel, group, head_size),
            out_shape=jax.ShapeDtypeStruct((HEADS // groups, kept, rows), f32),
            in_specs=[in_vmem()] * 3,
            out_specs=in_vmem(),
            cost_estimate=attention_cost(rows, rows, HEADS // groups),
            compiler_params=params(),
            name="near_part",
        )(query, keys, values)
        for group in range(groups)
    ]

    if pair_path:
        far = pl.pallas_call(
            functools.partial(far_kernel, lanes, clusters, head_size),
            out_shape=wide,
            in_specs=[in_smem()] + [anywhere()] * 3 + [in_vmem()] * 7,
            out_specs=in_vmem(),
            scratch_shapes=[
                pltpu.VMEM((rows, columns), bf16),
                pltpu.VMEM((rows, columns), bf16),
                pltpu.VMEM((HEADS, tall, rows), bf16),
                pltpu.VMEM((columns, rows), bf16),
            ]
            + scalars
            + [pltpu.SemaphoreType.DMA((2,))],
            cost_estimate=attention_cost(rows, rows, HEADS),
            compiler_params=params(),
            name="far",
        )(
            dest, from_next, from_prior, from_across, query, keys, values, norms, gain_first,
            w_query_key, w_value,
        )
    else:
        targets = dest // clusters
        members = lax.rem(targets - lax.axis_index("ball") + lanes, lanes)
        present = jnp.zeros((lanes,), jnp.int32).at[members].set(1)
        slot = jnp.cumsum(present) - present
        blocks = packed.reshape(owners, share, columns)
        empty = jnp.zeros((owners, share, columns), bf16)
        arrived, back = empty, empty

        def picked(source, offset):
            return lax.dynamic_index_in_dim(source, jnp.minimum(slot[offset], owners - 1), 0, False)

        def put(target, offset, block):
            index = jnp.minimum(slot[offset], owners - 1)
            placed = lax.dynamic_update_index_in_dim(target, block, index, 0)
            return jnp.where(present[offset] == 1, placed, target)

        for offset in range(lanes):
            block = picked(blocks, offset)
            arrived = put(arrived, offset, shift(block, offset) if offset else block)
        far_rotated = pl.pallas_call(
            functools.partial(owner_far_kernel, head_size),
            out_shape=wide,
            in_specs=[in_vmem()] * 4,
            out_specs=in_vmem(),
            scratch_shapes=[
                pltpu.VMEM((columns, rows), bf16),
                pltpu.VMEM((rows, columns), bf16),
                pltpu.VMEM((HEADS, tall, rows), bf16),
                pltpu.VMEM((columns, rows), bf16),
            ],
            cost_estimate=attention_cost(rows, rows, HEADS),
            compiler_params=params(),
            name="owner_far",
        )(arrived.reshape(rows, columns), gain_first, w_query_key, w_value)
        leaving = far_rotated.reshape(owners, share, columns)
        for offset in range(lanes):
            block = picked(leaving, offset)
            back = put(back, offset, shift(block, lanes - offset) if offset else block)
        far = back.reshape(rows, columns)

    block_out = pl.pallas_call(
        functools.partial(finish_kernel, lanes, clusters, head_size, groups),
        out_shape=wide,
        in_specs=[in_smem()] + [in_vmem()] * (7 + groups + 4),
        out_specs=anywhere(),
        scratch_shapes=[
            pltpu.VMEM((regions * pooled, columns), bf16),
            pltpu.VMEM((HEADS, tall, regions * pooled), bf16),
            pltpu.VMEM((columns, rows), bf16),
            pltpu.VMEM((rows, columns), bf16),
        ]
        + scalars
        + [pltpu.SemaphoreType.DMA((clusters,))],
        cost_estimate=cost(20 * rows * columns * columns, 8 * rows * columns),
        compiler_params=params(),
        name="finish",
    )(
        dest, packed, far, query, keys, values, norms, gathered, *partial, w_out, gain_second,
        w_up, w_down,
    )
    return block_out.reshape(points.shape)


def solution(mesh):
    placed = (
        P("ball", "region", None, None),
        P(),
        P(),
        P(),
        P(),
        P(),
        P(),
        P(),
        P("ball", "region", None),
    )
    return jax.shard_map(
        per_device,
        mesh=mesh,
        in_specs=placed,
        out_specs=P("ball", "region", None, None),
        check_vma=False,
    )
```

time: 156 us -> 84.1 us (0.54); the launches traced: 153 us -> 83.9 us
  matrix products: 73.6 us -> 0 us
  Pallas kernels: 0 us -> 69.5 us
  blocking collectives: 28.6 us -> 0 us
  other arithmetic: 18.7 us -> 0.1 us
  local copies, waits for them, and re-layouts: 18.2 us -> 2.4 us
  starting transfers between devices: 13.6 us -> 10.4 us
    dot_general x59 -> x0, matrix products: 73.6 us -> none  [the longest x24 31.6 us: one_head(): jnp.einsum('nm,dm->dn', weights, value_head, preferred_element_type=jnp.f...]
    pallas_call x0 -> x6, Pallas kernels: none -> 69.5 us  [the longest x1 34.2 us: per_device(): pl.pallas_call(functools.partial(finish_kernel, lanes, clusters, head_siz...]
    all_gather x2 -> x0, blocking collectives: 28.6 us -> none  [the longest x1 14.4 us: per_device(): lax.all_gather(pooled(key_cols), 'region', axis=1, tiled=True)]
    reduce_sum x27 -> x0, other arithmetic: 15.2 us -> none  [the longest x16 11.7 us: one_head(): total = exponents[0].sum(axis=1, keepdims=True)]
    all_to_all x3 -> x0, starting transfers between devices: 13.6 us -> none  [the longest x1 5.17 us: per_device(): lax.all_to_all(sent_ids, 'ball', split_axis=0, concat_axis=0, tiled=True)]
    ppermute x0 -> x6, starting transfers between devices: none -> 10.4 us  [the longest x3 6.01 us: shift(): lax.ppermute(data, 'ball', [(i, (i + offset) % lanes) for i in range(lane...]
    reshape x7 -> x0, local copies, waits for them, and re-layouts: 7 us -> none  [the longest x1 2.35 us: per_device(): packed.astype(jnp.bfloat16).reshape(lanes, capacity * CLUSTER, inner)]
    convert_element_type x4 -> x0, local copies, waits for them, and re-layouts: 3.94 us -> none  [the longest x2 2.61 us: per_device(): flat.astype(jnp.float32) + near_out]
  transfers between devices with their start and end apart: 3 -> 6, of which waited for: 0 -> 2; matrix products, arithmetic and copies ran while one was open for 50% -> 0% of each run, Pallas kernels for 0% -> 10%
where the time goes in v2:
time: 84.1 us; the launch traced here: 83.9 us
  Pallas kernels  69.5 us (83%)
  starting transfers between devices  10.4 us (12%)
  local copies, waits for them, and re-layouts  2.4 us (3%)
  waiting for transfers between devices  1.25 us (1%)
    pallas_call x1, Pallas kernels, per_device(): pl.pallas_call(functools.partial(finish_kernel, lanes, clusters, head_siz...  34.2 us
    pallas_call x1, Pallas kernels, per_device(): pl.pallas_call(functools.partial(far_kernel, lanes, clusters, head_size),...  24.8 us
    pallas_call x2, Pallas kernels, per_device(): pl.pallas_call(functools.partial(near_part_kernel, group, head_size), out...  7.48 us
    ppermute x3, starting transfers between devices, shift(): lax.ppermute(data, 'ball', [(i, (i + offset) % lanes) for i in range(lane...  6.01 us
    ppermute x3, starting transfers between devices, per_device(): lax.ppermute(gathered, 'region', [(i, i ^ step) for i in range(regions)])  4.38 us
    unnamed x18, local copies, waits for them, and re-layouts  2.36 us
    pallas_call x1, Pallas kernels, per_device(): pl.pallas_call(functools.partial(pack_kernel, lanes, clusters), out_shape...  1.76 us
  transfers between devices with their start and end apart: 6, of which 2 were waited for; matrix products, arithmetic and copies ran while one was open for 0% of the time, Pallas kernels for 10%

profile of v2, /device:TPU:0, one launch (start us, length us, event | category | flops | bytes accessed | tf_op | source)
XLA Modules:
  0.0 83.9 jit_solution(3162506903642029252)
XLA Ops:
  0.0 0.7 copy-done.4
  0.7 1.0 %copy-done.2 = bf16[1,1,1024,256]{3,2,1,0:T(8,128)(2,1)S(1)} copy-done((bf16[1,1,1024,256]{3,2,1,0:T(8,128)(2,1)S(1)}, bf16[1,1,1024,256]{3,2,1,0:T(8,128)(2,1)}, u32[]{:S(2)}) %copy-start.2) | copy-done | bytes 524312
  1.7 1.8 %pack.1.points_ref = bf16[1024,256]{1,0:T(8,128)(2,1)S(1)} custom-call(s32[16]{0:T(128)S(1)} %bitcast.11, bf16[1024,256]{1,0:T(8,128)(2,1)S(1)} %bitcast.10), custom_call_target="tpu_custom_call" | custom-call | bytes 1048576 | tf_op jit(solution)/shard_map/pack/pallas_call | solution.py:440
  3.5 0.0 copy-start.8
  3.5 3.0 %collective-permute-start.2 = (bf16[1024,256]{1,0:T(8,128)(2,1)S(1)}, bf16[1024,256]{1,0:T(8,128)(2,1)S(1)}, u32[]{:S(2)}, u32[]{:S(2)}) collective-permute-start(bf16[1024,256]{1,0:T(8,128)(2,1)S(1)} %pack.1.points_ref), channel_id=1, source_target_pairs={{0,16},{8,24},{16,0},{24,8},{1,17},{9,25},{17,1},{25,9},{2,18},{10... | collective-permute-start | bytes 1572872 | tf_op jit(solution)/shard_map/ppermute | solution.py:438
  6.5 1.3 %project.1 = (bf16[256,1024]{1,0:T(8,128)(2,1)S(1)}, bf16[1024,256]{1,0:T(8,128)(2,1)S(1)}, bf16[8,48,1024]{2,1,0:T(8,128)(2,1)S(1)}, bf16[128,256]{1,0:T(8,128)(2,1)S(1)}, f32[8,128]{1,0:T(8,128)S(1)}) custom-call(bf16[1024,256]{1,0:T(8,128)(2,1)S(1)} %pack.1.points_ref, f32[1,256]{1,0:T(1,128)S(1)} %bitcast.15, bf16[256,512]{1,0:T(8,128)(2,1)S(1)} %copy-done.6, ...), custom_call_target="tpu_custom_call" | custom-call | flops 402653184 | bytes 2621440 | tf_op jit(solution)/shard_map/project/pallas_call | solution.py:457
  7.8 2.7 %collective-permute-start.3 = (bf16[1,128,256]{2,1,0:T(8,128)(2,1)S(1)}, bf16[1,128,256]{2,1,0:T(8,128)(2,1)S(1)}, u32[]{:S(2)}, u32[]{:S(2)}) collective-permute-start(bf16[1,128,256]{2,1,0:T(8,128)(2,1)S(1)} %bitcast.6), channel_id=1, source_target_pairs={{0,4},{1,5},{2,6},{3,7},{4,0},{5,1},{6,2},{7,3},{8,12},{9,13},{10,... | collective-permute-start | bytes 196616 | tf_op jit(solution)/shard_map/ppermute | solution.py:476
  10.5 1.5 %collective-permute-start.1 = (bf16[512,256]{1,0:T(8,128)(2,1)S(1)}, bf16[512,256]{1,0:T(8,128)(2,1)S(1)}, u32[]{:S(2)}, u32[]{:S(2)}) collective-permute-start(bf16[512,256]{1,0:T(8,128)(2,1)S(1)} %get-tuple-element.15), channel_id=1, source_target_pairs={{0,8},{8,16},{16,24},{24,0},{1,9},{9,17},{17,25},{25,1},{2,10},{10... | collective-permute-start | bytes 786440 | tf_op jit(solution)/shard_map/ppermute | solution.py:438
  12.0 1.4 %collective-permute-start = (bf16[512,256]{1,0:T(8,128)(2,1)S(1)}, bf16[512,256]{1,0:T(8,128)(2,1)S(1)}, u32[]{:S(2)}, u32[]{:S(2)}) collective-permute-start(bf16[512,256]{1,0:T(8,128)(2,1)S(1)} %get-tuple-element.16), channel_id=1, source_target_pairs={{0,24},{8,0},{16,8},{24,16},{1,25},{9,1},{17,9},{25,17},{2,26},{10... | collective-permute-start | bytes 786440 | tf_op jit(solution)/shard_map/ppermute | solution.py:438
  13.5 0.0 collective-permute-done.3
  13.5 1.6 %collective-permute-start.4 = (bf16[2,128,256]{2,1,0:T(8,128)(2,1)S(1)}, bf16[2,128,256]{2,1,0:T(8,128)(2,1)S(1)}, u32[]{:S(2)}, u32[]{:S(2)}) collective-permute-start(bf16[2,128,256]{2,1,0:T(8,128)(2,1)S(1)} %pad_maximum_fusion.2), channel_id=1, source_target_pairs={{0,2},{1,3},{2,0},{3,1},{4,6},{5,7},{6,4},{7,5},{8,10},{9,11},{10,... | collective-permute-start | bytes 393224 | tf_op jit(solution)/shard_map/ppermute | solution.py:476
  15.1 3.7 %near_part.3.rest_1_ = f32[4,40,1024]{2,1,0:T(8,128)S(1)} custom-call(bf16[256,1024]{1,0:T(8,128)(2,1)S(1)} %get-tuple-element.10.qt_ref, bf16[1024,256]{1,0:T(8,128)(2,1)S(1)} %get-tuple-element.11.k_ref, bf16[8,48,1024]{2,1,0:T(8,128)(2,1)S(1)} %get-tuple-element.12.vt_ref), custom_call_target="tpu_custom_call" | custom-call | flops 3221225472 | bytes 1048576 | tf_op jit(solution)/shard_map/near_part/pallas_call | solution.py:481
  18.9 0.0 collective-permute-done.4
  18.9 0.1 collective-permute-start.5
  19.0 3.7 %near_part.2.rest_0_ = f32[4,40,1024]{2,1,0:T(8,128)S(1)} custom-call(bf16[256,1024]{1,0:T(8,128)(2,1)S(1)} %get-tuple-element.10.qt_ref, bf16[1024,256]{1,0:T(8,128)(2,1)S(1)} %get-tuple-element.11.k_ref, bf16[8,48,1024]{2,1,0:T(8,128)(2,1)S(1)} %get-tuple-element.12.vt_ref), custom_call_target="tpu_custom_call" | custom-call | flops 3221225472 | bytes 1048576 | tf_op jit(solution)/shard_map/near_part/pallas_call | solution.py:481
  22.7 0.0 collective-permute-done.5
  22.8 0.1 pad_maximum_fusion.pool_ref
  22.8 0.0 collective-permute-done.1.prior_ref
  22.8 1.2 %collective-permute-done.next_ref = bf16[512,256]{1,0:T(8,128)(2,1)S(1)} collective-permute-done((bf16[512,256]{1,0:T(8,128)(2,1)S(1)}, bf16[512,256]{1,0:T(8,128)(2,1)S(1)}, u32[]{:S(2)}, u32[]{:S(2)}) %collective-permute-start) | collective-permute-done | bytes 262176 | tf_op jit(solution)/shard_map/ppermute | solution.py:438
  24.0 0.1 collective-permute-done.2.across_ref
  24.1 24.8 %far.1.far_ref = bf16[1024,256]{1,0:T(8,128)(2,1)S(1)} custom-call(s32[16]{0:T(128)S(1)} %bitcast.12, bf16[512,256]{1,0:T(8,128)(2,1)S(1)} %collective-permute-done.next_ref, bf16[512,256]{1,0:T(8,128)(2,1)S(1)} %collective-permute-done.1.prior_ref, bf16[1024,256]{1,0:T(8,128)(2,1)S(1)} %collective-permute-done.2.across_ref, ...), custom_call_target="tpu_custom_call" | custom-call | flops 6442450944 | bytes 1048576 | tf_op jit(solution)/shard_map/far/pallas_call | solution.py:494
  48.9 0.0 copy-start.5
  48.9 0.6 copy-done.5
  49.6 34.2 %finish.1 = bf16[1024,256]{1,0:T(8,128)(2,1)} custom-call(s32[16]{0:T(128)S(1)} %bitcast.13, bf16[1024,256]{1,0:T(8,128)(2,1)S(1)} %pack.1.points_ref, bf16[1024,256]{1,0:T(8,128)(2,1)S(1)} %far.1.far_ref, bf16[256,1024]{1,0:T(8,128)(2,1)S(1)} %get-tuple-element.10.qt_ref, bf16[1024,256]{1,0:T(8,128)(2,1)S(1)} %get-tuple-element.11.k_ref, ...), custom_call_target="tpu_custom_call" | custom-call | flops 1342177280 | bytes 2097152 | tf_op jit(solution)/shard_map/finish/pallas_call | solution.py:555
  (16 shorter events, 0.1 us)
Async XLA Ops:
  0.0 0.7 copy-start.4
  0.7 1.0 %copy-start.2 = (bf16[1,1,1024,256]{3,2,1,0:T(8,128)(2,1)S(1)}, bf16[1,1,1024,256]{3,2,1,0:T(8,128)(2,1)}, u32[]{:S(2)}) copy-start(bf16[1,1,1024,256]{3,2,1,0:T(8,128)(2,1)} %param.9) | copy-start | bytes 1572868
  1.7 4.8 %copy-start.6 = (bf16[256,512]{1,0:T(8,128)(2,1)S(1)}, bf16[256,512]{1,0:T(8,128)(2,1)}, u32[]{:S(2)}) copy-start(bf16[256,512]{1,0:T(8,128)(2,1)} %wqk_ref.3) | copy-start | bytes 786436
  1.7 4.8 %copy-start.7 = (bf16[256,256]{1,0:T(8,128)(2,1)S(1)}, bf16[256,256]{1,0:T(8,128)(2,1)}, u32[]{:S(2)}) copy-start(bf16[256,256]{1,0:T(8,128)(2,1)} %wv_ref.3) | copy-start | bytes 393220
  3.5 3.1 %copy-start.8 = (f32[256]{0:T(256)S(1)}, f32[256]{0:T(256)}, u32[]{:S(2)}) copy-start(f32[256]{0:T(256)} %param.10) | copy-start | bytes 3076
  3.5 20.6 %collective-permute-start.2 = (bf16[1024,256]{1,0:T(8,128)(2,1)S(1)}, bf16[1024,256]{1,0:T(8,128)(2,1)S(1)}, u32[]{:S(2)}, u32[]{:S(2)}) collective-permute-start(bf16[1024,256]{1,0:T(8,128)(2,1)S(1)} %pack.1.points_ref), channel_id=1, source_target_pairs={{0,16},{8,24},{16,0},{24,8},{1,17},{9,25},{17,1},{25,9},{2,18},{10... | collective-permute-start | bytes 1572872 | tf_op jit(solution)/shard_map/ppermute | solution.py:438
  7.8 5.7 %collective-permute-start.3 = (bf16[1,128,256]{2,1,0:T(8,128)(2,1)S(1)}, bf16[1,128,256]{2,1,0:T(8,128)(2,1)S(1)}, u32[]{:S(2)}, u32[]{:S(2)}) collective-permute-start(bf16[1,128,256]{2,1,0:T(8,128)(2,1)S(1)} %bitcast.6), channel_id=1, source_target_pairs={{0,4},{1,5},{2,6},{3,7},{4,0},{5,1},{6,2},{7,3},{8,12},{9,13},{10,... | collective-permute-start | bytes 196616 | tf_op jit(solution)/shard_map/ppermute | solution.py:476
  10.5 12.3 %collective-permute-start.1 = (bf16[512,256]{1,0:T(8,128)(2,1)S(1)}, bf16[512,256]{1,0:T(8,128)(2,1)S(1)}, u32[]{:S(2)}, u32[]{:S(2)}) collective-permute-start(bf16[512,256]{1,0:T(8,128)(2,1)S(1)} %get-tuple-element.15), channel_id=1, source_target_pairs={{0,8},{8,16},{16,24},{24,0},{1,9},{9,17},{17,25},{25,1},{2,10},{10... | collective-permute-start | bytes 786440 | tf_op jit(solution)/shard_map/ppermute | solution.py:438
  12.0 12.0 %collective-permute-start = (bf16[512,256]{1,0:T(8,128)(2,1)S(1)}, bf16[512,256]{1,0:T(8,128)(2,1)S(1)}, u32[]{:S(2)}, u32[]{:S(2)}) collective-permute-start(bf16[512,256]{1,0:T(8,128)(2,1)S(1)} %get-tuple-element.16), channel_id=1, source_target_pairs={{0,24},{8,0},{16,8},{24,16},{1,25},{9,1},{17,9},{25,17},{2,26},{10... | collective-permute-start | bytes 786440 | tf_op jit(solution)/shard_map/ppermute | solution.py:438
  13.5 5.4 %collective-permute-start.4 = (bf16[2,128,256]{2,1,0:T(8,128)(2,1)S(1)}, bf16[2,128,256]{2,1,0:T(8,128)(2,1)S(1)}, u32[]{:S(2)}, u32[]{:S(2)}) collective-permute-start(bf16[2,128,256]{2,1,0:T(8,128)(2,1)S(1)} %pad_maximum_fusion.2), channel_id=1, source_target_pairs={{0,2},{1,3},{2,0},{3,1},{4,6},{5,7},{6,4},{7,5},{8,10},{9,11},{10,... | collective-permute-start | bytes 393224 | tf_op jit(solution)/shard_map/ppermute | solution.py:476
  18.9 3.8 %collective-permute-start.5 = (bf16[4,128,256]{2,1,0:T(8,128)(2,1)S(1)}, bf16[4,128,256]{2,1,0:T(8,128)(2,1)S(1)}, u32[]{:S(2)}, u32[]{:S(2)}) collective-permute-start(bf16[4,128,256]{2,1,0:T(8,128)(2,1)S(1)} %pad_maximum_fusion.1), channel_id=1, source_target_pairs={{0,1},{1,0},{2,3},{3,2},{4,5},{5,4},{6,7},{7,6},{8,9},{9,8},{10,11... | collective-permute-start | bytes 786440 | tf_op jit(solution)/shard_map/ppermute | solution.py:476
  24.1 24.9 %copy-start = (bf16[256,1024]{1,0:T(8,128)(2,1)S(1)}, bf16[256,1024]{1,0:T(8,128)(2,1)}, u32[]{:S(2)}) copy-start(bf16[256,1024]{1,0:T(8,128)(2,1)} %rest_4_.1) | copy-start | bytes 1572868
  24.1 24.9 %copy-start.1 = (bf16[1024,256]{1,0:T(8,128)(2,1)S(1)}, bf16[1024,256]{1,0:T(8,128)(2,1)}, u32[]{:S(2)}) copy-start(bf16[1024,256]{1,0:T(8,128)(2,1)} %rest_5_.1) | copy-start | bytes 1572868
  24.1 24.9 %copy-start.3 = (bf16[256,256]{1,0:T(8,128)(2,1)S(1)}, bf16[256,256]{1,0:T(8,128)(2,1)}, u32[]{:S(2)}) copy-start(bf16[256,256]{1,0:T(8,128)(2,1)} %rest_2_.1) | copy-start | bytes 393220
  48.9 0.7 copy-start.5

commit v3 on v2

--- a/solution.py
+++ b/solution.py
@@ -13,6 +13,10 @@
 POOL = 16
 TILE = 128
 SLOW_BLOCK = 256
+QUERY_BLOCK = 512
+KEY_BLOCK = 256
+AHEAD = 3
+ROW_BLOCK = 256
 SAFE_EXPONENT = 104.0
 VMEM_LIMIT = 48 * 1024 * 1024
 
@@ -26,6 +30,10 @@
 
 def in_smem():
     return pl.BlockSpec(memory_space=pltpu.SMEM)
+
+
+def in_hbm():
+    return pl.BlockSpec(memory_space=pltpu.HBM)
 
 
 def anywhere():
@@ -106,16 +114,58 @@
     return jnp.where(row == head % (TILE // head_size), query, bf16(0))
 
 
-def run_jobs(jobs, ahead=1):
-    waiting = [scores() for scores, _ in jobs[:ahead]]
-    for index, (_, finish) in enumerate(jobs):
+def run_jobs(jobs, ahead=AHEAD):
+    waiting = [first() for first, _ in jobs[:ahead]]
+    for index, (_, second) in enumerate(jobs):
         if index + ahead < len(jobs):
             waiting.append(jobs[index + ahead][0]())
-        finish(waiting.pop(0))
+        second(waiting.pop(0))
 
 
 def plain_weights(scores, head_size):
     return jnp.exp2(scores * factor_of(head_size)).astype(bf16)
+
+
+def plain_attention(qt_ref, columns_of_query, heads, parts_of, head_size, store):
+    per_tile = TILE // head_size
+    kept = head_size + 8
+    sums = {}
+    jobs = []
+
+    def job(start, head, key_ref, value_ref, first, last):
+        tile = slice(head // per_tile * TILE, (head // per_tile + 1) * TILE)
+        queries = slice(start, start + QUERY_BLOCK)
+        rows = slice(first, first + KEY_BLOCK)
+
+        def scores():
+            query = masked_query(qt_ref[tile, queries], head, head_size)
+            return dot32(key_ref[rows, tile], query)
+
+        def mix(values):
+            mixed = dot32(value_ref[head, :, rows], plain_weights(values, head_size))[:kept]
+            if (start, head) in sums:
+                mixed = mixed + sums.pop((start, head))
+            if last:
+                store(head, queries, mixed)
+            else:
+                sums[start, head] = mixed
+
+        return scores, mix
+
+    for start in columns_of_query:
+        for head in heads:
+            blocks = [
+                (keys, values, row)
+                for keys, values, first, end in parts_of(start)
+                for row in range(first, end, KEY_BLOCK)
+            ]
+            for index, (keys, values, row) in enumerate(blocks):
+                jobs.append(job(start, head, keys, values, row, index + 1 == len(blocks)))
+    run_jobs(jobs)
+
+
+def divided(sums, head_size):
+    return (sums[:head_size] / sums[head_size : head_size + 1]).astype(bf16)
 
 
 def head_norms(rows, head_size):
@@ -159,8 +209,18 @@
     lax.fori_loop(0, HEADS * (count // SLOW_BLOCK), step, 0)
 
 
-def pack_kernel(lanes, clusters, dest_ref, points_ref, packed_ref, slots, counts, sems):
-    places, _ = packed_places(dest_ref, clusters, lanes, slots, counts)
+def gelu(value):
+    slope = math.sqrt(2.0 / math.pi)
+    inner = value * (value * value * (0.044715 * slope) + slope)
+    half = 0.5 * value
+    return half + half * jnp.tanh(inner)
+
+
+def pack_kernel(lanes, clusters, dest_hbm, points_ref, packed_ref, dest, slots, counts, sems):
+    fetch = pltpu.make_async_copy(dest_hbm, dest, sems.at[clusters])
+    fetch.start()
+    fetch.wait()
+    places, _ = packed_places(dest, clusters, lanes, slots, counts)
     copies = [
         pltpu.make_async_copy(
             points_ref.at[pl.ds(cluster * CLUSTER, CLUSTER)],
@@ -199,132 +259,26 @@
 
 def near_part_kernel(group, head_size, qt_ref, k_ref, vt_ref, o_ref):
     per_tile = TILE // head_size
-    kept = o_ref.shape[1]
-    tile = slice(group * TILE, (group + 1) * TILE)
-
-    def job(inner):
-        head = group * per_tile + inner
-
-        def scores():
-            return dot32(k_ref[:, tile], masked_query(qt_ref[tile, :], head, head_size))
-
-        def finish(values):
-            mixed = dot32(vt_ref[head], plain_weights(values, head_size))
-            o_ref[inner] = mixed[:kept]
-
-        return scores, finish
-
-    run_jobs([job(inner) for inner in range(per_tile)])
-
-
-def far_fast(head_size, qt_ref, k_ref, vt_ref, kr_ref, vr_ref, y_ref):
-    half = k_ref.shape[0] // 2
+    rows = k_ref.shape[0]
+
+    def store(head, queries, sums):
+        o_ref[head % per_tile, :, queries] = sums
+
+    plain_attention(
+        qt_ref,
+        range(0, rows, QUERY_BLOCK),
+        range(group * per_tile, (group + 1) * per_tile),
+        lambda start: [(k_ref, vt_ref, 0, rows)],
+        head_size,
+        store,
+    )
+
+
+def near_kernel(head_size, qt_ref, k_ref, vt_ref, norms_ref, pool_ref, *rest):
+    partial = rest[:-3]
+    y_ref, kp_ref, vp_ref = rest[-3:]
+    rows = k_ref.shape[0]
     per_tile = TILE // head_size
-    jobs = []
-    sums = {}
-
-    def job(side, head, own):
-        tile = slice(head // per_tile * TILE, (head // per_tile + 1) * TILE)
-        queries = slice(side * half, (side + 1) * half)
-        rows = queries if own else slice((1 - side) * half, (2 - side) * half)
-        key_ref, value_ref = (k_ref, vt_ref) if own else (kr_ref, vr_ref)
-
-        def scores():
-            query = masked_query(qt_ref[tile, queries], head, head_size)
-            return dot32(key_ref[rows, tile], query)
-
-        def finish(values):
-            mixed = dot32(value_ref[head, :, rows], plain_weights(values, head_size))
-            if own:
-                sums[side, head] = mixed
-                return
-            mixed = mixed + sums.pop((side, head))
-            y_ref[head * head_size : (head + 1) * head_size, queries] = (
-                mixed[:head_size] / mixed[head_size : head_size + 1]
-            ).astype(bf16)
-
-        return scores, finish
-
-    for side in range(2):
-        for head in range(HEADS):
-            for own in (True, False):
-                jobs.append(job(side, head, own))
-    run_jobs(jobs)
-
-
-def far_kernel(
-    lanes, clusters, head_size, dest_ref, next_ref, prior_ref, across_ref, qt_ref, k_ref, vt_ref,
-    norms_ref, gain_ref, wqk_ref, wv_ref, out_ref, x_ref, kr_ref, vr_ref, y_ref, slots, counts,
-    sems,
-):
-    rows, columns = x_ref.shape
-    half = rows // 2
-    _, across = packed_places(dest_ref, clusters, lanes, slots, counts)
-
-    def whole():
-        return pltpu.make_async_copy(across_ref, x_ref, sems.at[0])
-
-    def first():
-        return pltpu.make_async_copy(next_ref, x_ref.at[pl.ds(0, half)], sems.at[0])
-
-    def second():
-        return pltpu.make_async_copy(prior_ref, x_ref.at[pl.ds(half, half)], sems.at[1])
-
-    @pl.when(across)
-    def _():
-        whole().start()
-        whole().wait()
-
-    @pl.when(jnp.logical_not(across))
-    def _():
-        first().start()
-        second().start()
-        first().wait()
-        second().wait()
-
-    normed = rms_norm(x_ref[...], gain_ref[...])
-    keys = dot32(normed, wqk_ref[:, columns:]).astype(bf16)
-    values = dot32(normed, wv_ref[...]).astype(bf16)
-    kr_ref[...] = keys
-    for head, extended in enumerate(extended_values(values, head_size)):
-        vr_ref[head] = extended
-    key_norms = jnp.maximum(norms_ref[1:2], head_norms(keys, head_size))
-    safe = exponents_safe(norms_ref[0:1], key_norms, head_size)
-
-    @pl.when(safe)
-    def _():
-        far_fast(head_size, qt_ref, k_ref, vt_ref, kr_ref, vr_ref, y_ref)
-
-    @pl.when(jnp.logical_not(safe))
-    def _():
-        for side in range(2):
-            mine = slice(side * half, (side + 1) * half)
-            other = slice((1 - side) * half, (2 - side) * half)
-            shifted_attention(
-                qt_ref,
-                side * half,
-                half,
-                [
-                    lambda tile, head, mine=mine: (k_ref[mine, tile], vt_ref[head, :, mine]),
-                    lambda tile, head, other=other: (kr_ref[other, tile], vr_ref[head, :, other]),
-                ],
-                head_size,
-                y_ref,
-            )
-
-    out_ref[...] = y_ref[...].T
-
-
-def finish_kernel(
-    lanes, clusters, head_size, groups, dest_ref, points_ref, far_ref, qt_ref, k_ref, vt_ref,
-    norms_ref, pool_ref, *rest
-):
-    partial = rest[:groups]
-    (wo_ref, gain_ref, up_ref, down_ref, out_ref, kp_ref, vp_ref, y_ref, done_ref, slots, counts,
-     sems) = rest[groups:]
-    rows, columns = points_ref.shape
-    per_tile = TILE // head_size
-    kept = partial[0].shape[1]
     regions, pooled = pool_ref.shape[0], pool_ref.shape[1] // 2
     for region in range(regions):
         kp_ref[region * pooled : (region + 1) * pooled] = pool_ref[region, :pooled]
@@ -334,24 +288,20 @@
     key_norms = jnp.maximum(norms_ref[1:2], head_norms(kp_ref[...], head_size))
     safe = exponents_safe(norms_ref[0:1], key_norms, head_size)
 
-    def job(head):
-        tile = slice(head // per_tile * TILE, (head // per_tile + 1) * TILE)
-
-        def scores():
-            return dot32(kp_ref[:, tile], masked_query(qt_ref[tile, :], head, head_size))
-
-        def finish(values):
-            mixed = dot32(vp_ref[head], plain_weights(values, head_size))[:kept]
-            mixed = mixed + partial[head // per_tile][head % per_tile]
-            y_ref[head * head_size : (head + 1) * head_size, :] = (
-                mixed[:head_size] / mixed[head_size : head_size + 1]
-            ).astype(bf16)
-
-        return scores, finish
+    def store(head, queries, sums):
+        sums = sums + partial[head // per_tile][head % per_tile, :, queries]
+        y_ref[head * head_size : (head + 1) * head_size, queries] = divided(sums, head_size)
 
     @pl.when(safe)
     def _():
-        run_jobs([job(head) for head in range(HEADS)])
+        plain_attention(
+            qt_ref,
+            range(0, rows, QUERY_BLOCK),
+            range(HEADS),
+            lambda start: [(kp_ref, vp_ref, 0, regions * pooled)],
+            head_size,
+            store,
+        )
 
     @pl.when(jnp.logical_not(safe))
     def _():
@@ -367,30 +317,119 @@
             y_ref,
         )
 
-    step = min(rows, 512)
-    for start in range(0, rows, step):
-        block = slice(start, start + step)
-        after = (
-            points_ref[block].astype(f32)
-            + dot32(y_ref[:, block].T, wo_ref[...])
-            + dot32(far_ref[block], wo_ref[...])
-        ).astype(bf16)
-        normed = rms_norm(after, gain_ref[...])
-        hidden = jax.nn.gelu(dot32(normed, up_ref[...]), approximate=True).astype(bf16)
-        done_ref[block] = (after.astype(f32) + dot32(hidden, down_ref[...])).astype(bf16)
+
+def far_attention(
+    head_size, across, next_ref, prior_ref, across_ref, qt_ref, k_ref, vt_ref, norms_ref,
+    gain_ref, wqk_ref, wv_ref, kr_ref, vr_ref, y_ref,
+):
+    rows, columns = k_ref.shape
+    half = rows // 2
+    apart = jnp.concatenate([next_ref[...], prior_ref[...]], axis=0)
+    normed = rms_norm(jnp.where(across, across_ref[...], apart), gain_ref[...])
+    keys = dot32(normed, wqk_ref[:, columns:]).astype(bf16)
+    values = dot32(normed, wv_ref[...]).astype(bf16)
+    kr_ref[...] = keys
+    for head, extended in enumerate(extended_values(values, head_size)):
+        vr_ref[head] = extended
+    key_norms = jnp.maximum(norms_ref[1:2], head_norms(keys, head_size))
+    safe = exponents_safe(norms_ref[0:1], key_norms, head_size)
+
+    def store(head, queries, sums):
+        y_ref[head * head_size : (head + 1) * head_size, queries] = divided(sums, head_size)
+
+    def parts_of(start):
+        mine = start // half * half
+        other = half - mine
+        return [(k_ref, vt_ref, mine, mine + half), (kr_ref, vr_ref, other, other + half)]
+
+    @pl.when(safe)
+    def _():
+        plain_attention(
+            qt_ref, range(0, rows, QUERY_BLOCK), range(HEADS), parts_of, head_size, store
+        )
+
+    @pl.when(jnp.logical_not(safe))
+    def _():
+        for start in (0, half):
+            mine, other = slice(start, start + half), slice(half - start, rows - start)
+            shifted_attention(
+                qt_ref,
+                start,
+                half,
+                [
+                    lambda tile, head, mine=mine: (k_ref[mine, tile], vt_ref[head, :, mine]),
+                    lambda tile, head, other=other: (kr_ref[other, tile], vr_ref[head, :, other]),
+                ],
+                head_size,
+                y_ref,
+            )
+
+
+def output_rows(
+    places, points_ref, near_ref, far_ref, wo_ref, gain_ref, up_ref, down_ref, out_ref, done_ref,
+    origin, sems,
+):
+    rows = points_ref.shape[0]
+    for cluster, place in enumerate(places):
+        origin[place // CLUSTER] = cluster
+
+    def back(slot):
+        return pltpu.make_async_copy(
+            done_ref.at[pl.ds(slot * CLUSTER, CLUSTER)],
+            out_ref.at[pl.ds(pl.multiple_of(origin[slot] * CLUSTER, CLUSTER), CLUSTER)],
+            sems.at[slot],
+        )
+
+    def job(start):
+        block = slice(start, start + ROW_BLOCK)
+
+        def widen():
+            after = (
+                points_ref[block].astype(f32)
+                + dot32(near_ref[:, block].T, wo_ref[...])
+                + dot32(far_ref[:, block].T, wo_ref[...])
+            ).astype(bf16)
+            return after, dot32(rms_norm(after, gain_ref[...]), up_ref[...])
+
+        def narrow(widened):
+            after, hidden = widened
+            hidden = gelu(hidden).astype(bf16)
+            done_ref[block] = (after.astype(f32) + dot32(hidden, down_ref[...])).astype(bf16)
+            for slot in range(start // CLUSTER, (start + ROW_BLOCK) // CLUSTER):
+                back(slot).start()
+
+        return widen, narrow
+
+    run_jobs([job(start) for start in range(0, rows, ROW_BLOCK)], ahead=1)
+    for slot in range(rows // CLUSTER):
+        back(slot).wait()
+
+
+def far_finish_kernel(
+    lanes, clusters, head_size, dest_ref, points_ref, near_ref, next_ref, prior_ref, across_ref,
+    qt_ref, k_ref, vt_ref, norms_ref, gain_ref, wqk_ref, wv_ref, wo_ref, gain_second, up_ref,
+    down_ref, out_ref, kr_ref, vr_ref, y_ref, done_ref, slots, counts, origin, sems,
+):
+    places, across = packed_places(dest_ref, clusters, lanes, slots, counts)
+    far_attention(
+        head_size, across, next_ref, prior_ref, across_ref, qt_ref, k_ref, vt_ref, norms_ref,
+        gain_ref, wqk_ref, wv_ref, kr_ref, vr_ref, y_ref,
+    )
+    output_rows(
+        places, points_ref, near_ref, y_ref, wo_ref, gain_second, up_ref, down_ref, out_ref,
+        done_ref, origin, sems,
+    )
+
+
+def finish_kernel(
+    lanes, clusters, dest_ref, points_ref, near_ref, far_ref, wo_ref, gain_ref, up_ref, down_ref,
+    out_ref, done_ref, slots, counts, origin, sems,
+):
     places, _ = packed_places(dest_ref, clusters, lanes, slots, counts)
-    copies = [
-        pltpu.make_async_copy(
-            done_ref.at[pl.ds(place, CLUSTER)],
-            out_ref.at[pl.ds(cluster * CLUSTER, CLUSTER)],
-            sems.at[cluster],
-        )
-        for cluster, place in enumerate(places)
-    ]
-    for copy in copies:
-        copy.start()
-    for copy in copies:
-        copy.wait()
+    output_rows(
+        places, points_ref, near_ref, far_ref, wo_ref, gain_ref, up_ref, down_ref, out_ref,
+        done_ref, origin, sems,
+    )
 
 
 def owner_far_kernel(head_size, x_ref, gain_ref, wqk_ref, wv_ref, out_ref, qt, k, vt, y):
@@ -440,9 +479,11 @@
     packed = pl.pallas_call(
         functools.partial(pack_kernel, lanes, clusters),
         out_shape=wide,
-        in_specs=[in_smem(), anywhere()],
+        in_specs=[in_hbm(), in_hbm()],
         out_specs=anywhere(),
-        scratch_shapes=scalars + [pltpu.SemaphoreType.DMA((clusters,))],
+        scratch_shapes=[pltpu.SMEM((clusters,), jnp.int32)]
+        + scalars
+        + [pltpu.SemaphoreType.DMA((clusters + 1,))],
         cost_estimate=cost(0, 4 * rows * columns),
         compiler_params=params(),
         name="pack",
@@ -490,26 +531,43 @@
         for group in range(groups)
     ]
 
+    near = pl.pallas_call(
+        functools.partial(near_kernel, head_size),
+        out_shape=turned,
+        in_specs=[in_vmem()] * (5 + groups),
+        out_specs=in_vmem(),
+        scratch_shapes=[
+            pltpu.VMEM((regions * pooled, columns), bf16),
+            pltpu.VMEM((HEADS, tall, regions * pooled), bf16),
+        ],
+        cost_estimate=attention_cost(rows, regions * pooled, HEADS),
+        compiler_params=params(),
+        name="near",
+    )(query, keys, values, norms, gathered, *partial)
+
+    last_scratch = (
+        [pltpu.VMEM((rows, columns), bf16)]
+        + scalars
+        + [pltpu.SMEM((clusters,), jnp.int32), pltpu.SemaphoreType.DMA((clusters,))]
+    )
     if pair_path:
-        far = pl.pallas_call(
-            functools.partial(far_kernel, lanes, clusters, head_size),
+        block_out = pl.pallas_call(
+            functools.partial(far_finish_kernel, lanes, clusters, head_size),
             out_shape=wide,
-            in_specs=[in_smem()] + [anywhere()] * 3 + [in_vmem()] * 7,
-            out_specs=in_vmem(),
+            in_specs=[in_smem()] + [in_vmem()] * 16,
+            out_specs=anywhere(),
             scratch_shapes=[
-                pltpu.VMEM((rows, columns), bf16),
                 pltpu.VMEM((rows, columns), bf16),
                 pltpu.VMEM((HEADS, tall, rows), bf16),
                 pltpu.VMEM((columns, rows), bf16),
             ]
-            + scalars
-            + [pltpu.SemaphoreType.DMA((2,))],
+            + last_scratch,
             cost_estimate=attention_cost(rows, rows, HEADS),
             compiler_params=params(),
-            name="far",
+            name="far_finish",
         )(
-            dest, from_next, from_prior, from_across, query, keys, values, norms, gain_first,
-            w_query_key, w_value,
+            dest, packed, near, from_next, from_prior, from_across, query, keys, values, norms,
+            gain_first, w_query_key, w_value, w_out, gain_second, w_up, w_down,
         )
     else:
         targets = dest // clusters
@@ -550,28 +608,18 @@
         for offset in range(lanes):
             block = picked(leaving, offset)
             back = put(back, offset, shift(block, lanes - offset) if offset else block)
-        far = back.reshape(rows, columns)
-
-    block_out = pl.pallas_call(
-        functools.partial(finish_kernel, lanes, clusters, head_size, groups),
-        out_shape=wide,
-        in_specs=[in_smem()] + [in_vmem()] * (7 + groups + 4),
-        out_specs=anywhere(),
-        scratch_shapes=[
-            pltpu.VMEM((regions * pooled, columns), bf16),
-            pltpu.VMEM((HEADS, tall, regions * pooled), bf16),
-            pltpu.VMEM((columns, rows), bf16),
-            pltpu.VMEM((rows, columns), bf16),
-        ]
-        + scalars
-        + [pltpu.SemaphoreType.DMA((clusters,))],
-        cost_estimate=cost(20 * rows * columns * columns, 8 * rows * columns),
-        compiler_params=params(),
-        name="finish",
-    )(
-        dest, packed, far, query, keys, values, norms, gathered, *partial, w_out, gain_second,
-        w_up, w_down,
-    )
+        block_out = pl.pallas_call(
+            functools.partial(finish_kernel, lanes, clusters),
+            out_shape=wide,
+            in_specs=[in_smem()] + [in_vmem()] * 7,
+            out_specs=anywhere(),
+            scratch_shapes=last_scratch,
+            cost_estimate=cost(20 * rows * columns * columns, 8 * rows * columns),
+            compiler_params=params(),
+            name="finish",
+        )(
+            dest, packed, near, back.reshape(rows, columns).T, w_out, gain_second, w_up, w_down
+        )
     return block_out.reshape(points.shape)
 
 

time: 84.1 us -> 80.8 us (0.961)
  Pallas kernels: 69.5 us -> 67.1 us
  starting transfers between devices: 10.4 us -> 9.17 us
    pallas_call x2, Pallas kernels: 7.48 us -> 6 us  [per_device(): pl.pallas_call(functools.partial(near_part_kernel, group, head_size), out...]
    ppermute x3, waiting for transfers between devices: 0.02 us -> 1.46 us  [per_device(): lax.ppermute(gathered, 'region', [(i, i ^ step) for i in range(regions)])]
    ppermute x3, waiting for transfers between devices: 1.23 us -> 0.01 us  [shift(): lax.ppermute(data, 'ball', [(i, (i + offset) % lanes) for i in range(lane...]
    ppermute x3, starting transfers between devices: 6.01 us -> 5.11 us  [shift(): lax.ppermute(data, 'ball', [(i, (i + offset) % lanes) for i in range(lane...]
    pallas_call x2, Pallas kernels: 59 us -> 58.1 us  [the longest x1 30.3 us: per_device(): pl.pallas_call(functools.partial(near_kernel, head_size), out_shape=turne...]
  transfers between devices with their start and end apart: 6 -> 6, of which waited for: 2 -> 2; matrix products, arithmetic and copies ran while one was open for 0% -> 0% of each run, Pallas kernels for 10% -> 47%
where the time goes in v3:
time: 80.8 us; the launch traced here: 80.6 us
  Pallas kernels  67.1 us (83%)
  starting transfers between devices  9.17 us (11%)
  local copies, waits for them, and re-layouts  2.38 us (3%)
  waiting for transfers between devices  1.47 us (2%)
    pallas_call x1, Pallas kernels, per_device(): pl.pallas_call(functools.partial(near_kernel, head_size), out_shape=turne...  30.3 us
    pallas_call x1, Pallas kernels, per_device(): pl.pallas_call(functools.partial(far_finish_kernel, lanes, clusters, head...  27.8 us
    pallas_call x2, Pallas kernels, per_device(): pl.pallas_call(functools.partial(near_part_kernel, group, head_size), out...  6 us
    ppermute x3, starting transfers between devices, shift(): lax.ppermute(data, 'ball', [(i, (i + offset) % lanes) for i in range(lane...  5.11 us
    ppermute x3, starting transfers between devices, per_device(): lax.ppermute(gathered, 'region', [(i, i ^ step) for i in range(regions)])  4.06 us
    unnamed x18, local copies, waits for them, and re-layouts  2.34 us
    pallas_call x1, Pallas kernels, per_device(): pl.pallas_call(functools.partial(pack_kernel, lanes, clusters), out_shape...  1.77 us
  transfers between devices with their start and end apart: 6, of which 2 were waited for; matrix products, arithmetic and copies ran while one was open for 0% of the time, Pallas kernels for 47%

profile of v3, /device:TPU:0, one launch (start us, length us, event | category | flops | bytes accessed | tf_op | source)
XLA Modules:
  0.0 80.6 jit_solution(9095034594144862120)
XLA Ops:
  0.0 0.7 copy-done.1
  0.7 1.0 %copy-done = bf16[1,1,1024,256]{3,2,1,0:T(8,128)(2,1)S(1)} copy-done((bf16[1,1,1024,256]{3,2,1,0:T(8,128)(2,1)S(1)}, bf16[1,1,1024,256]{3,2,1,0:T(8,128)(2,1)}, u32[]{:S(2)}) %copy-start) | copy-done | bytes 524312
  1.7 1.8 %pack.1.points_ref = bf16[1024,256]{1,0:T(8,128)(2,1)S(1)} custom-call(s32[16]{0:T(128)S(1)} %bitcast.11, bf16[1024,256]{1,0:T(8,128)(2,1)S(1)} %bitcast.10), custom_call_target="tpu_custom_call" | custom-call | bytes 1048576 | tf_op jit(solution)/shard_map/pack/pallas_call | solution.py:479
  3.5 0.0 copy-start.7
  3.5 3.0 %collective-permute-start.5 = (bf16[1024,256]{1,0:T(8,128)(2,1)S(1)}, bf16[1024,256]{1,0:T(8,128)(2,1)S(1)}, u32[]{:S(2)}, u32[]{:S(2)}) collective-permute-start(bf16[1024,256]{1,0:T(8,128)(2,1)S(1)} %pack.1.points_ref), channel_id=1, source_target_pairs={{0,16},{8,24},{16,0},{24,8},{1,17},{9,25},{17,1},{25,9},{2,18},{10... | collective-permute-start | bytes 1572872 | tf_op jit(solution)/shard_map/ppermute | solution.py:477
  6.5 1.3 %project.1 = (bf16[256,1024]{1,0:T(8,128)(2,1)S(1)}, bf16[1024,256]{1,0:T(8,128)(2,1)S(1)}, bf16[8,48,1024]{2,1,0:T(8,128)(2,1)S(1)}, bf16[128,256]{1,0:T(8,128)(2,1)S(1)}, f32[8,128]{1,0:T(8,128)S(1)}) custom-call(bf16[1024,256]{1,0:T(8,128)(2,1)S(1)} %pack.1.points_ref, f32[1,256]{1,0:T(1,128)S(1)} %bitcast.13, bf16[256,512]{1,0:T(8,128)(2,1)S(1)} %copy-done.4, ...), custom_call_target="tpu_custom_call" | custom-call | flops 402653184 | bytes 2621440 | tf_op jit(solution)/shard_map/project/pallas_call | solution.py:498
  7.8 2.7 %collective-permute-start = (bf16[1,128,256]{2,1,0:T(8,128)(2,1)S(1)}, bf16[1,128,256]{2,1,0:T(8,128)(2,1)S(1)}, u32[]{:S(2)}, u32[]{:S(2)}) collective-permute-start(bf16[1,128,256]{2,1,0:T(8,128)(2,1)S(1)} %bitcast.6), channel_id=1, source_target_pairs={{0,4},{1,5},{2,6},{3,7},{4,0},{5,1},{6,2},{7,3},{8,12},{9,13},{10,... | collective-permute-start | bytes 196616 | tf_op jit(solution)/shard_map/ppermute | solution.py:517
  10.5 1.6 %collective-permute-start.3 = (bf16[512,256]{1,0:T(8,128)(2,1)S(1)}, bf16[512,256]{1,0:T(8,128)(2,1)S(1)}, u32[]{:S(2)}, u32[]{:S(2)}) collective-permute-start(bf16[512,256]{1,0:T(8,128)(2,1)S(1)} %get-tuple-element.16), channel_id=1, source_target_pairs={{0,24},{8,0},{16,8},{24,16},{1,25},{9,1},{17,9},{25,17},{2,26},{10... | collective-permute-start | bytes 786440 | tf_op jit(solution)/shard_map/ppermute | solution.py:477
  12.1 0.5 collective-permute-start.4
  12.6 0.8 collective-permute-done
  13.3 1.3 %collective-permute-start.1 = (bf16[2,128,256]{2,1,0:T(8,128)(2,1)S(1)}, bf16[2,128,256]{2,1,0:T(8,128)(2,1)S(1)}, u32[]{:S(2)}, u32[]{:S(2)}) collective-permute-start(bf16[2,128,256]{2,1,0:T(8,128)(2,1)S(1)} %pad_maximum_fusion.2), channel_id=1, source_target_pairs={{0,2},{1,3},{2,0},{3,1},{4,6},{5,7},{6,4},{7,5},{8,10},{9,11},{10,... | collective-permute-start | bytes 393224 | tf_op jit(solution)/shard_map/ppermute | solution.py:517
  14.7 3.0 %near_part.3.rest_1_ = f32[4,40,1024]{2,1,0:T(8,128)S(1)} custom-call(bf16[256,1024]{1,0:T(8,128)(2,1)S(1)} %get-tuple-element.10.qt_ref, bf16[1024,256]{1,0:T(8,128)(2,1)S(1)} %get-tuple-element.11.k_ref, bf16[8,48,1024]{2,1,0:T(8,128)(2,1)S(1)} %get-tuple-element.12.vt_ref), custom_call_target="tpu_custom_call" | custom-call | flops 3221225472 | bytes 1048576 | tf_op jit(solution)/shard_map/near_part/pallas_call | solution.py:522
  17.7 0.7 collective-permute-done.1
  18.4 0.1 collective-permute-start.2
  18.5 3.0 %near_part.2.rest_0_ = f32[4,40,1024]{2,1,0:T(8,128)S(1)} custom-call(bf16[256,1024]{1,0:T(8,128)(2,1)S(1)} %get-tuple-element.10.qt_ref, bf16[1024,256]{1,0:T(8,128)(2,1)S(1)} %get-tuple-element.11.k_ref, bf16[8,48,1024]{2,1,0:T(8,128)(2,1)S(1)} %get-tuple-element.12.vt_ref), custom_call_target="tpu_custom_call" | custom-call | flops 3221225472 | bytes 1048576 | tf_op jit(solution)/shard_map/near_part/pallas_call | solution.py:522
  21.5 0.0 collective-permute-done.2
  21.5 0.1 pad_maximum_fusion.pool_ref
  21.6 0.0 copy-start.2
  21.6 0.0 copy-start.3
  21.6 0.0 copy-start.6
  21.6 30.3 %near.1.near_ref = bf16[256,1024]{1,0:T(8,128)(2,1)S(1)} custom-call(bf16[256,1024]{1,0:T(8,128)(2,1)S(1)} %get-tuple-element.10.qt_ref, bf16[1024,256]{1,0:T(8,128)(2,1)S(1)} %get-tuple-element.11.k_ref, bf16[8,48,1024]{2,1,0:T(8,128)(2,1)S(1)} %get-tuple-element.12.vt_ref, f32[8,128]{1,0:T(8,128)S(1)} %get-tuple-element.13.norms_ref, ...), custom_call_target="tpu_custom_call" | custom-call | flops 3221225472 | bytes 1048576 | tf_op jit(solution)/shard_map/near/pallas_call | solution.py:534
  52.0 0.0 copy-start.8
  52.0 0.6 copy-done.8
  52.6 27.8 %far_finish.1 = bf16[1024,256]{1,0:T(8,128)(2,1)} custom-call(s32[16]{0:T(128)S(1)} %bitcast.12, bf16[1024,256]{1,0:T(8,128)(2,1)S(1)} %pack.1.points_ref, bf16[256,1024]{1,0:T(8,128)(2,1)S(1)} %near.1.near_ref, bf16[512,256]{1,0:T(8,128)(2,1)S(1)} %collective-permute-done.3.next_ref, bf16[512,256]{1,0:T(8,128)(2,1)S(1)} %collective-permute-done.4.prior_ref, ...), custom_call_target="tpu_custom_call" | custom-call | flops 6442450944 | bytes 1048576 | tf_op jit(solution)/shard_map/far_finish/pallas_call | solution.py:554
  (16 shorter events, 0.1 us)
Async XLA Ops:
  0.0 0.7 copy-start.1
  0.7 1.0 %copy-start = (bf16[1,1,1024,256]{3,2,1,0:T(8,128)(2,1)S(1)}, bf16[1,1,1024,256]{3,2,1,0:T(8,128)(2,1)}, u32[]{:S(2)}) copy-start(bf16[1,1,1024,256]{3,2,1,0:T(8,128)(2,1)} %param.9) | copy-start | bytes 1572868
  1.7 4.8 %copy-start.4 = (bf16[256,512]{1,0:T(8,128)(2,1)S(1)}, bf16[256,512]{1,0:T(8,128)(2,1)}, u32[]{:S(2)}) copy-start(bf16[256,512]{1,0:T(8,128)(2,1)} %wqk_ref.3) | copy-start | bytes 786436
  1.7 4.8 %copy-start.5 = (bf16[256,256]{1,0:T(8,128)(2,1)S(1)}, bf16[256,256]{1,0:T(8,128)(2,1)}, u32[]{:S(2)}) copy-start(bf16[256,256]{1,0:T(8,128)(2,1)} %wv_ref.3) | copy-start | bytes 393220
  3.5 3.1 %copy-start.7 = (f32[256]{0:T(256)S(1)}, f32[256]{0:T(256)}, u32[]{:S(2)}) copy-start(f32[256]{0:T(256)} %param.10) | copy-start | bytes 3076
  3.5 48.5 %collective-permute-start.5 = (bf16[1024,256]{1,0:T(8,128)(2,1)S(1)}, bf16[1024,256]{1,0:T(8,128)(2,1)S(1)}, u32[]{:S(2)}, u32[]{:S(2)}) collective-permute-start(bf16[1024,256]{1,0:T(8,128)(2,1)S(1)} %pack.1.points_ref), channel_id=1, source_target_pairs={{0,16},{8,24},{16,0},{24,8},{1,17},{9,25},{17,1},{25,9},{2,18},{10... | collective-permute-start | bytes 1572872 | tf_op jit(solution)/shard_map/ppermute | solution.py:477
  7.8 5.5 %collective-permute-start = (bf16[1,128,256]{2,1,0:T(8,128)(2,1)S(1)}, bf16[1,128,256]{2,1,0:T(8,128)(2,1)S(1)}, u32[]{:S(2)}, u32[]{:S(2)}) collective-permute-start(bf16[1,128,256]{2,1,0:T(8,128)(2,1)S(1)} %bitcast.6), channel_id=1, source_target_pairs={{0,4},{1,5},{2,6},{3,7},{4,0},{5,1},{6,2},{7,3},{8,12},{9,13},{10,... | collective-permute-start | bytes 196616 | tf_op jit(solution)/shard_map/ppermute | solution.py:517
  10.5 41.5 %collective-permute-start.3 = (bf16[512,256]{1,0:T(8,128)(2,1)S(1)}, bf16[512,256]{1,0:T(8,128)(2,1)S(1)}, u32[]{:S(2)}, u32[]{:S(2)}) collective-permute-start(bf16[512,256]{1,0:T(8,128)(2,1)S(1)} %get-tuple-element.16), channel_id=1, source_target_pairs={{0,24},{8,0},{16,8},{24,16},{1,25},{9,1},{17,9},{25,17},{2,26},{10... | collective-permute-start | bytes 786440 | tf_op jit(solution)/shard_map/ppermute | solution.py:477
  12.1 39.9 %collective-permute-start.4 = (bf16[512,256]{1,0:T(8,128)(2,1)S(1)}, bf16[512,256]{1,0:T(8,128)(2,1)S(1)}, u32[]{:S(2)}, u32[]{:S(2)}) collective-permute-start(bf16[512,256]{1,0:T(8,128)(2,1)S(1)} %get-tuple-element.15), channel_id=1, source_target_pairs={{0,8},{8,16},{16,24},{24,0},{1,9},{9,17},{17,25},{25,1},{2,10},{10... | collective-permute-start | bytes 786440 | tf_op jit(solution)/shard_map/ppermute | solution.py:477
  13.3 5.0 %collective-permute-start.1 = (bf16[2,128,256]{2,1,0:T(8,128)(2,1)S(1)}, bf16[2,128,256]{2,1,0:T(8,128)(2,1)S(1)}, u32[]{:S(2)}, u32[]{:S(2)}) collective-permute-start(bf16[2,128,256]{2,1,0:T(8,128)(2,1)S(1)} %pad_maximum_fusion.2), channel_id=1, source_target_pairs={{0,2},{1,3},{2,0},{3,1},{4,6},{5,7},{6,4},{7,5},{8,10},{9,11},{10,... | collective-permute-start | bytes 393224 | tf_op jit(solution)/shard_map/ppermute | solution.py:517
  18.4 3.1 %collective-permute-start.2 = (bf16[4,128,256]{2,1,0:T(8,128)(2,1)S(1)}, bf16[4,128,256]{2,1,0:T(8,128)(2,1)S(1)}, u32[]{:S(2)}, u32[]{:S(2)}) collective-permute-start(bf16[4,128,256]{2,1,0:T(8,128)(2,1)S(1)} %pad_maximum_fusion.1), channel_id=1, source_target_pairs={{0,1},{1,0},{2,3},{3,2},{4,5},{5,4},{6,7},{7,6},{8,9},{9,8},{10,11... | collective-permute-start | bytes 786440 | tf_op jit(solution)/shard_map/ppermute | solution.py:517
  21.6 30.4 %copy-start.2 = (bf16[256,1024]{1,0:T(8,128)(2,1)S(1)}, bf16[256,1024]{1,0:T(8,128)(2,1)}, u32[]{:S(2)}) copy-start(bf16[256,1024]{1,0:T(8,128)(2,1)} %up_ref.1) | copy-start | bytes 1572868
  21.6 30.4 %copy-start.3 = (bf16[1024,256]{1,0:T(8,128)(2,1)S(1)}, bf16[1024,256]{1,0:T(8,128)(2,1)}, u32[]{:S(2)}) copy-start(bf16[1024,256]{1,0:T(8,128)(2,1)} %down_ref.1) | copy-start | bytes 1572868
  21.6 30.4 %copy-start.6 = (bf16[256,256]{1,0:T(8,128)(2,1)S(1)}, bf16[256,256]{1,0:T(8,128)(2,1)}, u32[]{:S(2)}) copy-start(bf16[256,256]{1,0:T(8,128)(2,1)} %wo_ref.1) | copy-start | bytes 393220
  52.0 0.7 copy-start.8

commit v4 on v3

--- a/solution.py
+++ b/solution.py
@@ -126,7 +126,7 @@
     return jnp.exp2(scores * factor_of(head_size)).astype(bf16)
 
 
-def plain_attention(qt_ref, columns_of_query, heads, parts_of, head_size, store):
+def attention_jobs(qt_ref, columns_of_query, heads, parts_of, head_size, store):
     per_tile = TILE // head_size
     kept = head_size + 8
     sums = {}
@@ -161,7 +161,7 @@
             ]
             for index, (keys, values, row) in enumerate(blocks):
                 jobs.append(job(start, head, keys, values, row, index + 1 == len(blocks)))
-    run_jobs(jobs)
+    return jobs
 
 
 def divided(sums, head_size):
@@ -216,9 +216,19 @@
     return half + half * jnp.tanh(inner)
 
 
-def pack_kernel(lanes, clusters, dest_hbm, points_ref, packed_ref, dest, slots, counts, sems):
+def pack_kernel(
+    lanes, clusters, dest_hbm, points_ref, gain_first, gain_second, packed_ref, first_ref,
+    second_ref, dest_ref, dest, slots, counts, sems,
+):
     fetch = pltpu.make_async_copy(dest_hbm, dest, sems.at[clusters])
     fetch.start()
+    moved = [
+        pltpu.make_async_copy(gain_first, first_ref, sems.at[clusters + 1]),
+        pltpu.make_async_copy(gain_second, second_ref, sems.at[clusters + 2]),
+        pltpu.make_async_copy(dest_hbm, dest_ref, sems.at[clusters + 3]),
+    ]
+    for copy in moved:
+        copy.start()
     fetch.wait()
     places, _ = packed_places(dest, clusters, lanes, slots, counts)
     copies = [
@@ -231,15 +241,15 @@
     ]
     for copy in copies:
         copy.start()
-    for copy in copies:
+    for copy in moved + copies:
         copy.wait()
 
 
 def project_kernel(
-    head_size, points_ref, gain_ref, wqk_ref, wv_ref, qt_ref, k_ref, vt_ref, pool_ref, norms_ref
+    head_size, packed_ref, gain_ref, wqk_ref, wv_ref, qt_ref, k_ref, vt_ref, pool_ref, facts_ref
 ):
-    rows, columns = points_ref.shape
-    normed = rms_norm(points_ref[...], gain_ref[...])
+    rows, columns = packed_ref.shape
+    normed = rms_norm(packed_ref[...], gain_ref[...])
     paired = dot32(normed, wqk_ref[...]).astype(bf16)
     values = dot32(normed, wv_ref[...]).astype(bf16)
     query, keys = paired[:, :columns], paired[:, columns:]
@@ -253,48 +263,48 @@
     qt_ref[...] = query.T
     for head, extended in enumerate(extended_values(values, head_size)):
         vt_ref[head] = extended
-    norms_ref[0:1] = head_norms(query, head_size)
-    norms_ref[1:2] = head_norms(keys, head_size)
-
-
-def near_part_kernel(group, head_size, qt_ref, k_ref, vt_ref, o_ref):
-    per_tile = TILE // head_size
+    facts_ref[0:1] = head_norms(query, head_size)
+    facts_ref[1:2] = head_norms(keys, head_size)
+
+
+def near_part_kernel(heads, head_size, qt_ref, k_ref, vt_ref, o_ref):
     rows = k_ref.shape[0]
 
     def store(head, queries, sums):
-        o_ref[head % per_tile, :, queries] = sums
-
-    plain_attention(
-        qt_ref,
-        range(0, rows, QUERY_BLOCK),
-        range(group * per_tile, (group + 1) * per_tile),
-        lambda start: [(k_ref, vt_ref, 0, rows)],
-        head_size,
-        store,
-    )
-
-
-def near_kernel(head_size, qt_ref, k_ref, vt_ref, norms_ref, pool_ref, *rest):
-    partial = rest[:-3]
+        o_ref[head - heads[0], :, queries] = sums
+
+    run_jobs(
+        attention_jobs(
+            qt_ref,
+            range(0, rows, QUERY_BLOCK),
+            heads,
+            lambda start: [(k_ref, vt_ref, 0, rows)],
+            head_size,
+            store,
+        )
+    )
+
+
+def near_kernel(head_size, qt_ref, k_ref, vt_ref, facts_ref, pool_ref, *rest):
+    partial = [(ref, inner) for ref in rest[:-3] for inner in range(ref.shape[0])]
     y_ref, kp_ref, vp_ref = rest[-3:]
     rows = k_ref.shape[0]
-    per_tile = TILE // head_size
     regions, pooled = pool_ref.shape[0], pool_ref.shape[1] // 2
     for region in range(regions):
         kp_ref[region * pooled : (region + 1) * pooled] = pool_ref[region, :pooled]
     gathered = jnp.concatenate([pool_ref[r, pooled:] for r in range(regions)], axis=0)
     for head, extended in enumerate(extended_values(gathered, head_size)):
         vp_ref[head] = extended
-    key_norms = jnp.maximum(norms_ref[1:2], head_norms(kp_ref[...], head_size))
-    safe = exponents_safe(norms_ref[0:1], key_norms, head_size)
+    key_norms = jnp.maximum(facts_ref[1:2], head_norms(kp_ref[...], head_size))
+    safe = exponents_safe(facts_ref[0:1], key_norms, head_size)
 
     def store(head, queries, sums):
-        sums = sums + partial[head // per_tile][head % per_tile, :, queries]
+        ref, inner = partial[head]
+        sums = sums + ref[inner, :, queries]
         y_ref[head * head_size : (head + 1) * head_size, queries] = divided(sums, head_size)
 
-    @pl.when(safe)
-    def _():
-        plain_attention(
+    run_jobs(
+        attention_jobs(
             qt_ref,
             range(0, rows, QUERY_BLOCK),
             range(HEADS),
@@ -302,6 +312,7 @@
             head_size,
             store,
         )
+    )
 
     @pl.when(jnp.logical_not(safe))
     def _():
@@ -318,10 +329,64 @@
         )
 
 
-def far_attention(
-    head_size, across, next_ref, prior_ref, across_ref, qt_ref, k_ref, vt_ref, norms_ref,
-    gain_ref, wqk_ref, wv_ref, kr_ref, vr_ref, y_ref,
+class OutputRows:
+    def __init__(
+        self, places, points_ref, near_ref, far_ref, wo_ref, gain_ref, up_ref, down_ref, out_ref,
+        done_ref, origin, sems,
+    ):
+        for cluster, place in enumerate(places):
+            origin[place // CLUSTER] = cluster
+        self.refs = points_ref, near_ref, far_ref, wo_ref, gain_ref, up_ref, down_ref
+        self.out_ref, self.done_ref, self.origin, self.sems = out_ref, done_ref, origin, sems
+        self.rows = points_ref.shape[0]
+
+    def back(self, slot):
+        target = pl.multiple_of(self.origin[slot] * CLUSTER, CLUSTER)
+        return pltpu.make_async_copy(
+            self.done_ref.at[pl.ds(slot * CLUSTER, CLUSTER)],
+            self.out_ref.at[pl.ds(target, CLUSTER)],
+            self.sems.at[slot],
+        )
+
+    def job(self, start):
+        points_ref, near_ref, far_ref, wo_ref, gain_ref, up_ref, down_ref = self.refs
+        block = slice(start, start + ROW_BLOCK)
+
+        def widen():
+            after = (
+                points_ref[block].astype(f32)
+                + dot32(near_ref[:, block].T, wo_ref[...])
+                + dot32(far_ref[:, block].T, wo_ref[...])
+            ).astype(bf16)
+            return after, dot32(rms_norm(after, gain_ref[...]), up_ref[...])
+
+        def narrow(widened):
+            after, hidden = widened
+            hidden = gelu(hidden).astype(bf16)
+            self.done_ref[block] = (after.astype(f32) + dot32(hidden, down_ref[...])).astype(bf16)
+            for slot in range(start // CLUSTER, (start + ROW_BLOCK) // CLUSTER):
+                self.back(slot).start()
+
+        return widen, narrow
+
+    def jobs(self, first, end):
+        return [self.job(start) for start in range(first, end, ROW_BLOCK)]
+
+    def wait(self):
+        for slot in range(self.rows // CLUSTER):
+            self.back(slot).wait()
+
+
+def far_finish_kernel(
+    lanes, clusters, head_size, dest_ref, points_ref, near_ref, next_ref, prior_ref, across_ref,
+    qt_ref, k_ref, vt_ref, facts_ref, gain_ref, gain_second, wqk_ref, wv_ref, wo_ref, up_ref,
+    down_ref, out_ref, kr_ref, vr_ref, y_ref, done_ref, slots, counts, origin, sems,
 ):
+    places, across = packed_places(dest_ref, clusters, lanes, slots, counts)
+    output = OutputRows(
+        places, points_ref, near_ref, y_ref, wo_ref, gain_second, up_ref, down_ref, out_ref,
+        done_ref, origin, sems,
+    )
     rows, columns = k_ref.shape
     half = rows // 2
     apart = jnp.concatenate([next_ref[...], prior_ref[...]], axis=0)
@@ -331,8 +396,8 @@
     kr_ref[...] = keys
     for head, extended in enumerate(extended_values(values, head_size)):
         vr_ref[head] = extended
-    key_norms = jnp.maximum(norms_ref[1:2], head_norms(keys, head_size))
-    safe = exponents_safe(norms_ref[0:1], key_norms, head_size)
+    key_norms = jnp.maximum(facts_ref[1:2], head_norms(keys, head_size))
+    safe = exponents_safe(facts_ref[0:1], key_norms, head_size)
 
     def store(head, queries, sums):
         y_ref[head * head_size : (head + 1) * head_size, queries] = divided(sums, head_size)
@@ -342,11 +407,14 @@
         other = half - mine
         return [(k_ref, vt_ref, mine, mine + half), (kr_ref, vr_ref, other, other + half)]
 
-    @pl.when(safe)
-    def _():
-        plain_attention(
-            qt_ref, range(0, rows, QUERY_BLOCK), range(HEADS), parts_of, head_size, store
-        )
+    def attend(start, end):
+        return attention_jobs(
+            qt_ref, range(start, end, QUERY_BLOCK), range(HEADS), parts_of, head_size, store
+        )
+
+    run_jobs(attend(0, rows))
+    run_jobs(output.jobs(0, rows), ahead=1)
+    output.wait()
 
     @pl.when(jnp.logical_not(safe))
     def _():
@@ -363,62 +431,8 @@
                 head_size,
                 y_ref,
             )
-
-
-def output_rows(
-    places, points_ref, near_ref, far_ref, wo_ref, gain_ref, up_ref, down_ref, out_ref, done_ref,
-    origin, sems,
-):
-    rows = points_ref.shape[0]
-    for cluster, place in enumerate(places):
-        origin[place // CLUSTER] = cluster
-
-    def back(slot):
-        return pltpu.make_async_copy(
-            done_ref.at[pl.ds(slot * CLUSTER, CLUSTER)],
-            out_ref.at[pl.ds(pl.multiple_of(origin[slot] * CLUSTER, CLUSTER), CLUSTER)],
-            sems.at[slot],
-        )
-
-    def job(start):
-        block = slice(start, start + ROW_BLOCK)
-
-        def widen():
-            after = (
-                points_ref[block].astype(f32)
-                + dot32(near_ref[:, block].T, wo_ref[...])
-                + dot32(far_ref[:, block].T, wo_ref[...])
-            ).astype(bf16)
-            return after, dot32(rms_norm(after, gain_ref[...]), up_ref[...])
-
-        def narrow(widened):
-            after, hidden = widened
-            hidden = gelu(hidden).astype(bf16)
-            done_ref[block] = (after.astype(f32) + dot32(hidden, down_ref[...])).astype(bf16)
-            for slot in range(start // CLUSTER, (start + ROW_BLOCK) // CLUSTER):
-                back(slot).start()
-
-        return widen, narrow
-
-    run_jobs([job(start) for start in range(0, rows, ROW_BLOCK)], ahead=1)
-    for slot in range(rows // CLUSTER):
-        back(slot).wait()
-
-
-def far_finish_kernel(
-    lanes, clusters, head_size, dest_ref, points_ref, near_ref, next_ref, prior_ref, across_ref,
-    qt_ref, k_ref, vt_ref, norms_ref, gain_ref, wqk_ref, wv_ref, wo_ref, gain_second, up_ref,
-    down_ref, out_ref, kr_ref, vr_ref, y_ref, done_ref, slots, counts, origin, sems,
-):
-    places, across = packed_places(dest_ref, clusters, lanes, slots, counts)
-    far_attention(
-        head_size, across, next_ref, prior_ref, across_ref, qt_ref, k_ref, vt_ref, norms_ref,
-        gain_ref, wqk_ref, wv_ref, kr_ref, vr_ref, y_ref,
-    )
-    output_rows(
-        places, points_ref, near_ref, y_ref, wo_ref, gain_second, up_ref, down_ref, out_ref,
-        done_ref, origin, sems,
-    )
+        run_jobs(output.jobs(0, rows), ahead=1)
+        output.wait()
 
 
 def finish_kernel(
@@ -426,10 +440,12 @@
     out_ref, done_ref, slots, counts, origin, sems,
 ):
     places, _ = packed_places(dest_ref, clusters, lanes, slots, counts)
-    output_rows(
+    output = OutputRows(
         places, points_ref, near_ref, far_ref, wo_ref, gain_ref, up_ref, down_ref, out_ref,
         done_ref, origin, sems,
     )
+    run_jobs(output.jobs(0, output.rows), ahead=1)
+    output.wait()
 
 
 def owner_far_kernel(head_size, x_ref, gain_ref, wqk_ref, wv_ref, out_ref, qt, k, vt, y):
@@ -464,7 +480,6 @@
     dest = cluster_dest.reshape(clusters)
     gain_first = gain_attn.reshape(1, columns)
     gain_second = gain_mlp.reshape(1, columns)
-    groups = columns // TILE
     wide = jax.ShapeDtypeStruct((rows, columns), bf16)
     turned = jax.ShapeDtypeStruct((columns, rows), bf16)
     extended = jax.ShapeDtypeStruct((HEADS, tall, rows), bf16)
@@ -476,26 +491,32 @@
     def shift(data, offset):
         return lax.ppermute(data, "ball", [(i, (i + offset) % lanes) for i in range(lanes)])
 
-    packed = pl.pallas_call(
+    row_of_gains = jax.ShapeDtypeStruct((1, columns), f32)
+    packed, gain_first, gain_second, dest = pl.pallas_call(
         functools.partial(pack_kernel, lanes, clusters),
-        out_shape=wide,
-        in_specs=[in_hbm(), in_hbm()],
-        out_specs=anywhere(),
+        out_shape=[wide, row_of_gains, row_of_gains, jax.ShapeDtypeStruct(dest.shape, jnp.int32)],
+        in_specs=[in_hbm()] * 4,
+        out_specs=[anywhere()] * 4,
         scratch_shapes=[pltpu.SMEM((clusters,), jnp.int32)]
         + scalars
-        + [pltpu.SemaphoreType.DMA((clusters + 1,))],
+        + [pltpu.SemaphoreType.DMA((clusters + 4,))],
         cost_estimate=cost(0, 4 * rows * columns),
         compiler_params=params(),
         name="pack",
-    )(dest, flat)
+    )(
+        *(
+            pltpu.with_memory_space_constraint(held, pltpu.HBM)
+            for held in (dest, flat, gain_first, gain_second)
+        )
+    )
 
     pair_path = owners == 2 and lanes == 4
     if pair_path:
+        from_across = shift(packed, 2)
         from_next = shift(packed[:share], lanes - 1)
         from_prior = shift(packed[share:], 1)
-        from_across = shift(packed, 2)
-
-    query, keys, values, pool, norms = pl.pallas_call(
+
+    query, keys, values, pool, facts = pl.pallas_call(
         functools.partial(project_kernel, head_size),
         out_shape=[
             turned,
@@ -511,30 +532,31 @@
         name="project",
     )(packed, gain_first, w_query_key, w_value)
 
+    def across_regions(data, mask):
+        return lax.ppermute(data, "region", [(i, i ^ mask) for i in range(regions)])
+
     gathered = pool.reshape(1, 2 * pooled, columns)
     step = regions // 2
     while step:
-        other = lax.ppermute(gathered, "region", [(i, i ^ step) for i in range(regions)])
-        gathered = jnp.concatenate([gathered, other], axis=0)
+        gathered = jnp.concatenate([gathered, across_regions(gathered, step)], axis=0)
         step //= 2
-
     partial = [
         pl.pallas_call(
-            functools.partial(near_part_kernel, group, head_size),
-            out_shape=jax.ShapeDtypeStruct((HEADS // groups, kept, rows), f32),
+            functools.partial(near_part_kernel, heads, head_size),
+            out_shape=jax.ShapeDtypeStruct((len(heads), kept, rows), f32),
             in_specs=[in_vmem()] * 3,
             out_specs=in_vmem(),
-            cost_estimate=attention_cost(rows, rows, HEADS // groups),
+            cost_estimate=attention_cost(rows, rows, len(heads)),
             compiler_params=params(),
             name="near_part",
         )(query, keys, values)
-        for group in range(groups)
+        for heads in (range(HEADS // 2), range(HEADS // 2, HEADS))
     ]
 
     near = pl.pallas_call(
         functools.partial(near_kernel, head_size),
         out_shape=turned,
-        in_specs=[in_vmem()] * (5 + groups),
+        in_specs=[in_vmem()] * (5 + len(partial)),
         out_specs=in_vmem(),
         scratch_shapes=[
             pltpu.VMEM((regions * pooled, columns), bf16),
@@ -543,7 +565,7 @@
         cost_estimate=attention_cost(rows, regions * pooled, HEADS),
         compiler_params=params(),
         name="near",
-    )(query, keys, values, norms, gathered, *partial)
+    )(query, keys, values, facts, gathered, *partial)
 
     last_scratch = (
         [pltpu.VMEM((rows, columns), bf16)]
@@ -566,8 +588,8 @@
             compiler_params=params(),
             name="far_finish",
         )(
-            dest, packed, near, from_next, from_prior, from_across, query, keys, values, norms,
-            gain_first, w_query_key, w_value, w_out, gain_second, w_up, w_down,
+            dest, packed, near, from_next, from_prior, from_across, query, keys, values, facts,
+            gain_first, gain_second, w_query_key, w_value, w_out, w_up, w_down,
         )
     else:
         targets = dest // clusters

time: 80.8 us -> 90.7 us (1.12)
  Pallas kernels: 67.1 us -> 79.3 us
  local copies, waits for them, and re-layouts: 2.38 us -> 0.06 us
    pallas_call x1, Pallas kernels: 27.8 us -> 36.8 us  [per_device(): pl.pallas_call(functools.partial(far_finish_kernel, lanes, clusters, head...]
    pallas_call x1, Pallas kernels: 30.3 us -> 33.1 us  [per_device(): pl.pallas_call(functools.partial(near_kernel, head_size), out_shape=turne...]
    unnamed x18 -> x10, local copies, waits for them, and re-layouts: 2.34 us -> 0.03 us
  transfers between devices with their start and end apart: 6 -> 6, of which waited for: 2 -> 2; matrix products, arithmetic and copies ran while one was open for 0% -> 0% of each run, Pallas kernels for 47% -> 45%
where the time goes in v4:
time: 90.7 us; the launch traced here: 90.4 us
  Pallas kernels  79.3 us (87%)
  starting transfers between devices  9.18 us (10%)
  waiting for transfers between devices  1.47 us (2%)
    pallas_call x1, Pallas kernels, per_device(): pl.pallas_call(functools.partial(far_finish_kernel, lanes, clusters, head...  36.8 us
    pallas_call x1, Pallas kernels, per_device(): pl.pallas_call(functools.partial(near_kernel, head_size), out_shape=turne...  33.1 us
    pallas_call x2, Pallas kernels, per_device(): pl.pallas_call(functools.partial(near_part_kernel, heads, head_size), out...  5.97 us
    ppermute x3, starting transfers between devices, shift(): lax.ppermute(data, 'ball', [(i, (i + offset) % lanes) for i in range(lane...  5.11 us
    ppermute x3, starting transfers between devices, across_regions(): return lax.ppermute(data, 'region', [(i, i ^ mask) for i in range(regions)])  4.07 us
    pallas_call x1, Pallas kernels, per_device(): pl.pallas_call(functools.partial(pack_kernel, lanes, clusters), out_shape...  2.14 us
  transfers between devices with their start and end apart: 6, of which 2 were waited for; matrix products, arithmetic and copies ran while one was open for 0% of the time, Pallas kernels for 45%

profile of v4, /device:TPU:0, one launch (start us, length us, event | category | flops | bytes accessed | tf_op | source)
XLA Modules:
  0.0 90.4 jit_solution(11763397647994306502)
XLA Ops:
  0.0 2.1 %pack.1 = (bf16[1024,256]{1,0:T(8,128)(2,1)S(1)}, f32[1,256]{1,0:T(1,128)S(1)}, f32[1,256]{1,0:T(1,128)S(1)}, s32[16]{0:T(128)S(1)}) custom-call(s32[16]{0:T(128)} %bitcast.13, bf16[1024,256]{1,0:T(8,128)(2,1)} %bitcast.10, f32[1,256]{1,0:T(1,128)} %bitcast.11, f32[1,256]{1,0:T(1,128)} %bitcast.12), custom_call_target="tpu_custom_call" | custom-call | bytes 1048576 | tf_op jit(solution)/shard_map/pack/pallas_call | solution.py:495
  2.1 3.0 %collective-permute-start.5 = (bf16[1024,256]{1,0:T(8,128)(2,1)S(1)}, bf16[1024,256]{1,0:T(8,128)(2,1)S(1)}, u32[]{:S(2)}, u32[]{:S(2)}) collective-permute-start(bf16[1024,256]{1,0:T(8,128)(2,1)S(1)} %get-tuple-element.15.packed_ref.points_ref), channel_id=1, source_target_pairs={{0,16},{8,24},{16,0},{24,8},{1,17},{9,25},{17,1},{25,9},{2,18},{10... | collective-permute-start | bytes 1572872 | tf_op jit(solution)/shard_map/ppermute | solution.py:492
  5.2 1.2 %project.1 = (bf16[256,1024]{1,0:T(8,128)(2,1)S(1)}, bf16[1024,256]{1,0:T(8,128)(2,1)S(1)}, bf16[8,48,1024]{2,1,0:T(8,128)(2,1)S(1)}, bf16[128,256]{1,0:T(8,128)(2,1)S(1)}, f32[8,128]{1,0:T(8,128)S(1)}) custom-call(bf16[1024,256]{1,0:T(8,128)(2,1)S(1)} %get-tuple-element.15.packed_ref.points_ref, f32[1,256]{1,0:T(1,128)S(1)} %get-tuple-element.16.gain_ref, ...), custom_call_target="tpu_custom_call" | custom-call | flops 402653184 | bytes 2621440 | tf_op jit(solution)/shard_map/project/pallas_call | solution.py:519
  6.4 2.7 %collective-permute-start = (bf16[1,128,256]{2,1,0:T(8,128)(2,1)S(1)}, bf16[1,128,256]{2,1,0:T(8,128)(2,1)S(1)}, u32[]{:S(2)}, u32[]{:S(2)}) collective-permute-start(bf16[1,128,256]{2,1,0:T(8,128)(2,1)S(1)} %bitcast.6), channel_id=1, source_target_pairs={{0,4},{1,5},{2,6},{3,7},{4,0},{5,1},{6,2},{7,3},{8,12},{9,13},{10,... | collective-permute-start | bytes 196616 | tf_op jit(solution)/shard_map/ppermute | solution.py:536
  9.1 1.5 %collective-permute-start.3 = (bf16[512,256]{1,0:T(8,128)(2,1)S(1)}, bf16[512,256]{1,0:T(8,128)(2,1)S(1)}, u32[]{:S(2)}, u32[]{:S(2)}) collective-permute-start(bf16[512,256]{1,0:T(8,128)(2,1)S(1)} %get-tuple-element.24), channel_id=1, source_target_pairs={{0,24},{8,0},{16,8},{24,16},{1,25},{9,1},{17,9},{25,17},{2,26},{10... | collective-permute-start | bytes 786440 | tf_op jit(solution)/shard_map/ppermute | solution.py:492
  10.6 0.6 collective-permute-start.4
  11.2 0.8 collective-permute-done
  12.0 1.3 %collective-permute-start.1 = (bf16[2,128,256]{2,1,0:T(8,128)(2,1)S(1)}, bf16[2,128,256]{2,1,0:T(8,128)(2,1)S(1)}, u32[]{:S(2)}, u32[]{:S(2)}) collective-permute-start(bf16[2,128,256]{2,1,0:T(8,128)(2,1)S(1)} %pad_maximum_fusion.2), channel_id=1, source_target_pairs={{0,2},{1,3},{2,0},{3,1},{4,6},{5,7},{6,4},{7,5},{8,10},{9,11},{10,... | collective-permute-start | bytes 393224 | tf_op jit(solution)/shard_map/ppermute | solution.py:536
  13.3 3.0 %near_part.2.rest_0_ = f32[4,40,1024]{2,1,0:T(8,128)S(1)} custom-call(bf16[256,1024]{1,0:T(8,128)(2,1)S(1)} %get-tuple-element.17.qt_ref, bf16[1024,256]{1,0:T(8,128)(2,1)S(1)} %get-tuple-element.18.k_ref, bf16[8,48,1024]{2,1,0:T(8,128)(2,1)S(1)} %get-tuple-element.19.vt_ref), custom_call_target="tpu_custom_call" | custom-call | flops 3221225472 | bytes 1048576 | tf_op jit(solution)/shard_map/near_part/pallas_call | solution.py:544
  16.3 0.7 collective-permute-done.1
  17.0 0.1 collective-permute-start.2
  17.1 3.0 %near_part.3.rest_1_ = f32[4,40,1024]{2,1,0:T(8,128)S(1)} custom-call(bf16[256,1024]{1,0:T(8,128)(2,1)S(1)} %get-tuple-element.17.qt_ref, bf16[1024,256]{1,0:T(8,128)(2,1)S(1)} %get-tuple-element.18.k_ref, bf16[8,48,1024]{2,1,0:T(8,128)(2,1)S(1)} %get-tuple-element.19.vt_ref), custom_call_target="tpu_custom_call" | custom-call | flops 3221225472 | bytes 1048576 | tf_op jit(solution)/shard_map/near_part/pallas_call | solution.py:544
  20.1 0.0 collective-permute-done.2
  20.1 0.1 pad_maximum_fusion.pool_ref
  20.2 0.0 copy-start
  20.2 0.0 copy-start.1
  20.2 0.0 copy-start.4
  20.2 33.1 %near.1.near_ref = bf16[256,1024]{1,0:T(8,128)(2,1)S(1)} custom-call(bf16[256,1024]{1,0:T(8,128)(2,1)S(1)} %get-tuple-element.17.qt_ref, bf16[1024,256]{1,0:T(8,128)(2,1)S(1)} %get-tuple-element.18.k_ref, bf16[8,48,1024]{2,1,0:T(8,128)(2,1)S(1)} %get-tuple-element.19.vt_ref, f32[8,128]{1,0:T(8,128)S(1)} %get-tuple-element.20.facts_ref, ...), custom_call_target="tpu_custom_call" | custom-call | flops 3221225472 | bytes 1048576 | tf_op jit(solution)/shard_map/near/pallas_call | solution.py:556
  53.4 0.0 collective-permute-done.3.next_ref
  53.4 0.0 collective-permute-done.4.prior_ref
  53.4 0.0 collective-permute-done.5.across_ref
  53.4 0.0 copy-done
  53.4 0.0 copy-done.1
  53.4 36.8 %far_finish.1 = bf16[1024,256]{1,0:T(8,128)(2,1)} custom-call(s32[16]{0:T(128)S(1)} %get-tuple-element.14.dest_ref, bf16[1024,256]{1,0:T(8,128)(2,1)S(1)} %get-tuple-element.15.packed_ref.points_ref, bf16[256,1024]{1,0:T(8,128)(2,1)S(1)} %near.1.near_ref, bf16[512,256]{1,0:T(8,128)(2,1)S(1)} %collective-permute-done.3.next_ref, ...), custom_call_target="tpu_custom_call" | custom-call | flops 6442450944 | bytes 1048576 | tf_op jit(solution)/shard_map/far_finish/pallas_call | solution.py:576
  (8 shorter events, 0.1 us)
Async XLA Ops:
  0.0 5.2 %copy-start.2 = (bf16[256,512]{1,0:T(8,128)(2,1)S(1)}, bf16[256,512]{1,0:T(8,128)(2,1)}, u32[]{:S(2)}) copy-start(bf16[256,512]{1,0:T(8,128)(2,1)} %wqk_ref.3) | copy-start | bytes 786436
  0.0 5.2 %copy-start.3 = (bf16[256,256]{1,0:T(8,128)(2,1)S(1)}, bf16[256,256]{1,0:T(8,128)(2,1)}, u32[]{:S(2)}) copy-start(bf16[256,256]{1,0:T(8,128)(2,1)} %wv_ref.3) | copy-start | bytes 393220
  2.1 51.2 %collective-permute-start.5 = (bf16[1024,256]{1,0:T(8,128)(2,1)S(1)}, bf16[1024,256]{1,0:T(8,128)(2,1)S(1)}, u32[]{:S(2)}, u32[]{:S(2)}) collective-permute-start(bf16[1024,256]{1,0:T(8,128)(2,1)S(1)} %get-tuple-element.15.packed_ref.points_ref), channel_id=1, source_target_pairs={{0,16},{8,24},{16,0},{24,8},{1,17},{9,25},{17,1},{25,9},{2,18},{10... | collective-permute-start | bytes 1572872 | tf_op jit(solution)/shard_map/ppermute | solution.py:492
  6.4 5.5 %collective-permute-start = (bf16[1,128,256]{2,1,0:T(8,128)(2,1)S(1)}, bf16[1,128,256]{2,1,0:T(8,128)(2,1)S(1)}, u32[]{:S(2)}, u32[]{:S(2)}) collective-permute-start(bf16[1,128,256]{2,1,0:T(8,128)(2,1)S(1)} %bitcast.6), channel_id=1, source_target_pairs={{0,4},{1,5},{2,6},{3,7},{4,0},{5,1},{6,2},{7,3},{8,12},{9,13},{10,... | collective-permute-start | bytes 196616 | tf_op jit(solution)/shard_map/ppermute | solution.py:536
  9.1 44.2 %collective-permute-start.3 = (bf16[512,256]{1,0:T(8,128)(2,1)S(1)}, bf16[512,256]{1,0:T(8,128)(2,1)S(1)}, u32[]{:S(2)}, u32[]{:S(2)}) collective-permute-start(bf16[512,256]{1,0:T(8,128)(2,1)S(1)} %get-tuple-element.24), channel_id=1, source_target_pairs={{0,24},{8,0},{16,8},{24,16},{1,25},{9,1},{17,9},{25,17},{2,26},{10... | collective-permute-start | bytes 786440 | tf_op jit(solution)/shard_map/ppermute | solution.py:492
  10.6 42.7 %collective-permute-start.4 = (bf16[512,256]{1,0:T(8,128)(2,1)S(1)}, bf16[512,256]{1,0:T(8,128)(2,1)S(1)}, u32[]{:S(2)}, u32[]{:S(2)}) collective-permute-start(bf16[512,256]{1,0:T(8,128)(2,1)S(1)} %get-tuple-element.23), channel_id=1, source_target_pairs={{0,8},{8,16},{16,24},{24,0},{1,9},{9,17},{17,25},{25,1},{2,10},{10... | collective-permute-start | bytes 786440 | tf_op jit(solution)/shard_map/ppermute | solution.py:492
  12.0 5.0 %collective-permute-start.1 = (bf16[2,128,256]{2,1,0:T(8,128)(2,1)S(1)}, bf16[2,128,256]{2,1,0:T(8,128)(2,1)S(1)}, u32[]{:S(2)}, u32[]{:S(2)}) collective-permute-start(bf16[2,128,256]{2,1,0:T(8,128)(2,1)S(1)} %pad_maximum_fusion.2), channel_id=1, source_target_pairs={{0,2},{1,3},{2,0},{3,1},{4,6},{5,7},{6,4},{7,5},{8,10},{9,11},{10,... | collective-permute-start | bytes 393224 | tf_op jit(solution)/shard_map/ppermute | solution.py:536
  17.0 3.1 %collective-permute-start.2 = (bf16[4,128,256]{2,1,0:T(8,128)(2,1)S(1)}, bf16[4,128,256]{2,1,0:T(8,128)(2,1)S(1)}, u32[]{:S(2)}, u32[]{:S(2)}) collective-permute-start(bf16[4,128,256]{2,1,0:T(8,128)(2,1)S(1)} %pad_maximum_fusion.1), channel_id=1, source_target_pairs={{0,1},{1,0},{2,3},{3,2},{4,5},{5,4},{6,7},{7,6},{8,9},{9,8},{10,11... | collective-permute-start | bytes 786440 | tf_op jit(solution)/shard_map/ppermute | solution.py:536
  20.2 33.2 %copy-start = (bf16[256,1024]{1,0:T(8,128)(2,1)S(1)}, bf16[256,1024]{1,0:T(8,128)(2,1)}, u32[]{:S(2)}) copy-start(bf16[256,1024]{1,0:T(8,128)(2,1)} %up_ref.1) | copy-start | bytes 1572868
  20.2 33.2 %copy-start.1 = (bf16[1024,256]{1,0:T(8,128)(2,1)S(1)}, bf16[1024,256]{1,0:T(8,128)(2,1)}, u32[]{:S(2)}) copy-start(bf16[1024,256]{1,0:T(8,128)(2,1)} %down_ref.1) | copy-start | bytes 1572868
  20.2 33.2 %copy-start.4 = (bf16[256,256]{1,0:T(8,128)(2,1)S(1)}, bf16[256,256]{1,0:T(8,128)(2,1)}, u32[]{:S(2)}) copy-start(bf16[256,256]{1,0:T(8,128)(2,1)} %wo_ref.1) | copy-start | bytes 393220

commit v5 on v4

--- a/solution.py
+++ b/solution.py
@@ -15,7 +15,9 @@
 SLOW_BLOCK = 256
 QUERY_BLOCK = 512
 KEY_BLOCK = 256
-AHEAD = 3
+AHEAD = 2
+PREPARE_AFTER = 4
+FIRST_HEADS = 5
 ROW_BLOCK = 256
 SAFE_EXPONENT = 104.0
 VMEM_LIMIT = 48 * 1024 * 1024
@@ -389,30 +391,43 @@
     )
     rows, columns = k_ref.shape
     half = rows // 2
-    apart = jnp.concatenate([next_ref[...], prior_ref[...]], axis=0)
-    normed = rms_norm(jnp.where(across, across_ref[...], apart), gain_ref[...])
-    keys = dot32(normed, wqk_ref[:, columns:]).astype(bf16)
-    values = dot32(normed, wv_ref[...]).astype(bf16)
-    kr_ref[...] = keys
-    for head, extended in enumerate(extended_values(values, head_size)):
-        vr_ref[head] = extended
-    key_norms = jnp.maximum(facts_ref[1:2], head_norms(keys, head_size))
-    safe = exponents_safe(facts_ref[0:1], key_norms, head_size)
+    found = {}
+
+    def prepare(_):
+        apart = jnp.concatenate([next_ref[...], prior_ref[...]], axis=0)
+        normed = rms_norm(jnp.where(across, across_ref[...], apart), gain_ref[...])
+        keys = dot32(normed, wqk_ref[:, columns:]).astype(bf16)
+        values = dot32(normed, wv_ref[...]).astype(bf16)
+        kr_ref[...] = keys
+        for head, extended in enumerate(extended_values(values, head_size)):
+            vr_ref[head] = extended
+        key_norms = jnp.maximum(facts_ref[1:2], head_norms(keys, head_size))
+        found["safe"] = exponents_safe(facts_ref[0:1], key_norms, head_size)
+
+    def keep(head, queries, sums):
+        found[head, queries.start] = sums
 
     def store(head, queries, sums):
+        sums = sums + found.pop((head, queries.start))
         y_ref[head * head_size : (head + 1) * head_size, queries] = divided(sums, head_size)
 
-    def parts_of(start):
+    def own_part(start):
         mine = start // half * half
-        other = half - mine
-        return [(k_ref, vt_ref, mine, mine + half), (kr_ref, vr_ref, other, other + half)]
-
-    def attend(start, end):
+        return [(k_ref, vt_ref, mine, mine + half)]
+
+    def arrived_part(start):
+        other = half - start // half * half
+        return [(kr_ref, vr_ref, other, other + half)]
+
+    def attend(parts_of, finish):
         return attention_jobs(
-            qt_ref, range(start, end, QUERY_BLOCK), range(HEADS), parts_of, head_size, store
-        )
-
-    run_jobs(attend(0, rows))
+            qt_ref, range(0, rows, QUERY_BLOCK), range(HEADS), parts_of, head_size, finish
+        )
+
+    jobs = attend(own_part, keep)
+    jobs.insert(PREPARE_AFTER, (lambda: None, prepare))
+    run_jobs(jobs + attend(arrived_part, store))
+    safe = found["safe"]
     run_jobs(output.jobs(0, rows), ahead=1)
     output.wait()
 
@@ -550,7 +565,7 @@
             compiler_params=params(),
             name="near_part",
         )(query, keys, values)
-        for heads in (range(HEADS // 2), range(HEADS // 2, HEADS))
+        for heads in (range(FIRST_HEADS), range(FIRST_HEADS, HEADS))
     ]
 
     near = pl.pallas_call(

time: 90.7 us -> 92.3 us (1.018)
  waiting for transfers between devices: 1.47 us -> 4 us
    ppermute x3, waiting for transfers between devices: 1.46 us -> 4 us  [across_regions(): return lax.ppermute(data, 'region', [(i, i ^ mask) for i in range(regions)])]
    ppermute x3, starting transfers between devices: 5.11 us -> 4.03 us  [shift(): lax.ppermute(data, 'ball', [(i, (i + offset) % lanes) for i in range(lane...]
  transfers between devices with their start and end apart: 6 -> 6, of which waited for: 2 -> 2; matrix products, arithmetic and copies ran while one was open for 0% -> 0% of each run, Pallas kernels for 45% -> 42%
where the time goes in v5:
time: 92.3 us; the launch traced here: 92.1 us
  Pallas kernels  78.7 us (85%)
  starting transfers between devices  8.83 us (10%)
  waiting for transfers between devices  4 us (4%)
    pallas_call x1, Pallas kernels, per_device(): pl.pallas_call(functools.partial(far_finish_kernel, lanes, clusters, head...  36.3 us
    pallas_call x1, Pallas kernels, per_device(): pl.pallas_call(functools.partial(near_kernel, head_size), out_shape=turne...  33 us
    pallas_call x2, Pallas kernels, per_device(): pl.pallas_call(functools.partial(near_part_kernel, heads, head_size), out...  5.97 us
    ppermute x3, starting transfers between devices, across_regions(): return lax.ppermute(data, 'region', [(i, i ^ mask) for i in range(regions)])  4.81 us
    ppermute x3, starting transfers between devices, shift(): lax.ppermute(data, 'ball', [(i, (i + offset) % lanes) for i in range(lane...  4.03 us
    ppermute x3, waiting for transfers between devices, across_regions(): return lax.ppermute(data, 'region', [(i, i ^ mask) for i in range(regions)])  4 us
    pallas_call x1, Pallas kernels, per_device(): pl.pallas_call(functools.partial(pack_kernel, lanes, clusters), out_shape...  2.14 us
  transfers between devices with their start and end apart: 6, of which 2 were waited for; matrix products, arithmetic and copies ran while one was open for 0% of the time, Pallas kernels for 42%

profile of v5, /device:TPU:0, one launch (start us, length us, event | category | flops | bytes accessed | tf_op | source)
XLA Modules:
  0.0 92.1 jit_solution(11716803399527111230)
XLA Ops:
  0.0 2.1 %pack.1 = (bf16[1024,256]{1,0:T(8,128)(2,1)S(1)}, f32[1,256]{1,0:T(1,128)S(1)}, f32[1,256]{1,0:T(1,128)S(1)}, s32[16]{0:T(128)S(1)}) custom-call(s32[16]{0:T(128)} %bitcast.13, bf16[1024,256]{1,0:T(8,128)(2,1)} %bitcast.10, f32[1,256]{1,0:T(1,128)} %bitcast.11, f32[1,256]{1,0:T(1,128)} %bitcast.12), custom_call_target="tpu_custom_call" | custom-call | bytes 1048576 | tf_op jit(solution)/shard_map/pack/pallas_call | solution.py:510
  2.1 0.0 copy-done.2
  2.2 0.0 copy-done.3
  2.2 1.2 %project.1 = (bf16[256,1024]{1,0:T(8,128)(2,1)S(1)}, bf16[1024,256]{1,0:T(8,128)(2,1)S(1)}, bf16[8,48,1024]{2,1,0:T(8,128)(2,1)S(1)}, bf16[128,256]{1,0:T(8,128)(2,1)S(1)}, f32[8,128]{1,0:T(8,128)S(1)}) custom-call(bf16[1024,256]{1,0:T(8,128)(2,1)S(1)} %get-tuple-element.15.packed_ref.points_ref, f32[1,256]{1,0:T(1,128)S(1)} %get-tuple-element.16.gain_ref, ...), custom_call_target="tpu_custom_call" | custom-call | flops 402653184 | bytes 2621440 | tf_op jit(solution)/shard_map/project/pallas_call | solution.py:534
  3.4 4.1 %collective-permute-start = (bf16[1,128,256]{2,1,0:T(8,128)(2,1)S(1)}, bf16[1,128,256]{2,1,0:T(8,128)(2,1)S(1)}, u32[]{:S(2)}, u32[]{:S(2)}) collective-permute-start(bf16[1,128,256]{2,1,0:T(8,128)(2,1)S(1)} %bitcast.6), channel_id=1, source_target_pairs={{0,4},{1,5},{2,6},{3,7},{4,0},{5,1},{6,2},{7,3},{8,12},{9,13},{10,... | collective-permute-start | bytes 196616 | tf_op jit(solution)/shard_map/ppermute | solution.py:551
  7.5 1.5 %collective-permute-start.5 = (bf16[1024,256]{1,0:T(8,128)(2,1)S(1)}, bf16[1024,256]{1,0:T(8,128)(2,1)S(1)}, u32[]{:S(2)}, u32[]{:S(2)}) collective-permute-start(bf16[1024,256]{1,0:T(8,128)(2,1)S(1)} %get-tuple-element.15.packed_ref.points_ref), channel_id=1, source_target_pairs={{0,16},{8,24},{16,0},{24,8},{1,17},{9,25},{17,1},{25,9},{2,18},{10... | collective-permute-start | bytes 1572872 | tf_op jit(solution)/shard_map/ppermute | solution.py:507
  9.1 2.1 %collective-permute-done = bf16[1,128,256]{2,1,0:T(8,128)(2,1)S(1)} collective-permute-done((bf16[1,128,256]{2,1,0:T(8,128)(2,1)S(1)}, bf16[1,128,256]{2,1,0:T(8,128)(2,1)S(1)}, u32[]{:S(2)}, u32[]{:S(2)}) %collective-permute-start) | collective-permute-done | bytes 65568 | tf_op jit(solution)/shard_map/ppermute | solution.py:551
  11.2 0.6 collective-permute-start.1
  11.9 2.5 %collective-permute-start.3 = (bf16[512,256]{1,0:T(8,128)(2,1)S(1)}, bf16[512,256]{1,0:T(8,128)(2,1)S(1)}, u32[]{:S(2)}, u32[]{:S(2)}) collective-permute-start(bf16[512,256]{1,0:T(8,128)(2,1)S(1)} %get-tuple-element.24), channel_id=1, source_target_pairs={{0,24},{8,0},{16,8},{24,16},{1,25},{9,1},{17,9},{25,17},{2,26},{10... | collective-permute-start | bytes 786440 | tf_op jit(solution)/shard_map/ppermute | solution.py:507
  14.4 0.0 collective-permute-start.4
  14.4 1.9 %collective-permute-done.1 = bf16[2,128,256]{2,1,0:T(8,128)(2,1)S(1)} collective-permute-done((bf16[2,128,256]{2,1,0:T(8,128)(2,1)S(1)}, bf16[2,128,256]{2,1,0:T(8,128)(2,1)S(1)}, u32[]{:S(2)}, u32[]{:S(2)}) %collective-permute-start.1) | collective-permute-done | bytes 131104 | tf_op jit(solution)/shard_map/ppermute | solution.py:551
  16.3 0.1 collective-permute-start.2
  16.3 3.7 %near_part.2.rest_0_ = f32[5,40,1024]{2,1,0:T(8,128)S(1)} custom-call(bf16[256,1024]{1,0:T(8,128)(2,1)S(1)} %get-tuple-element.17.qt_ref, bf16[1024,256]{1,0:T(8,128)(2,1)S(1)} %get-tuple-element.18.k_ref, bf16[8,48,1024]{2,1,0:T(8,128)(2,1)S(1)} %get-tuple-element.19.vt_ref), custom_call_target="tpu_custom_call" | custom-call | flops 4026531840 | bytes 1048576 | tf_op jit(solution)/shard_map/near_part/pallas_call | solution.py:559
  20.0 2.3 %near_part.3.rest_1_ = f32[3,40,1024]{2,1,0:T(8,128)S(1)} custom-call(bf16[256,1024]{1,0:T(8,128)(2,1)S(1)} %get-tuple-element.17.qt_ref, bf16[1024,256]{1,0:T(8,128)(2,1)S(1)} %get-tuple-element.18.k_ref, bf16[8,48,1024]{2,1,0:T(8,128)(2,1)S(1)} %get-tuple-element.19.vt_ref), custom_call_target="tpu_custom_call" | custom-call | flops 2415919104 | bytes 1048576 | tf_op jit(solution)/shard_map/near_part/pallas_call | solution.py:559
  22.3 0.0 collective-permute-done.2
  22.3 0.1 pad_maximum_fusion.pool_ref
  22.4 0.0 copy-start
  22.4 0.0 copy-start.1
  22.4 0.0 copy-start.4
  22.4 33.0 %near.1.near_ref = bf16[256,1024]{1,0:T(8,128)(2,1)S(1)} custom-call(bf16[256,1024]{1,0:T(8,128)(2,1)S(1)} %get-tuple-element.17.qt_ref, bf16[1024,256]{1,0:T(8,128)(2,1)S(1)} %get-tuple-element.18.k_ref, bf16[8,48,1024]{2,1,0:T(8,128)(2,1)S(1)} %get-tuple-element.19.vt_ref, f32[8,128]{1,0:T(8,128)S(1)} %get-tuple-element.20.facts_ref, ...), custom_call_target="tpu_custom_call" | custom-call | flops 3221225472 | bytes 1048576 | tf_op jit(solution)/shard_map/near/pallas_call | solution.py:571
  55.5 0.0 collective-permute-done.3.next_ref
  55.5 0.0 collective-permute-done.4.prior_ref
  55.5 0.0 collective-permute-done.5.across_ref
  55.5 36.3 %far_finish.1 = bf16[1024,256]{1,0:T(8,128)(2,1)} custom-call(s32[16]{0:T(128)S(1)} %get-tuple-element.14.dest_ref, bf16[1024,256]{1,0:T(8,128)(2,1)S(1)} %get-tuple-element.15.packed_ref.points_ref, bf16[256,1024]{1,0:T(8,128)(2,1)S(1)} %near.1.near_ref, bf16[512,256]{1,0:T(8,128)(2,1)S(1)} %collective-permute-done.3.next_ref, ...), custom_call_target="tpu_custom_call" | custom-call | flops 6442450944 | bytes 1048576 | tf_op jit(solution)/shard_map/far_finish/pallas_call | solution.py:591
  (8 shorter events, 0.1 us)
Async XLA Ops:
  0.0 2.2 %copy-start.2 = (bf16[256,512]{1,0:T(8,128)(2,1)S(1)}, bf16[256,512]{1,0:T(8,128)(2,1)}, u32[]{:S(2)}) copy-start(bf16[256,512]{1,0:T(8,128)(2,1)} %wqk_ref.3) | copy-start | bytes 786436
  0.0 2.2 %copy-start.3 = (bf16[256,256]{1,0:T(8,128)(2,1)S(1)}, bf16[256,256]{1,0:T(8,128)(2,1)}, u32[]{:S(2)}) copy-start(bf16[256,256]{1,0:T(8,128)(2,1)} %wv_ref.3) | copy-start | bytes 393220
  3.4 7.8 %collective-permute-start = (bf16[1,128,256]{2,1,0:T(8,128)(2,1)S(1)}, bf16[1,128,256]{2,1,0:T(8,128)(2,1)S(1)}, u32[]{:S(2)}, u32[]{:S(2)}) collective-permute-start(bf16[1,128,256]{2,1,0:T(8,128)(2,1)S(1)} %bitcast.6), channel_id=1, source_target_pairs={{0,4},{1,5},{2,6},{3,7},{4,0},{5,1},{6,2},{7,3},{8,12},{9,13},{10,... | collective-permute-start | bytes 196616 | tf_op jit(solution)/shard_map/ppermute | solution.py:551
  7.5 48.0 %collective-permute-start.5 = (bf16[1024,256]{1,0:T(8,128)(2,1)S(1)}, bf16[1024,256]{1,0:T(8,128)(2,1)S(1)}, u32[]{:S(2)}, u32[]{:S(2)}) collective-permute-start(bf16[1024,256]{1,0:T(8,128)(2,1)S(1)} %get-tuple-element.15.packed_ref.points_ref), channel_id=1, source_target_pairs={{0,16},{8,24},{16,0},{24,8},{1,17},{9,25},{17,1},{25,9},{2,18},{10... | collective-permute-start | bytes 1572872 | tf_op jit(solution)/shard_map/ppermute | solution.py:507
  11.2 5.0 %collective-permute-start.1 = (bf16[2,128,256]{2,1,0:T(8,128)(2,1)S(1)}, bf16[2,128,256]{2,1,0:T(8,128)(2,1)S(1)}, u32[]{:S(2)}, u32[]{:S(2)}) collective-permute-start(bf16[2,128,256]{2,1,0:T(8,128)(2,1)S(1)} %pad_maximum_fusion.2), channel_id=1, source_target_pairs={{0,2},{1,3},{2,0},{3,1},{4,6},{5,7},{6,4},{7,5},{8,10},{9,11},{10,... | collective-permute-start | bytes 393224 | tf_op jit(solution)/shard_map/ppermute | solution.py:551
  11.9 43.6 %collective-permute-start.3 = (bf16[512,256]{1,0:T(8,128)(2,1)S(1)}, bf16[512,256]{1,0:T(8,128)(2,1)S(1)}, u32[]{:S(2)}, u32[]{:S(2)}) collective-permute-start(bf16[512,256]{1,0:T(8,128)(2,1)S(1)} %get-tuple-element.24), channel_id=1, source_target_pairs={{0,24},{8,0},{16,8},{24,16},{1,25},{9,1},{17,9},{25,17},{2,26},{10... | collective-permute-start | bytes 786440 | tf_op jit(solution)/shard_map/ppermute | solution.py:507
  14.4 41.1 %collective-permute-start.4 = (bf16[512,256]{1,0:T(8,128)(2,1)S(1)}, bf16[512,256]{1,0:T(8,128)(2,1)S(1)}, u32[]{:S(2)}, u32[]{:S(2)}) collective-permute-start(bf16[512,256]{1,0:T(8,128)(2,1)S(1)} %get-tuple-element.23), channel_id=1, source_target_pairs={{0,8},{8,16},{16,24},{24,0},{1,9},{9,17},{17,25},{25,1},{2,10},{10... | collective-permute-start | bytes 786440 | tf_op jit(solution)/shard_map/ppermute | solution.py:507
  16.3 6.1 %collective-permute-start.2 = (bf16[4,128,256]{2,1,0:T(8,128)(2,1)S(1)}, bf16[4,128,256]{2,1,0:T(8,128)(2,1)S(1)}, u32[]{:S(2)}, u32[]{:S(2)}) collective-permute-start(bf16[4,128,256]{2,1,0:T(8,128)(2,1)S(1)} %pad_maximum_fusion.1), channel_id=1, source_target_pairs={{0,1},{1,0},{2,3},{3,2},{4,5},{5,4},{6,7},{7,6},{8,9},{9,8},{10,11... | collective-permute-start | bytes 786440 | tf_op jit(solution)/shard_map/ppermute | solution.py:551
  22.4 33.1 %copy-start = (bf16[256,1024]{1,0:T(8,128)(2,1)S(1)}, bf16[256,1024]{1,0:T(8,128)(2,1)}, u32[]{:S(2)}) copy-start(bf16[256,1024]{1,0:T(8,128)(2,1)} %up_ref.1) | copy-start | bytes 1572868
  22.4 33.1 %copy-start.1 = (bf16[1024,256]{1,0:T(8,128)(2,1)S(1)}, bf16[1024,256]{1,0:T(8,128)(2,1)}, u32[]{:S(2)}) copy-start(bf16[1024,256]{1,0:T(8,128)(2,1)} %down_ref.1) | copy-start | bytes 1572868
  22.4 33.1 %copy-start.4 = (bf16[256,256]{1,0:T(8,128)(2,1)S(1)}, bf16[256,256]{1,0:T(8,128)(2,1)}, u32[]{:S(2)}) copy-start(bf16[256,256]{1,0:T(8,128)(2,1)} %wo_ref.1) | copy-start | bytes 393220

commit v6 on v5

--- a/solution.py
+++ b/solution.py
@@ -561,7 +561,7 @@
             out_shape=jax.ShapeDtypeStruct((len(heads), kept, rows), f32),
             in_specs=[in_vmem()] * 3,
             out_specs=in_vmem(),
-            cost_estimate=attention_cost(rows, rows, len(heads)),
+            cost_estimate=attention_cost(rows, rows, HEADS // 2),
             compiler_params=params(),
             name="near_part",
         )(query, keys, values)

time: 92.3 us -> 89.4 us (0.969)
  waiting for transfers between devices: 4 us -> 0.79 us
    ppermute x3, waiting for transfers between devices: 4 us -> 0.78 us  [across_regions(): return lax.ppermute(data, 'region', [(i, i ^ mask) for i in range(regions)])]
    ppermute x3, starting transfers between devices: 4.03 us -> 5.11 us  [shift(): lax.ppermute(data, 'ball', [(i, (i + offset) % lanes) for i in range(lane...]
  transfers between devices with their start and end apart: 6 -> 6, of which waited for: 2 -> 1; matrix products, arithmetic and copies ran while one was open for 0% -> 0% of each run, Pallas kernels for 42% -> 45%
where the time goes in v6:
time: 89.4 us; the launch traced here: 89.2 us
  Pallas kernels  78.7 us (88%)
  starting transfers between devices  9.18 us (10%)
    pallas_call x1, Pallas kernels, per_device(): pl.pallas_call(functools.partial(far_finish_kernel, lanes, clusters, head...  36.3 us
    pallas_call x1, Pallas kernels, per_device(): pl.pallas_call(functools.partial(near_kernel, head_size), out_shape=turne...  33.1 us
    pallas_call x2, Pallas kernels, per_device(): pl.pallas_call(functools.partial(near_part_kernel, heads, head_size), out...  5.96 us
    ppermute x3, starting transfers between devices, shift(): lax.ppermute(data, 'ball', [(i, (i + offset) % lanes) for i in range(lane...  5.11 us
    ppermute x3, starting transfers between devices, across_regions(): return lax.ppermute(data, 'region', [(i, i ^ mask) for i in range(regions)])  4.07 us
    pallas_call x1, Pallas kernels, per_device(): pl.pallas_call(functools.partial(pack_kernel, lanes, clusters), out_shape...  2.14 us
  transfers between devices with their start and end apart: 6, of which 1 were waited for; matrix products, arithmetic and copies ran while one was open for 0% of the time, Pallas kernels for 45%

profile of v6, /device:TPU:0, one launch (start us, length us, event | category | flops | bytes accessed | tf_op | source)
XLA Modules:
  0.0 89.2 jit_solution(15002150621144378937)
XLA Ops:
  0.0 2.1 %pack.1 = (bf16[1024,256]{1,0:T(8,128)(2,1)S(1)}, f32[1,256]{1,0:T(1,128)S(1)}, f32[1,256]{1,0:T(1,128)S(1)}, s32[16]{0:T(128)S(1)}) custom-call(s32[16]{0:T(128)} %bitcast.13, bf16[1024,256]{1,0:T(8,128)(2,1)} %bitcast.10, f32[1,256]{1,0:T(1,128)} %bitcast.11, f32[1,256]{1,0:T(1,128)} %bitcast.12), custom_call_target="tpu_custom_call" | custom-call | bytes 1048576 | tf_op jit(solution)/shard_map/pack/pallas_call | solution.py:510
  2.1 3.0 %collective-permute-start.5 = (bf16[1024,256]{1,0:T(8,128)(2,1)S(1)}, bf16[1024,256]{1,0:T(8,128)(2,1)S(1)}, u32[]{:S(2)}, u32[]{:S(2)}) collective-permute-start(bf16[1024,256]{1,0:T(8,128)(2,1)S(1)} %get-tuple-element.15.packed_ref.points_ref), channel_id=1, source_target_pairs={{0,16},{8,24},{16,0},{24,8},{1,17},{9,25},{17,1},{25,9},{2,18},{10... | collective-permute-start | bytes 1572872 | tf_op jit(solution)/shard_map/ppermute | solution.py:507
  5.2 0.0 copy-done.2
  5.2 0.0 copy-done.3
  5.2 1.2 %project.1 = (bf16[256,1024]{1,0:T(8,128)(2,1)S(1)}, bf16[1024,256]{1,0:T(8,128)(2,1)S(1)}, bf16[8,48,1024]{2,1,0:T(8,128)(2,1)S(1)}, bf16[128,256]{1,0:T(8,128)(2,1)S(1)}, f32[8,128]{1,0:T(8,128)S(1)}) custom-call(bf16[1024,256]{1,0:T(8,128)(2,1)S(1)} %get-tuple-element.15.packed_ref.points_ref, f32[1,256]{1,0:T(1,128)S(1)} %get-tuple-element.16.gain_ref, ...), custom_call_target="tpu_custom_call" | custom-call | flops 402653184 | bytes 2621440 | tf_op jit(solution)/shard_map/project/pallas_call | solution.py:534
  6.4 2.7 %collective-permute-start = (bf16[1,128,256]{2,1,0:T(8,128)(2,1)S(1)}, bf16[1,128,256]{2,1,0:T(8,128)(2,1)S(1)}, u32[]{:S(2)}, u32[]{:S(2)}) collective-permute-start(bf16[1,128,256]{2,1,0:T(8,128)(2,1)S(1)} %bitcast.6), channel_id=1, source_target_pairs={{0,4},{1,5},{2,6},{3,7},{4,0},{5,1},{6,2},{7,3},{8,12},{9,13},{10,... | collective-permute-start | bytes 196616 | tf_op jit(solution)/shard_map/ppermute | solution.py:551
  9.1 1.5 %collective-permute-start.3 = (bf16[512,256]{1,0:T(8,128)(2,1)S(1)}, bf16[512,256]{1,0:T(8,128)(2,1)S(1)}, u32[]{:S(2)}, u32[]{:S(2)}) collective-permute-start(bf16[512,256]{1,0:T(8,128)(2,1)S(1)} %get-tuple-element.24), channel_id=1, source_target_pairs={{0,24},{8,0},{16,8},{24,16},{1,25},{9,1},{17,9},{25,17},{2,26},{10... | collective-permute-start | bytes 786440 | tf_op jit(solution)/shard_map/ppermute | solution.py:507
  10.6 0.6 collective-permute-start.4
  11.2 0.8 collective-permute-done
  12.0 1.3 %collective-permute-start.1 = (bf16[2,128,256]{2,1,0:T(8,128)(2,1)S(1)}, bf16[2,128,256]{2,1,0:T(8,128)(2,1)S(1)}, u32[]{:S(2)}, u32[]{:S(2)}) collective-permute-start(bf16[2,128,256]{2,1,0:T(8,128)(2,1)S(1)} %pad_maximum_fusion.2), channel_id=1, source_target_pairs={{0,2},{1,3},{2,0},{3,1},{4,6},{5,7},{6,4},{7,5},{8,10},{9,11},{10,... | collective-permute-start | bytes 393224 | tf_op jit(solution)/shard_map/ppermute | solution.py:551
  13.3 3.7 %near_part.2.rest_0_ = f32[5,40,1024]{2,1,0:T(8,128)S(1)} custom-call(bf16[256,1024]{1,0:T(8,128)(2,1)S(1)} %get-tuple-element.17.qt_ref, bf16[1024,256]{1,0:T(8,128)(2,1)S(1)} %get-tuple-element.18.k_ref, bf16[8,48,1024]{2,1,0:T(8,128)(2,1)S(1)} %get-tuple-element.19.vt_ref), custom_call_target="tpu_custom_call" | custom-call | flops 3221225472 | bytes 1048576 | tf_op jit(solution)/shard_map/near_part/pallas_call | solution.py:559
  17.0 0.0 collective-permute-done.1
  17.0 0.1 collective-permute-start.2
  17.1 2.3 %near_part.3.rest_1_ = f32[3,40,1024]{2,1,0:T(8,128)S(1)} custom-call(bf16[256,1024]{1,0:T(8,128)(2,1)S(1)} %get-tuple-element.17.qt_ref, bf16[1024,256]{1,0:T(8,128)(2,1)S(1)} %get-tuple-element.18.k_ref, bf16[8,48,1024]{2,1,0:T(8,128)(2,1)S(1)} %get-tuple-element.19.vt_ref), custom_call_target="tpu_custom_call" | custom-call | flops 3221225472 | bytes 1048576 | tf_op jit(solution)/shard_map/near_part/pallas_call | solution.py:559
  19.4 0.0 collective-permute-done.2
  19.4 0.1 pad_maximum_fusion.pool_ref
  19.5 0.0 copy-start
  19.5 0.0 copy-start.1
  19.5 0.0 copy-start.4
  19.5 33.1 %near.1.near_ref = bf16[256,1024]{1,0:T(8,128)(2,1)S(1)} custom-call(bf16[256,1024]{1,0:T(8,128)(2,1)S(1)} %get-tuple-element.17.qt_ref, bf16[1024,256]{1,0:T(8,128)(2,1)S(1)} %get-tuple-element.18.k_ref, bf16[8,48,1024]{2,1,0:T(8,128)(2,1)S(1)} %get-tuple-element.19.vt_ref, f32[8,128]{1,0:T(8,128)S(1)} %get-tuple-element.20.facts_ref, ...), custom_call_target="tpu_custom_call" | custom-call | flops 3221225472 | bytes 1048576 | tf_op jit(solution)/shard_map/near/pallas_call | solution.py:571
  52.6 0.0 collective-permute-done.3.next_ref
  52.6 0.0 collective-permute-done.4.prior_ref
  52.6 0.0 collective-permute-done.5.across_ref
  52.7 36.3 %far_finish.1 = bf16[1024,256]{1,0:T(8,128)(2,1)} custom-call(s32[16]{0:T(128)S(1)} %get-tuple-element.14.dest_ref, bf16[1024,256]{1,0:T(8,128)(2,1)S(1)} %get-tuple-element.15.packed_ref.points_ref, bf16[256,1024]{1,0:T(8,128)(2,1)S(1)} %near.1.near_ref, bf16[512,256]{1,0:T(8,128)(2,1)S(1)} %collective-permute-done.3.next_ref, ...), custom_call_target="tpu_custom_call" | custom-call | flops 6442450944 | bytes 1048576 | tf_op jit(solution)/shard_map/far_finish/pallas_call | solution.py:591
  (8 shorter events, 0.1 us)
Async XLA Ops:
  0.0 5.2 %copy-start.2 = (bf16[256,512]{1,0:T(8,128)(2,1)S(1)}, bf16[256,512]{1,0:T(8,128)(2,1)}, u32[]{:S(2)}) copy-start(bf16[256,512]{1,0:T(8,128)(2,1)} %wqk_ref.3) | copy-start | bytes 786436
  0.0 5.2 %copy-start.3 = (bf16[256,256]{1,0:T(8,128)(2,1)S(1)}, bf16[256,256]{1,0:T(8,128)(2,1)}, u32[]{:S(2)}) copy-start(bf16[256,256]{1,0:T(8,128)(2,1)} %wv_ref.3) | copy-start | bytes 393220
  2.1 50.5 %collective-permute-start.5 = (bf16[1024,256]{1,0:T(8,128)(2,1)S(1)}, bf16[1024,256]{1,0:T(8,128)(2,1)S(1)}, u32[]{:S(2)}, u32[]{:S(2)}) collective-permute-start(bf16[1024,256]{1,0:T(8,128)(2,1)S(1)} %get-tuple-element.15.packed_ref.points_ref), channel_id=1, source_target_pairs={{0,16},{8,24},{16,0},{24,8},{1,17},{9,25},{17,1},{25,9},{2,18},{10... | collective-permute-start | bytes 1572872 | tf_op jit(solution)/shard_map/ppermute | solution.py:507
  6.4 5.5 %collective-permute-start = (bf16[1,128,256]{2,1,0:T(8,128)(2,1)S(1)}, bf16[1,128,256]{2,1,0:T(8,128)(2,1)S(1)}, u32[]{:S(2)}, u32[]{:S(2)}) collective-permute-start(bf16[1,128,256]{2,1,0:T(8,128)(2,1)S(1)} %bitcast.6), channel_id=1, source_target_pairs={{0,4},{1,5},{2,6},{3,7},{4,0},{5,1},{6,2},{7,3},{8,12},{9,13},{10,... | collective-permute-start | bytes 196616 | tf_op jit(solution)/shard_map/ppermute | solution.py:551
  9.1 43.5 %collective-permute-start.3 = (bf16[512,256]{1,0:T(8,128)(2,1)S(1)}, bf16[512,256]{1,0:T(8,128)(2,1)S(1)}, u32[]{:S(2)}, u32[]{:S(2)}) collective-permute-start(bf16[512,256]{1,0:T(8,128)(2,1)S(1)} %get-tuple-element.24), channel_id=1, source_target_pairs={{0,24},{8,0},{16,8},{24,16},{1,25},{9,1},{17,9},{25,17},{2,26},{10... | collective-permute-start | bytes 786440 | tf_op jit(solution)/shard_map/ppermute | solution.py:507
  10.6 42.0 %collective-permute-start.4 = (bf16[512,256]{1,0:T(8,128)(2,1)S(1)}, bf16[512,256]{1,0:T(8,128)(2,1)S(1)}, u32[]{:S(2)}, u32[]{:S(2)}) collective-permute-start(bf16[512,256]{1,0:T(8,128)(2,1)S(1)} %get-tuple-element.23), channel_id=1, source_target_pairs={{0,8},{8,16},{16,24},{24,0},{1,9},{9,17},{17,25},{25,1},{2,10},{10... | collective-permute-start | bytes 786440 | tf_op jit(solution)/shard_map/ppermute | solution.py:507
  12.0 5.0 %collective-permute-start.1 = (bf16[2,128,256]{2,1,0:T(8,128)(2,1)S(1)}, bf16[2,128,256]{2,1,0:T(8,128)(2,1)S(1)}, u32[]{:S(2)}, u32[]{:S(2)}) collective-permute-start(bf16[2,128,256]{2,1,0:T(8,128)(2,1)S(1)} %pad_maximum_fusion.2), channel_id=1, source_target_pairs={{0,2},{1,3},{2,0},{3,1},{4,6},{5,7},{6,4},{7,5},{8,10},{9,11},{10,... | collective-permute-start | bytes 393224 | tf_op jit(solution)/shard_map/ppermute | solution.py:551
  17.0 2.4 %collective-permute-start.2 = (bf16[4,128,256]{2,1,0:T(8,128)(2,1)S(1)}, bf16[4,128,256]{2,1,0:T(8,128)(2,1)S(1)}, u32[]{:S(2)}, u32[]{:S(2)}) collective-permute-start(bf16[4,128,256]{2,1,0:T(8,128)(2,1)S(1)} %pad_maximum_fusion.1), channel_id=1, source_target_pairs={{0,1},{1,0},{2,3},{3,2},{4,5},{5,4},{6,7},{7,6},{8,9},{9,8},{10,11... | collective-permute-start | bytes 786440 | tf_op jit(solution)/shard_map/ppermute | solution.py:551
  19.5 33.1 %copy-start = (bf16[256,1024]{1,0:T(8,128)(2,1)S(1)}, bf16[256,1024]{1,0:T(8,128)(2,1)}, u32[]{:S(2)}) copy-start(bf16[256,1024]{1,0:T(8,128)(2,1)} %up_ref.1) | copy-start | bytes 1572868
  19.5 33.1 %copy-start.1 = (bf16[1024,256]{1,0:T(8,128)(2,1)S(1)}, bf16[1024,256]{1,0:T(8,128)(2,1)}, u32[]{:S(2)}) copy-start(bf16[1024,256]{1,0:T(8,128)(2,1)} %down_ref.1) | copy-start | bytes 1572868
  19.5 33.1 %copy-start.4 = (bf16[256,256]{1,0:T(8,128)(2,1)S(1)}, bf16[256,256]{1,0:T(8,128)(2,1)}, u32[]{:S(2)}) copy-start(bf16[256,256]{1,0:T(8,128)(2,1)} %wo_ref.1) | copy-start | bytes 393220

commit v7 on v6

--- a/solution.py
+++ b/solution.py
@@ -17,7 +17,7 @@
 KEY_BLOCK = 256
 AHEAD = 2
 PREPARE_AFTER = 4
-FIRST_HEADS = 5
+FIRST_HEADS = 6
 ROW_BLOCK = 256
 SAFE_EXPONENT = 104.0
 VMEM_LIMIT = 48 * 1024 * 1024

time: 89.4 us -> 89.4 us (level)
  no operation moved by 1% of the time
where the time goes in v7:
time: 89.4 us; the launch traced here: 89.2 us
  Pallas kernels  78.7 us (88%)
  starting transfers between devices  9.18 us (10%)
    pallas_call x1, Pallas kernels, per_device(): pl.pallas_call(functools.partial(far_finish_kernel, lanes, clusters, head...  36.3 us
    pallas_call x1, Pallas kernels, per_device(): pl.pallas_call(functools.partial(near_kernel, head_size), out_shape=turne...  33.1 us
    pallas_call x2, Pallas kernels, per_device(): pl.pallas_call(functools.partial(near_part_kernel, heads, head_size), out...  5.96 us
    ppermute x3, starting transfers between devices, shift(): lax.ppermute(data, 'ball', [(i, (i + offset) % lanes) for i in range(lane...  5.11 us
    ppermute x3, starting transfers between devices, across_regions(): return lax.ppermute(data, 'region', [(i, i ^ mask) for i in range(regions)])  4.07 us
    pallas_call x1, Pallas kernels, per_device(): pl.pallas_call(functools.partial(pack_kernel, lanes, clusters), out_shape...  2.14 us
  transfers between devices with their start and end apart: 6, of which 1 were waited for; matrix products, arithmetic and copies ran while one was open for 0% of the time, Pallas kernels for 45%

profile of v7, /device:TPU:0, one launch (start us, length us, event | category | flops | bytes accessed | tf_op | source)
XLA Modules:
  0.0 89.2 jit_solution(4248329771466922097)
XLA Ops:
  0.0 2.1 %pack.1 = (bf16[1024,256]{1,0:T(8,128)(2,1)S(1)}, f32[1,256]{1,0:T(1,128)S(1)}, f32[1,256]{1,0:T(1,128)S(1)}, s32[16]{0:T(128)S(1)}) custom-call(s32[16]{0:T(128)} %bitcast.13, bf16[1024,256]{1,0:T(8,128)(2,1)} %bitcast.10, f32[1,256]{1,0:T(1,128)} %bitcast.11, f32[1,256]{1,0:T(1,128)} %bitcast.12), custom_call_target="tpu_custom_call" | custom-call | bytes 1048576 | tf_op jit(solution)/shard_map/pack/pallas_call | solution.py:510
  2.1 3.0 %collective-permute-start.5 = (bf16[1024,256]{1,0:T(8,128)(2,1)S(1)}, bf16[1024,256]{1,0:T(8,128)(2,1)S(1)}, u32[]{:S(2)}, u32[]{:S(2)}) collective-permute-start(bf16[1024,256]{1,0:T(8,128)(2,1)S(1)} %get-tuple-element.15.packed_ref.points_ref), channel_id=1, source_target_pairs={{0,16},{8,24},{16,0},{24,8},{1,17},{9,25},{17,1},{25,9},{2,18},{10... | collective-permute-start | bytes 1572872 | tf_op jit(solution)/shard_map/ppermute | solution.py:507
  5.2 0.0 copy-done.2
  5.2 0.0 copy-done.3
  5.2 1.2 %project.1 = (bf16[256,1024]{1,0:T(8,128)(2,1)S(1)}, bf16[1024,256]{1,0:T(8,128)(2,1)S(1)}, bf16[8,48,1024]{2,1,0:T(8,128)(2,1)S(1)}, bf16[128,256]{1,0:T(8,128)(2,1)S(1)}, f32[8,128]{1,0:T(8,128)S(1)}) custom-call(bf16[1024,256]{1,0:T(8,128)(2,1)S(1)} %get-tuple-element.15.packed_ref.points_ref, f32[1,256]{1,0:T(1,128)S(1)} %get-tuple-element.16.gain_ref, ...), custom_call_target="tpu_custom_call" | custom-call | flops 402653184 | bytes 2621440 | tf_op jit(solution)/shard_map/project/pallas_call | solution.py:534
  6.4 2.7 %collective-permute-start = (bf16[1,128,256]{2,1,0:T(8,128)(2,1)S(1)}, bf16[1,128,256]{2,1,0:T(8,128)(2,1)S(1)}, u32[]{:S(2)}, u32[]{:S(2)}) collective-permute-start(bf16[1,128,256]{2,1,0:T(8,128)(2,1)S(1)} %bitcast.6), channel_id=1, source_target_pairs={{0,4},{1,5},{2,6},{3,7},{4,0},{5,1},{6,2},{7,3},{8,12},{9,13},{10,... | collective-permute-start | bytes 196616 | tf_op jit(solution)/shard_map/ppermute | solution.py:551
  9.1 1.5 %collective-permute-start.3 = (bf16[512,256]{1,0:T(8,128)(2,1)S(1)}, bf16[512,256]{1,0:T(8,128)(2,1)S(1)}, u32[]{:S(2)}, u32[]{:S(2)}) collective-permute-start(bf16[512,256]{1,0:T(8,128)(2,1)S(1)} %get-tuple-element.24), channel_id=1, source_target_pairs={{0,24},{8,0},{16,8},{24,16},{1,25},{9,1},{17,9},{25,17},{2,26},{10... | collective-permute-start | bytes 786440 | tf_op jit(solution)/shard_map/ppermute | solution.py:507
  10.6 0.6 collective-permute-start.4
  11.2 0.8 collective-permute-done
  12.0 1.3 %collective-permute-start.1 = (bf16[2,128,256]{2,1,0:T(8,128)(2,1)S(1)}, bf16[2,128,256]{2,1,0:T(8,128)(2,1)S(1)}, u32[]{:S(2)}, u32[]{:S(2)}) collective-permute-start(bf16[2,128,256]{2,1,0:T(8,128)(2,1)S(1)} %pad_maximum_fusion.2), channel_id=1, source_target_pairs={{0,2},{1,3},{2,0},{3,1},{4,6},{5,7},{6,4},{7,5},{8,10},{9,11},{10,... | collective-permute-start | bytes 393224 | tf_op jit(solution)/shard_map/ppermute | solution.py:551
  13.3 4.4 %near_part.2.rest_0_ = f32[6,40,1024]{2,1,0:T(8,128)S(1)} custom-call(bf16[256,1024]{1,0:T(8,128)(2,1)S(1)} %get-tuple-element.17.qt_ref, bf16[1024,256]{1,0:T(8,128)(2,1)S(1)} %get-tuple-element.18.k_ref, bf16[8,48,1024]{2,1,0:T(8,128)(2,1)S(1)} %get-tuple-element.19.vt_ref), custom_call_target="tpu_custom_call" | custom-call | flops 3221225472 | bytes 1048576 | tf_op jit(solution)/shard_map/near_part/pallas_call | solution.py:559
  17.7 0.0 collective-permute-done.1
  17.7 0.1 collective-permute-start.2
  17.8 1.6 %near_part.3.rest_1_ = f32[2,40,1024]{2,1,0:T(8,128)S(1)} custom-call(bf16[256,1024]{1,0:T(8,128)(2,1)S(1)} %get-tuple-element.17.qt_ref, bf16[1024,256]{1,0:T(8,128)(2,1)S(1)} %get-tuple-element.18.k_ref, bf16[8,48,1024]{2,1,0:T(8,128)(2,1)S(1)} %get-tuple-element.19.vt_ref), custom_call_target="tpu_custom_call" | custom-call | flops 3221225472 | bytes 1048576 | tf_op jit(solution)/shard_map/near_part/pallas_call | solution.py:559
  19.4 0.0 collective-permute-done.2
  19.4 0.1 pad_maximum_fusion.pool_ref
  19.5 0.0 copy-start
  19.5 0.0 copy-start.1
  19.5 0.0 copy-start.4
  19.5 33.1 %near.1.near_ref = bf16[256,1024]{1,0:T(8,128)(2,1)S(1)} custom-call(bf16[256,1024]{1,0:T(8,128)(2,1)S(1)} %get-tuple-element.17.qt_ref, bf16[1024,256]{1,0:T(8,128)(2,1)S(1)} %get-tuple-element.18.k_ref, bf16[8,48,1024]{2,1,0:T(8,128)(2,1)S(1)} %get-tuple-element.19.vt_ref, f32[8,128]{1,0:T(8,128)S(1)} %get-tuple-element.20.facts_ref, ...), custom_call_target="tpu_custom_call" | custom-call | flops 3221225472 | bytes 1048576 | tf_op jit(solution)/shard_map/near/pallas_call | solution.py:571
  52.6 0.0 collective-permute-done.3.next_ref
  52.6 0.0 collective-permute-done.4.prior_ref
  52.6 0.0 collective-permute-done.5.across_ref
  52.7 36.3 %far_finish.1 = bf16[1024,256]{1,0:T(8,128)(2,1)} custom-call(s32[16]{0:T(128)S(1)} %get-tuple-element.14.dest_ref, bf16[1024,256]{1,0:T(8,128)(2,1)S(1)} %get-tuple-element.15.packed_ref.points_ref, bf16[256,1024]{1,0:T(8,128)(2,1)S(1)} %near.1.near_ref, bf16[512,256]{1,0:T(8,128)(2,1)S(1)} %collective-permute-done.3.next_ref, ...), custom_call_target="tpu_custom_call" | custom-call | flops 6442450944 | bytes 1048576 | tf_op jit(solution)/shard_map/far_finish/pallas_call | solution.py:591
  (8 shorter events, 0.1 us)
Async XLA Ops:
  0.0 5.2 %copy-start.2 = (bf16[256,512]{1,0:T(8,128)(2,1)S(1)}, bf16[256,512]{1,0:T(8,128)(2,1)}, u32[]{:S(2)}) copy-start(bf16[256,512]{1,0:T(8,128)(2,1)} %wqk_ref.3) | copy-start | bytes 786436
  0.0 5.2 %copy-start.3 = (bf16[256,256]{1,0:T(8,128)(2,1)S(1)}, bf16[256,256]{1,0:T(8,128)(2,1)}, u32[]{:S(2)}) copy-start(bf16[256,256]{1,0:T(8,128)(2,1)} %wv_ref.3) | copy-start | bytes 393220
  2.1 50.5 %collective-permute-start.5 = (bf16[1024,256]{1,0:T(8,128)(2,1)S(1)}, bf16[1024,256]{1,0:T(8,128)(2,1)S(1)}, u32[]{:S(2)}, u32[]{:S(2)}) collective-permute-start(bf16[1024,256]{1,0:T(8,128)(2,1)S(1)} %get-tuple-element.15.packed_ref.points_ref), channel_id=1, source_target_pairs={{0,16},{8,24},{16,0},{24,8},{1,17},{9,25},{17,1},{25,9},{2,18},{10... | collective-permute-start | bytes 1572872 | tf_op jit(solution)/shard_map/ppermute | solution.py:507
  6.4 5.5 %collective-permute-start = (bf16[1,128,256]{2,1,0:T(8,128)(2,1)S(1)}, bf16[1,128,256]{2,1,0:T(8,128)(2,1)S(1)}, u32[]{:S(2)}, u32[]{:S(2)}) collective-permute-start(bf16[1,128,256]{2,1,0:T(8,128)(2,1)S(1)} %bitcast.6), channel_id=1, source_target_pairs={{0,4},{1,5},{2,6},{3,7},{4,0},{5,1},{6,2},{7,3},{8,12},{9,13},{10,... | collective-permute-start | bytes 196616 | tf_op jit(solution)/shard_map/ppermute | solution.py:551
  9.1 43.5 %collective-permute-start.3 = (bf16[512,256]{1,0:T(8,128)(2,1)S(1)}, bf16[512,256]{1,0:T(8,128)(2,1)S(1)}, u32[]{:S(2)}, u32[]{:S(2)}) collective-permute-start(bf16[512,256]{1,0:T(8,128)(2,1)S(1)} %get-tuple-element.24), channel_id=1, source_target_pairs={{0,24},{8,0},{16,8},{24,16},{1,25},{9,1},{17,9},{25,17},{2,26},{10... | collective-permute-start | bytes 786440 | tf_op jit(solution)/shard_map/ppermute | solution.py:507
  10.6 42.0 %collective-permute-start.4 = (bf16[512,256]{1,0:T(8,128)(2,1)S(1)}, bf16[512,256]{1,0:T(8,128)(2,1)S(1)}, u32[]{:S(2)}, u32[]{:S(2)}) collective-permute-start(bf16[512,256]{1,0:T(8,128)(2,1)S(1)} %get-tuple-element.23), channel_id=1, source_target_pairs={{0,8},{8,16},{16,24},{24,0},{1,9},{9,17},{17,25},{25,1},{2,10},{10... | collective-permute-start | bytes 786440 | tf_op jit(solution)/shard_map/ppermute | solution.py:507
  12.0 5.7 %collective-permute-start.1 = (bf16[2,128,256]{2,1,0:T(8,128)(2,1)S(1)}, bf16[2,128,256]{2,1,0:T(8,128)(2,1)S(1)}, u32[]{:S(2)}, u32[]{:S(2)}) collective-permute-start(bf16[2,128,256]{2,1,0:T(8,128)(2,1)S(1)} %pad_maximum_fusion.2), channel_id=1, source_target_pairs={{0,2},{1,3},{2,0},{3,1},{4,6},{5,7},{6,4},{7,5},{8,10},{9,11},{10,... | collective-permute-start | bytes 393224 | tf_op jit(solution)/shard_map/ppermute | solution.py:551
  17.7 1.7 %collective-permute-start.2 = (bf16[4,128,256]{2,1,0:T(8,128)(2,1)S(1)}, bf16[4,128,256]{2,1,0:T(8,128)(2,1)S(1)}, u32[]{:S(2)}, u32[]{:S(2)}) collective-permute-start(bf16[4,128,256]{2,1,0:T(8,128)(2,1)S(1)} %pad_maximum_fusion.1), channel_id=1, source_target_pairs={{0,1},{1,0},{2,3},{3,2},{4,5},{5,4},{6,7},{7,6},{8,9},{9,8},{10,11... | collective-permute-start | bytes 786440 | tf_op jit(solution)/shard_map/ppermute | solution.py:551
  19.5 33.1 %copy-start = (bf16[256,1024]{1,0:T(8,128)(2,1)S(1)}, bf16[256,1024]{1,0:T(8,128)(2,1)}, u32[]{:S(2)}) copy-start(bf16[256,1024]{1,0:T(8,128)(2,1)} %up_ref.1) | copy-start | bytes 1572868
  19.5 33.1 %copy-start.1 = (bf16[1024,256]{1,0:T(8,128)(2,1)S(1)}, bf16[1024,256]{1,0:T(8,128)(2,1)}, u32[]{:S(2)}) copy-start(bf16[1024,256]{1,0:T(8,128)(2,1)} %down_ref.1) | copy-start | bytes 1572868
  19.5 33.1 %copy-start.4 = (bf16[256,256]{1,0:T(8,128)(2,1)S(1)}, bf16[256,256]{1,0:T(8,128)(2,1)}, u32[]{:S(2)}) copy-start(bf16[256,256]{1,0:T(8,128)(2,1)} %wo_ref.1) | copy-start | bytes 393220

commit v8 on v7

--- a/solution.py
+++ b/solution.py
@@ -70,7 +70,11 @@
         slots[offset] = 0
         counts[offset] = 0
     for cluster in range(clusters):
-        offset = lax.rem(dest_ref[cluster] // clusters - me + lanes, lanes)
+        if clusters & (clusters - 1) or lanes & (lanes - 1):
+            offset = lax.rem(dest_ref[cluster] // clusters - me + lanes, lanes)
+        else:
+            owner = lax.shift_right_logical(dest_ref[cluster], clusters.bit_length() - 1)
+            offset = (owner - me + lanes) & (lanes - 1)
         slots[offset] = 1
         offsets.append(offset)
     if capacity * 2 == clusters:

time: 89.4 us -> 89.3 us (level)
  no operation moved by 1% of the time
where the time goes in v8:
time: 89.3 us; the launch traced here: 89 us
  Pallas kernels  78.6 us (88%)
  starting transfers between devices  9.18 us (10%)
    pallas_call x1, Pallas kernels, per_device(): pl.pallas_call(functools.partial(far_finish_kernel, lanes, clusters, head...  36.3 us
    pallas_call x1, Pallas kernels, per_device(): pl.pallas_call(functools.partial(near_kernel, head_size), out_shape=turne...  33.1 us
    pallas_call x2, Pallas kernels, per_device(): pl.pallas_call(functools.partial(near_part_kernel, heads, head_size), out...  5.96 us
    ppermute x3, starting transfers between devices, shift(): lax.ppermute(data, 'ball', [(i, (i + offset) % lanes) for i in range(lane...  5.11 us
    ppermute x3, starting transfers between devices, across_regions(): return lax.ppermute(data, 'region', [(i, i ^ mask) for i in range(regions)])  4.07 us
    pallas_call x1, Pallas kernels, per_device(): pl.pallas_call(functools.partial(pack_kernel, lanes, clusters), out_shape...  2.05 us
  transfers between devices with their start and end apart: 6, of which 1 were waited for; matrix products, arithmetic and copies ran while one was open for 0% of the time, Pallas kernels for 45%

profile of v8, /device:TPU:0, one launch (start us, length us, event | category | flops | bytes accessed | tf_op | source)
XLA Modules:
  0.0 89.0 jit_solution(8587092756426445606)
XLA Ops:
  0.0 2.0 %pack.1 = (bf16[1024,256]{1,0:T(8,128)(2,1)S(1)}, f32[1,256]{1,0:T(1,128)S(1)}, f32[1,256]{1,0:T(1,128)S(1)}, s32[16]{0:T(128)S(1)}) custom-call(s32[16]{0:T(128)} %bitcast.13, bf16[1024,256]{1,0:T(8,128)(2,1)} %bitcast.10, f32[1,256]{1,0:T(1,128)} %bitcast.11, f32[1,256]{1,0:T(1,128)} %bitcast.12), custom_call_target="tpu_custom_call" | custom-call | bytes 1048576 | tf_op jit(solution)/shard_map/pack/pallas_call | solution.py:514
  2.1 3.0 %collective-permute-start.5 = (bf16[1024,256]{1,0:T(8,128)(2,1)S(1)}, bf16[1024,256]{1,0:T(8,128)(2,1)S(1)}, u32[]{:S(2)}, u32[]{:S(2)}) collective-permute-start(bf16[1024,256]{1,0:T(8,128)(2,1)S(1)} %get-tuple-element.15.packed_ref.points_ref), channel_id=1, source_target_pairs={{0,16},{8,24},{16,0},{24,8},{1,17},{9,25},{17,1},{25,9},{2,18},{10... | collective-permute-start | bytes 1572872 | tf_op jit(solution)/shard_map/ppermute | solution.py:511
  5.1 0.0 copy-done.2
  5.1 0.0 copy-done.3
  5.1 1.2 %project.1 = (bf16[256,1024]{1,0:T(8,128)(2,1)S(1)}, bf16[1024,256]{1,0:T(8,128)(2,1)S(1)}, bf16[8,48,1024]{2,1,0:T(8,128)(2,1)S(1)}, bf16[128,256]{1,0:T(8,128)(2,1)S(1)}, f32[8,128]{1,0:T(8,128)S(1)}) custom-call(bf16[1024,256]{1,0:T(8,128)(2,1)S(1)} %get-tuple-element.15.packed_ref.points_ref, f32[1,256]{1,0:T(1,128)S(1)} %get-tuple-element.16.gain_ref, ...), custom_call_target="tpu_custom_call" | custom-call | flops 402653184 | bytes 2621440 | tf_op jit(solution)/shard_map/project/pallas_call | solution.py:538
  6.4 2.7 %collective-permute-start = (bf16[1,128,256]{2,1,0:T(8,128)(2,1)S(1)}, bf16[1,128,256]{2,1,0:T(8,128)(2,1)S(1)}, u32[]{:S(2)}, u32[]{:S(2)}) collective-permute-start(bf16[1,128,256]{2,1,0:T(8,128)(2,1)S(1)} %bitcast.6), channel_id=1, source_target_pairs={{0,4},{1,5},{2,6},{3,7},{4,0},{5,1},{6,2},{7,3},{8,12},{9,13},{10,... | collective-permute-start | bytes 196616 | tf_op jit(solution)/shard_map/ppermute | solution.py:555
  9.0 1.5 %collective-permute-start.3 = (bf16[512,256]{1,0:T(8,128)(2,1)S(1)}, bf16[512,256]{1,0:T(8,128)(2,1)S(1)}, u32[]{:S(2)}, u32[]{:S(2)}) collective-permute-start(bf16[512,256]{1,0:T(8,128)(2,1)S(1)} %get-tuple-element.24), channel_id=1, source_target_pairs={{0,24},{8,0},{16,8},{24,16},{1,25},{9,1},{17,9},{25,17},{2,26},{10... | collective-permute-start | bytes 786440 | tf_op jit(solution)/shard_map/ppermute | solution.py:511
  10.5 0.6 collective-permute-start.4
  11.1 0.8 collective-permute-done
  11.9 1.3 %collective-permute-start.1 = (bf16[2,128,256]{2,1,0:T(8,128)(2,1)S(1)}, bf16[2,128,256]{2,1,0:T(8,128)(2,1)S(1)}, u32[]{:S(2)}, u32[]{:S(2)}) collective-permute-start(bf16[2,128,256]{2,1,0:T(8,128)(2,1)S(1)} %pad_maximum_fusion.2), channel_id=1, source_target_pairs={{0,2},{1,3},{2,0},{3,1},{4,6},{5,7},{6,4},{7,5},{8,10},{9,11},{10,... | collective-permute-start | bytes 393224 | tf_op jit(solution)/shard_map/ppermute | solution.py:555
  13.2 4.4 %near_part.2.rest_0_ = f32[6,40,1024]{2,1,0:T(8,128)S(1)} custom-call(bf16[256,1024]{1,0:T(8,128)(2,1)S(1)} %get-tuple-element.17.qt_ref, bf16[1024,256]{1,0:T(8,128)(2,1)S(1)} %get-tuple-element.18.k_ref, bf16[8,48,1024]{2,1,0:T(8,128)(2,1)S(1)} %get-tuple-element.19.vt_ref), custom_call_target="tpu_custom_call" | custom-call | flops 3221225472 | bytes 1048576 | tf_op jit(solution)/shard_map/near_part/pallas_call | solution.py:563
  17.6 0.0 collective-permute-done.1
  17.6 0.1 collective-permute-start.2
  17.7 1.6 %near_part.3.rest_1_ = f32[2,40,1024]{2,1,0:T(8,128)S(1)} custom-call(bf16[256,1024]{1,0:T(8,128)(2,1)S(1)} %get-tuple-element.17.qt_ref, bf16[1024,256]{1,0:T(8,128)(2,1)S(1)} %get-tuple-element.18.k_ref, bf16[8,48,1024]{2,1,0:T(8,128)(2,1)S(1)} %get-tuple-element.19.vt_ref), custom_call_target="tpu_custom_call" | custom-call | flops 3221225472 | bytes 1048576 | tf_op jit(solution)/shard_map/near_part/pallas_call | solution.py:563
  19.3 0.0 collective-permute-done.2
  19.3 0.1 pad_maximum_fusion.pool_ref
  19.4 0.0 copy-start
  19.4 0.0 copy-start.1
  19.4 0.0 copy-start.4
  19.4 33.1 %near.1.near_ref = bf16[256,1024]{1,0:T(8,128)(2,1)S(1)} custom-call(bf16[256,1024]{1,0:T(8,128)(2,1)S(1)} %get-tuple-element.17.qt_ref, bf16[1024,256]{1,0:T(8,128)(2,1)S(1)} %get-tuple-element.18.k_ref, bf16[8,48,1024]{2,1,0:T(8,128)(2,1)S(1)} %get-tuple-element.19.vt_ref, f32[8,128]{1,0:T(8,128)S(1)} %get-tuple-element.20.facts_ref, ...), custom_call_target="tpu_custom_call" | custom-call | flops 3221225472 | bytes 1048576 | tf_op jit(solution)/shard_map/near/pallas_call | solution.py:575
  52.5 0.0 collective-permute-done.3.next_ref
  52.5 0.0 collective-permute-done.4.prior_ref
  52.5 0.0 collective-permute-done.5.across_ref
  52.6 36.3 %far_finish.1 = bf16[1024,256]{1,0:T(8,128)(2,1)} custom-call(s32[16]{0:T(128)S(1)} %get-tuple-element.14.dest_ref, bf16[1024,256]{1,0:T(8,128)(2,1)S(1)} %get-tuple-element.15.packed_ref.points_ref, bf16[256,1024]{1,0:T(8,128)(2,1)S(1)} %near.1.near_ref, bf16[512,256]{1,0:T(8,128)(2,1)S(1)} %collective-permute-done.3.next_ref, ...), custom_call_target="tpu_custom_call" | custom-call | flops 6442450944 | bytes 1048576 | tf_op jit(solution)/shard_map/far_finish/pallas_call | solution.py:595
  (8 shorter events, 0.1 us)
Async XLA Ops:
  0.0 5.1 %copy-start.2 = (bf16[256,512]{1,0:T(8,128)(2,1)S(1)}, bf16[256,512]{1,0:T(8,128)(2,1)}, u32[]{:S(2)}) copy-start(bf16[256,512]{1,0:T(8,128)(2,1)} %wqk_ref.3) | copy-start | bytes 786436
  0.0 5.1 %copy-start.3 = (bf16[256,256]{1,0:T(8,128)(2,1)S(1)}, bf16[256,256]{1,0:T(8,128)(2,1)}, u32[]{:S(2)}) copy-start(bf16[256,256]{1,0:T(8,128)(2,1)} %wv_ref.3) | copy-start | bytes 393220
  2.1 50.5 %collective-permute-start.5 = (bf16[1024,256]{1,0:T(8,128)(2,1)S(1)}, bf16[1024,256]{1,0:T(8,128)(2,1)S(1)}, u32[]{:S(2)}, u32[]{:S(2)}) collective-permute-start(bf16[1024,256]{1,0:T(8,128)(2,1)S(1)} %get-tuple-element.15.packed_ref.points_ref), channel_id=1, source_target_pairs={{0,16},{8,24},{16,0},{24,8},{1,17},{9,25},{17,1},{25,9},{2,18},{10... | collective-permute-start | bytes 1572872 | tf_op jit(solution)/shard_map/ppermute | solution.py:511
  6.4 5.5 %collective-permute-start = (bf16[1,128,256]{2,1,0:T(8,128)(2,1)S(1)}, bf16[1,128,256]{2,1,0:T(8,128)(2,1)S(1)}, u32[]{:S(2)}, u32[]{:S(2)}) collective-permute-start(bf16[1,128,256]{2,1,0:T(8,128)(2,1)S(1)} %bitcast.6), channel_id=1, source_target_pairs={{0,4},{1,5},{2,6},{3,7},{4,0},{5,1},{6,2},{7,3},{8,12},{9,13},{10,... | collective-permute-start | bytes 196616 | tf_op jit(solution)/shard_map/ppermute | solution.py:555
  9.0 43.5 %collective-permute-start.3 = (bf16[512,256]{1,0:T(8,128)(2,1)S(1)}, bf16[512,256]{1,0:T(8,128)(2,1)S(1)}, u32[]{:S(2)}, u32[]{:S(2)}) collective-permute-start(bf16[512,256]{1,0:T(8,128)(2,1)S(1)} %get-tuple-element.24), channel_id=1, source_target_pairs={{0,24},{8,0},{16,8},{24,16},{1,25},{9,1},{17,9},{25,17},{2,26},{10... | collective-permute-start | bytes 786440 | tf_op jit(solution)/shard_map/ppermute | solution.py:511
  10.5 42.0 %collective-permute-start.4 = (bf16[512,256]{1,0:T(8,128)(2,1)S(1)}, bf16[512,256]{1,0:T(8,128)(2,1)S(1)}, u32[]{:S(2)}, u32[]{:S(2)}) collective-permute-start(bf16[512,256]{1,0:T(8,128)(2,1)S(1)} %get-tuple-element.23), channel_id=1, source_target_pairs={{0,8},{8,16},{16,24},{24,0},{1,9},{9,17},{17,25},{25,1},{2,10},{10... | collective-permute-start | bytes 786440 | tf_op jit(solution)/shard_map/ppermute | solution.py:511
  11.9 5.7 %collective-permute-start.1 = (bf16[2,128,256]{2,1,0:T(8,128)(2,1)S(1)}, bf16[2,128,256]{2,1,0:T(8,128)(2,1)S(1)}, u32[]{:S(2)}, u32[]{:S(2)}) collective-permute-start(bf16[2,128,256]{2,1,0:T(8,128)(2,1)S(1)} %pad_maximum_fusion.2), channel_id=1, source_target_pairs={{0,2},{1,3},{2,0},{3,1},{4,6},{5,7},{6,4},{7,5},{8,10},{9,11},{10,... | collective-permute-start | bytes 393224 | tf_op jit(solution)/shard_map/ppermute | solution.py:555
  17.6 1.7 %collective-permute-start.2 = (bf16[4,128,256]{2,1,0:T(8,128)(2,1)S(1)}, bf16[4,128,256]{2,1,0:T(8,128)(2,1)S(1)}, u32[]{:S(2)}, u32[]{:S(2)}) collective-permute-start(bf16[4,128,256]{2,1,0:T(8,128)(2,1)S(1)} %pad_maximum_fusion.1), channel_id=1, source_target_pairs={{0,1},{1,0},{2,3},{3,2},{4,5},{5,4},{6,7},{7,6},{8,9},{9,8},{10,11... | collective-permute-start | bytes 786440 | tf_op jit(solution)/shard_map/ppermute | solution.py:555
  19.4 33.1 %copy-start = (bf16[256,1024]{1,0:T(8,128)(2,1)S(1)}, bf16[256,1024]{1,0:T(8,128)(2,1)}, u32[]{:S(2)}) copy-start(bf16[256,1024]{1,0:T(8,128)(2,1)} %up_ref.1) | copy-start | bytes 1572868
  19.4 33.1 %copy-start.1 = (bf16[1024,256]{1,0:T(8,128)(2,1)S(1)}, bf16[1024,256]{1,0:T(8,128)(2,1)}, u32[]{:S(2)}) copy-start(bf16[1024,256]{1,0:T(8,128)(2,1)} %down_ref.1) | copy-start | bytes 1572868
  19.4 33.1 %copy-start.4 = (bf16[256,256]{1,0:T(8,128)(2,1)S(1)}, bf16[256,256]{1,0:T(8,128)(2,1)}, u32[]{:S(2)}) copy-start(bf16[256,256]{1,0:T(8,128)(2,1)} %wo_ref.1) | copy-start | bytes 393220
